TPU v7x, 128 devices: a whole 4x4x4 slice. The times are simulated.
128 devices in a mesh: win: 8 (over y, core), chan: 16 (over z, x).
Axes of the slice: x: 4, y: 4, z: 4, core: 2. Of those that a mesh axis runs over, the one named last changes fastest.
Arguments:
- spectra: bfloat16 [8, 2048, 8192], P(None, ('chan', 'win')), may hold values from -40 to 40
- pair_remote: int32 [16, 4], P('chan'), may hold values from 0 to 15, as said below
- pair_count: int32 [16], P('chan'), may hold values from 0 to 4, as said below
Outputs:
- correlations: float32 [8, 16, 4, 128, 256], P('win', 'chan')
Inputs may be any that keep to these rules, and one draw needn't show every extreme that they name: `pair_remote`: for owner block b, slots below pair_count[b] list distinct blocks r != b with |r - b| <= 2 in rising order; the other slots hold 0. `pair_count`: some owner block lists all 4 pairs.
All inputs are finite; a program needn't handle non-finite values.
Results may differ from a plain program's by a relative error of at most 0.0049.
Values may be sent and summed in bfloat16 or wider, within the bound.
No kernel may reach another device: no remote copies, remote signals or barrier semaphores. Data moves between devices by JAX's collectives and lax.ppermute only.
A program may use at most 64 MiB of HBM per device.

v0:
```python
import math

import jax
import jax.numpy as jnp
from jax import lax
from jax.sharding import PartitionSpec as P

BAND = 64
LAGS = 256
V = 8
REACH = 2


def shifted(block, axis, distance):
    devices = range(lax.axis_size(axis))
    route = [(i - distance, i) for i in devices if i - distance in devices]
    return lax.ppermute(block, axis, route)


def whiten(spectra):
    values = spectra.astype(jnp.float32)
    bin_count = values.shape[-1] // 2
    real_part = values[..., :bin_count]
    imag_part = values[..., bin_count:]
    magnitude = jnp.sqrt(real_part * real_part + imag_part * imag_part)
    shape = magnitude.shape[:-1] + (bin_count // BAND, BAND)
    level = jnp.mean(magnitude.reshape(shape), axis=-1, keepdims=True) + 1e-06
    level = jnp.broadcast_to(level, shape).reshape(magnitude.shape)
    return jnp.concatenate([real_part / level, imag_part / level], axis=-1).astype(jnp.bfloat16)


def phase_tables(bin_count):
    lag_index = jnp.arange(LAGS, dtype=jnp.int32) - LAGS // 2
    freq_index = jnp.arange(bin_count, dtype=jnp.int32)
    phase = lag_index[:, None] * freq_index[None, :] % (2 * bin_count)
    angle = phase.astype(jnp.float32) * (math.pi / bin_count)
    return (jnp.cos(angle), jnp.sin(angle))


def rotate(source, cos_table, sin_table):
    bin_count = source.shape[-1] // 2
    real_part = source[..., None, :bin_count]
    imag_part = source[..., None, bin_count:]
    rot_real = real_part * cos_table - imag_part * sin_table
    rot_imag = real_part * sin_table + imag_part * cos_table
    return jnp.concatenate([rot_real, rot_imag], axis=-1).astype(jnp.bfloat16)


def on_device(spectra, pair_remote, pair_count):
    whitened = whiten(spectra)
    remotes = pair_remote[0]
    live_count = pair_count[0]
    slot_count = remotes.shape[0]
    live = jnp.arange(slot_count, dtype=jnp.int32) < live_count
    offsets = list(range(-REACH, 0)) + list(range(1, REACH + 1))
    local_spec = lax.all_to_all(whitened, "win", split_axis=0, concat_axis=1, tiled=True)
    win_local = local_spec.shape[0]
    block_width = local_spec.shape[1]
    bin_count = local_spec.shape[2] // 2
    cos_table, sin_table = phase_tables(bin_count)
    stride = block_width // V
    scale = 1.0 / math.sqrt(bin_count * win_local * lax.axis_size("win"))
    empty = jnp.zeros((slot_count,) + local_spec.shape, jnp.bfloat16)
    distance = remotes - lax.axis_index("chan")
    gathered = empty
    for offset in offsets:
        moved = shifted(local_spec, "chan", -offset)
        gathered = jnp.where((distance == offset)[:, None, None, None], moved[None], gathered)

    def one_source(offset):
        channel = offset * stride
        source = lax.dynamic_slice_in_dim(local_spec, channel, 1, 1)[:, 0].astype(jnp.float32)
        rotated = rotate(source, cos_table, sin_table)
        return (
            jnp.einsum("wlk,swck->scl", rotated, gathered, preferred_element_type=jnp.float32)
            * scale
        )

    terms = lax.map(
        one_source, jnp.arange(V // lax.axis_size("win") * lax.axis_size("win"), dtype=jnp.int32)
    )
    stacked = lax.psum_scatter(terms[:, None], "win", scatter_dimension=0, tiled=True)
    return jnp.where(live[None, None, :, None, None], stacked, jnp.float32(0.0))


def solution(mesh):
    in_specs = (P(None, ("chan", "win"), None), P("chan", None), P("chan"))
    out_specs = P("win", "chan", None, None, None)
    return jax.shard_map(
        on_device, mesh=mesh, in_specs=in_specs, out_specs=out_specs, check_vma=False
    )
```

profile of v0, /device:TPU:34, one launch (start us, length us, event | category | flops | bytes accessed | tf_op | source)
XLA Modules:
  0.0 483.0 jit_solution(5514499853093160500)
XLA Ops:
  6.5 2.0 convert_element_type.31
  8.6 1.9 copy-done
  10.5 0.7 add_sqrt_fusion
  11.2 3.1 reshape.174
  14.2 3.3 reduce_sum.9
  17.6 2.6 broadcast_in_dim.104
  20.2 3.5 reshape.175
  23.7 2.7 divide_convert_fusion.1
  26.7 31.9 %all_to_all.12 = bf16[8,16,8192]{2,1,0:T(8,128)(2,1)} all-to-all(bf16[8,16,8192]{2,1,0:T(8,128)(2,1)S(1)} %pad_maximum_fusion), channel_id=1, replica_groups=mesh['win'=8,'chan'=16] {'win'}, dimensions={0} | all-to-all | bytes 4194304 | tf_op jit(solution)/shard_map/all_to_all | solution.py:56
  58.5 4.0 collective-permute-start.3
  62.6 3.1 collective-permute-start.2
  65.7 2.7 collective-permute-start.1
  68.4 4.5 collective-permute-start
  73.0 38.8 %collective-permute-done.3 = bf16[1,128,8192]{2,1,0:T(8,128)(2,1)} collective-permute-done((bf16[1,128,8192]{2,1,0:T(8,128)(2,1)}, bf16[1,128,8192]{2,1,0:T(8,128)(2,1)}, u32[]{:S(2)}, u32[]{:S(2)}) %collective-permute-start.3) | collective-permute-done | bytes 2097184 | tf_op jit(solution)/shard_map/ppermute | solution.py:17
  111.8 44.1 %collective-permute-done.2 = bf16[1,128,8192]{2,1,0:T(8,128)(2,1)} collective-permute-done((bf16[1,128,8192]{2,1,0:T(8,128)(2,1)}, bf16[1,128,8192]{2,1,0:T(8,128)(2,1)}, u32[]{:S(2)}, u32[]{:S(2)}) %collective-permute-start.2) | collective-permute-done | bytes 2097184 | tf_op jit(solution)/shard_map/ppermute | solution.py:17
  155.8 1.2 collective-permute-done.1
  157.1 43.5 %collective-permute-done = bf16[1,128,8192]{2,1,0:T(8,128)(2,1)} collective-permute-done((bf16[1,128,8192]{2,1,0:T(8,128)(2,1)}, bf16[1,128,8192]{2,1,0:T(8,128)(2,1)}, u32[]{:S(2)}, u32[]{:S(2)}) %collective-permute-start) | collective-permute-done | bytes 2097184 | tf_op jit(solution)/shard_map/ppermute | solution.py:17
  200.5 236.2 %while.13 = (s32[]{:T(128)}, f32[8,4,128,256]{3,2,1,0:T(8,128)}, s32[8]{0:T(128)S(1)}, bf16[1,128,8192]{2,1,0:T(8,128)(2,1)}, s32[256]{0:T(256)S(1)}, /*index=5*...) while((s32[]{:T(128)}, f32[8,4,128,256]{3,2,1,0:T(8,128)}, ...), condition=%wide.region_2.3_spmd.clone.clone.clone, body=%wide.region_1.2_spmd.clone.clone.clone.sunk | while | flops 2195857408 | bytes 19547884 | solution.py:79
  200.5 0.7 dynamic_slice.17
  201.9 0.9 bitcast_convert_fusion.2
  202.8 18.6 %subtract_convert_fusion.2 = (bf16[256,4096]{1,0:T(8,128)(2,1)S(1)}, bf16[256,4096]{1,0:T(8,128)(2,1)}) fusion(s32[256]{0:T(256)S(1)} %get-tuple-element.306, f32[4096]{0:T(1024)S(1)} %bitcast.58, f32[4096]{0:T(1024)S(1)} %bitcast.57), kind=kLoop, calls=%fused_computation.30.clone.1 | loop fusion | flops 23068672 | bytes 4228096 | tf_op jit(solution)/shard_map/convert.1
  221.5 7.5 %fusion.45 = f32[1,4,128,256]{2,3,1,0:T(8,128)S(1)} fusion(pred[4]{0:T(512)(128)(4,1)S(1)} %get-tuple-element.308, pred[4]{0:T(512)(128)(4,1)S(1)} %get-tuple-element.310, pred[4]{0:T(512)(128)(4,1)S(1)} %get-tuple-element.312, pred[4]{0:T(512)(128)(4,1)S(1)} %get-tuple-element.314, bf16[128,8192]{1,0:T(8,128)(2,1)} %get-tuple-element.307, ...), kind=kOutput, calls=%fused_computation.35.clone.1 | convolution fusion | flops 2172780544 | bytes 13107216 | tf_op jit(solution)/shard_map/while/body/eval_jaxpr/wlk,swck->scl/dot_general | solution.py:75
  229.0 0.2 copy.9
  229.2 0.8 constant_dynamic-update-slice_fusion.2
  230.1 0.7 dynamic_slice.17
  231.4 0.9 bitcast_convert_fusion.2
  232.4 18.6 %subtract_convert_fusion.2 = (bf16[256,4096]{1,0:T(8,128)(2,1)S(1)}, bf16[256,4096]{1,0:T(8,128)(2,1)}) fusion(s32[256]{0:T(256)S(1)} %get-tuple-element.306, f32[4096]{0:T(1024)S(1)} %bitcast.58, f32[4096]{0:T(1024)S(1)} %bitcast.57), kind=kLoop, calls=%fused_computation.30.clone.1 | loop fusion | flops 23068672 | bytes 4228096 | tf_op jit(solution)/shard_map/convert.1
  251.0 7.5 %fusion.45 = f32[1,4,128,256]{2,3,1,0:T(8,128)S(1)} fusion(pred[4]{0:T(512)(128)(4,1)S(1)} %get-tuple-element.308, pred[4]{0:T(512)(128)(4,1)S(1)} %get-tuple-element.310, pred[4]{0:T(512)(128)(4,1)S(1)} %get-tuple-element.312, pred[4]{0:T(512)(128)(4,1)S(1)} %get-tuple-element.314, bf16[128,8192]{1,0:T(8,128)(2,1)} %get-tuple-element.307, ...), kind=kOutput, calls=%fused_computation.35.clone.1 | convolution fusion | flops 2172780544 | bytes 13107216 | tf_op jit(solution)/shard_map/while/body/eval_jaxpr/wlk,swck->scl/dot_general | solution.py:75
  258.5 0.2 copy.9
  258.7 0.8 constant_dynamic-update-slice_fusion.2
  259.6 0.7 dynamic_slice.17
  260.9 0.9 bitcast_convert_fusion.2
  261.9 18.6 %subtract_convert_fusion.2 = (bf16[256,4096]{1,0:T(8,128)(2,1)S(1)}, bf16[256,4096]{1,0:T(8,128)(2,1)}) fusion(s32[256]{0:T(256)S(1)} %get-tuple-element.306, f32[4096]{0:T(1024)S(1)} %bitcast.58, f32[4096]{0:T(1024)S(1)} %bitcast.57), kind=kLoop, calls=%fused_computation.30.clone.1 | loop fusion | flops 23068672 | bytes 4228096 | tf_op jit(solution)/shard_map/convert.1
  280.5 7.5 %fusion.45 = f32[1,4,128,256]{2,3,1,0:T(8,128)S(1)} fusion(pred[4]{0:T(512)(128)(4,1)S(1)} %get-tuple-element.308, pred[4]{0:T(512)(128)(4,1)S(1)} %get-tuple-element.310, pred[4]{0:T(512)(128)(4,1)S(1)} %get-tuple-element.312, pred[4]{0:T(512)(128)(4,1)S(1)} %get-tuple-element.314, bf16[128,8192]{1,0:T(8,128)(2,1)} %get-tuple-element.307, ...), kind=kOutput, calls=%fused_computation.35.clone.1 | convolution fusion | flops 2172780544 | bytes 13107216 | tf_op jit(solution)/shard_map/while/body/eval_jaxpr/wlk,swck->scl/dot_general | solution.py:75
  288.0 0.2 copy.9
  288.2 0.9 constant_dynamic-update-slice_fusion.2
  289.1 0.7 dynamic_slice.17
  290.5 0.9 bitcast_convert_fusion.2
  291.4 18.6 %subtract_convert_fusion.2 = (bf16[256,4096]{1,0:T(8,128)(2,1)S(1)}, bf16[256,4096]{1,0:T(8,128)(2,1)}) fusion(s32[256]{0:T(256)S(1)} %get-tuple-element.306, f32[4096]{0:T(1024)S(1)} %bitcast.58, f32[4096]{0:T(1024)S(1)} %bitcast.57), kind=kLoop, calls=%fused_computation.30.clone.1 | loop fusion | flops 23068672 | bytes 4228096 | tf_op jit(solution)/shard_map/convert.1
  310.1 7.5 %fusion.45 = f32[1,4,128,256]{2,3,1,0:T(8,128)S(1)} fusion(pred[4]{0:T(512)(128)(4,1)S(1)} %get-tuple-element.308, pred[4]{0:T(512)(128)(4,1)S(1)} %get-tuple-element.310, pred[4]{0:T(512)(128)(4,1)S(1)} %get-tuple-element.312, pred[4]{0:T(512)(128)(4,1)S(1)} %get-tuple-element.314, bf16[128,8192]{1,0:T(8,128)(2,1)} %get-tuple-element.307, ...), kind=kOutput, calls=%fused_computation.35.clone.1 | convolution fusion | flops 2172780544 | bytes 13107216 | tf_op jit(solution)/shard_map/while/body/eval_jaxpr/wlk,swck->scl/dot_general | solution.py:75
  317.6 0.2 copy.9
  317.8 0.8 constant_dynamic-update-slice_fusion.2
  318.6 0.7 dynamic_slice.17
  320.0 0.9 bitcast_convert_fusion.2
  320.9 18.6 %subtract_convert_fusion.2 = (bf16[256,4096]{1,0:T(8,128)(2,1)S(1)}, bf16[256,4096]{1,0:T(8,128)(2,1)}) fusion(s32[256]{0:T(256)S(1)} %get-tuple-element.306, f32[4096]{0:T(1024)S(1)} %bitcast.58, f32[4096]{0:T(1024)S(1)} %bitcast.57), kind=kLoop, calls=%fused_computation.30.clone.1 | loop fusion | flops 23068672 | bytes 4228096 | tf_op jit(solution)/shard_map/convert.1
  339.6 7.5 %fusion.45 = f32[1,4,128,256]{2,3,1,0:T(8,128)S(1)} fusion(pred[4]{0:T(512)(128)(4,1)S(1)} %get-tuple-element.308, pred[4]{0:T(512)(128)(4,1)S(1)} %get-tuple-element.310, pred[4]{0:T(512)(128)(4,1)S(1)} %get-tuple-element.312, pred[4]{0:T(512)(128)(4,1)S(1)} %get-tuple-element.314, bf16[128,8192]{1,0:T(8,128)(2,1)} %get-tuple-element.307, ...), kind=kOutput, calls=%fused_computation.35.clone.1 | convolution fusion | flops 2172780544 | bytes 13107216 | tf_op jit(solution)/shard_map/while/body/eval_jaxpr/wlk,swck->scl/dot_general | solution.py:75
  347.3 0.9 constant_dynamic-update-slice_fusion.2
  348.1 0.7 dynamic_slice.17
  349.5 0.9 bitcast_convert_fusion.2
  350.5 18.6 %subtract_convert_fusion.2 = (bf16[256,4096]{1,0:T(8,128)(2,1)S(1)}, bf16[256,4096]{1,0:T(8,128)(2,1)}) fusion(s32[256]{0:T(256)S(1)} %get-tuple-element.306, f32[4096]{0:T(1024)S(1)} %bitcast.58, f32[4096]{0:T(1024)S(1)} %bitcast.57), kind=kLoop, calls=%fused_computation.30.clone.1 | loop fusion | flops 23068672 | bytes 4228096 | tf_op jit(solution)/shard_map/convert.1
  369.1 7.5 %fusion.45 = f32[1,4,128,256]{2,3,1,0:T(8,128)S(1)} fusion(pred[4]{0:T(512)(128)(4,1)S(1)} %get-tuple-element.308, pred[4]{0:T(512)(128)(4,1)S(1)} %get-tuple-element.310, pred[4]{0:T(512)(128)(4,1)S(1)} %get-tuple-element.312, pred[4]{0:T(512)(128)(4,1)S(1)} %get-tuple-element.314, bf16[128,8192]{1,0:T(8,128)(2,1)} %get-tuple-element.307, ...), kind=kOutput, calls=%fused_computation.35.clone.1 | convolution fusion | flops 2172780544 | bytes 13107216 | tf_op jit(solution)/shard_map/while/body/eval_jaxpr/wlk,swck->scl/dot_general | solution.py:75
  376.8 0.8 constant_dynamic-update-slice_fusion.2
  377.7 0.7 dynamic_slice.17
  379.0 0.9 bitcast_convert_fusion.2
  380.0 18.6 %subtract_convert_fusion.2 = (bf16[256,4096]{1,0:T(8,128)(2,1)S(1)}, bf16[256,4096]{1,0:T(8,128)(2,1)}) fusion(s32[256]{0:T(256)S(1)} %get-tuple-element.306, f32[4096]{0:T(1024)S(1)} %bitcast.58, f32[4096]{0:T(1024)S(1)} %bitcast.57), kind=kLoop, calls=%fused_computation.30.clone.1 | loop fusion | flops 23068672 | bytes 4228096 | tf_op jit(solution)/shard_map/convert.1
  398.6 7.5 %fusion.45 = f32[1,4,128,256]{2,3,1,0:T(8,128)S(1)} fusion(pred[4]{0:T(512)(128)(4,1)S(1)} %get-tuple-element.308, pred[4]{0:T(512)(128)(4,1)S(1)} %get-tuple-element.310, pred[4]{0:T(512)(128)(4,1)S(1)} %get-tuple-element.312, pred[4]{0:T(512)(128)(4,1)S(1)} %get-tuple-element.314, bf16[128,8192]{1,0:T(8,128)(2,1)} %get-tuple-element.307, ...), kind=kOutput, calls=%fused_computation.35.clone.1 | convolution fusion | flops 2172780544 | bytes 13107216 | tf_op jit(solution)/shard_map/while/body/eval_jaxpr/wlk,swck->scl/dot_general | solution.py:75
  406.3 0.8 constant_dynamic-update-slice_fusion.2
  407.2 0.7 dynamic_slice.17
  408.5 0.9 bitcast_convert_fusion.2
  409.5 18.6 %subtract_convert_fusion.2 = (bf16[256,4096]{1,0:T(8,128)(2,1)S(1)}, bf16[256,4096]{1,0:T(8,128)(2,1)}) fusion(s32[256]{0:T(256)S(1)} %get-tuple-element.306, f32[4096]{0:T(1024)S(1)} %bitcast.58, f32[4096]{0:T(1024)S(1)} %bitcast.57), kind=kLoop, calls=%fused_computation.30.clone.1 | loop fusion | flops 23068672 | bytes 4228096 | tf_op jit(solution)/shard_map/convert.1
  428.1 7.5 %fusion.45 = f32[1,4,128,256]{2,3,1,0:T(8,128)S(1)} fusion(pred[4]{0:T(512)(128)(4,1)S(1)} %get-tuple-element.308, pred[4]{0:T(512)(128)(4,1)S(1)} %get-tuple-element.310, pred[4]{0:T(512)(128)(4,1)S(1)} %get-tuple-element.312, pred[4]{0:T(512)(128)(4,1)S(1)} %get-tuple-element.314, bf16[128,8192]{1,0:T(8,128)(2,1)} %get-tuple-element.307, ...), kind=kOutput, calls=%fused_computation.35.clone.1 | convolution fusion | flops 2172780544 | bytes 13107216 | tf_op jit(solution)/shard_map/while/body/eval_jaxpr/wlk,swck->scl/dot_general | solution.py:75
  435.9 0.8 constant_dynamic-update-slice_fusion.2
  437.4 36.8 %reduce-scatter.2.cloned.1.call-done = f32[1,1,4,128,256]{4,3,2,1,0:T(8,128)} async-done(((f32[8,1,4,128,256]{4,3,2,1,0:T(8,128)}), f32[1,1,4,128,256]{4,3,2,1,0:T(8,128)}) %reduce-scatter.2.cloned.1.call-update) | async-done | bytes 524304 | tf_op jit(solution)/shard_map/reduce_scatter | solution.py:82
  474.2 1.9 broadcast_select_fusion
  (25 shorter events, 1.1 us)
Async XLA Ops:
  6.5 467.6 %reduce-scatter.2.cloned.1.call-start = ((), (), s32[]{:S(2)}) async-start(), calls=%async_computation.2 | async-start | bytes 4718592 | tf_op jit(solution)/shard_map/reduce_scatter | solution.py:82
  8.5 1.9 copy-start
  26.5 46.5 %copy-start.1 = (s32[1,4]{1,0:T(1,128)S(1)}, s32[1,4]{1,0:T(1,128)}, u32[]{:S(2)}) copy-start(s32[1,4]{1,0:T(1,128)} %param.6) | copy-start | bytes 52
  58.5 53.2 %collective-permute-start.3 = (bf16[1,128,8192]{2,1,0:T(8,128)(2,1)}, bf16[1,128,8192]{2,1,0:T(8,128)(2,1)}, u32[]{:S(2)}, u32[]{:S(2)}) collective-permute-start(bf16[1,128,8192]{2,1,0:T(8,128)(2,1)} %bitcast.1), channel_id=1, source_target_pairs={{0,2},{1,3},{2,4},{3,5},{4,6},{5,7},{6,8},{7,9},{8,10},{9,11},{10,... | collective-permute-start | bytes 6291464 | tf_op jit(solution)/shard_map/ppermute | solution.py:17
  62.6 93.3 %collective-permute-start.2 = (bf16[1,128,8192]{2,1,0:T(8,128)(2,1)}, bf16[1,128,8192]{2,1,0:T(8,128)(2,1)}, u32[]{:S(2)}, u32[]{:S(2)}) collective-permute-start(bf16[1,128,8192]{2,1,0:T(8,128)(2,1)} %bitcast.1), channel_id=1, source_target_pairs={{0,1},{1,2},{2,3},{3,4},{4,5},{5,6},{6,7},{7,8},{8,9},{9,10},{10,1... | collective-permute-start | bytes 6291464 | tf_op jit(solution)/shard_map/ppermute | solution.py:17
  65.7 91.3 %collective-permute-start.1 = (bf16[1,128,8192]{2,1,0:T(8,128)(2,1)}, bf16[1,128,8192]{2,1,0:T(8,128)(2,1)}, u32[]{:S(2)}, u32[]{:S(2)}) collective-permute-start(bf16[1,128,8192]{2,1,0:T(8,128)(2,1)} %bitcast.1), channel_id=1, source_target_pairs={{1,0},{2,1},{3,2},{4,3},{5,4},{6,5},{7,6},{8,7},{9,8},{10,9},{11,1... | collective-permute-start | bytes 6291464 | tf_op jit(solution)/shard_map/ppermute | solution.py:17
  68.4 132.1 %collective-permute-start = (bf16[1,128,8192]{2,1,0:T(8,128)(2,1)}, bf16[1,128,8192]{2,1,0:T(8,128)(2,1)}, u32[]{:S(2)}, u32[]{:S(2)}) collective-permute-start(bf16[1,128,8192]{2,1,0:T(8,128)(2,1)} %bitcast.1), channel_id=1, source_target_pairs={{2,0},{3,1},{4,2},{5,3},{6,4},{7,5},{8,6},{9,7},{10,8},{11,9},{12,... | collective-permute-start | bytes 6291464 | tf_op jit(solution)/shard_map/ppermute | solution.py:17
Sparse Core Ops, SparseCore 0:
  436.8 37.2 reduce-scatter.1
where the time goes:
time: 484 us; the launch traced here: 483 us
  other arithmetic  167 us (35%)
  waiting for transfers between devices  164 us (34%)
  matrix products  60.1 us (12%)
  blocking collectives  31.9 us (7%)
  local copies, waits for them, and re-layouts  24.8 us (5%)
  starting transfers between devices  14.3 us (3%)
  between operations  14.2 us (3%)
  loops' own time  5.83 us (1%)
    another operation x9, other arithmetic  152 us
    ppermute x4, waiting for transfers between devices, shifted(): return lax.ppermute(block, axis, route)  128 us
    dot_general x8, matrix products, one_source(): jnp.einsum('wlk,swck->scl', rotated, gathered, preferred_element_type=jnp...  60.1 us
    reduce_scatter x1, waiting for transfers between devices, on_device(): lax.psum_scatter(terms[:, None], 'win', scatter_dimension=0, tiled=True)  36.8 us
    all_to_all x1, blocking collectives, on_device(): lax.all_to_all(whitened, 'win', split_axis=0, concat_axis=1, tiled=True)  31.9 us
    ppermute x4, starting transfers between devices, shifted(): return lax.ppermute(block, axis, route)  14.3 us
  transfers between devices with their start and end apart: 5, of which 5 were waited for; matrix products, arithmetic and copies ran while one was open for 0% of the time, Pallas kernels for 0%

commit v1 on v0

v1 whole, which is shorter than its diff:
```python
import functools
import math

import jax
import jax.numpy as jnp
import ml_dtypes
import numpy as np
from jax import lax
from jax.experimental import pallas as pl
from jax.experimental.pallas import tpu as pltpu
from jax.sharding import PartitionSpec as P

BAND = 64
LAGS = 256
REACH = 2
CHUNK = 1024
VMEM = 48 * 1024 * 1024
OFFSETS = (-2, -1, 1, 2)


def lag_table(bins):
    t = np.arange(LAGS) - LAGS // 2
    f = np.arange(bins)
    angle = ((f[:, None] * t[None, :]) % (2 * bins)) * (math.pi / bins)
    table = np.concatenate([np.cos(angle), -np.sin(angle)], axis=0)
    return table.astype(np.float32).astype(ml_dtypes.bfloat16)


def band_matrix():
    band = np.arange(128) // BAND
    return (band[:, None] == band[None, :]).astype(ml_dtypes.bfloat16)


def whiten_rows(values, ones):
    rows, width = values.shape
    bins = width // 2
    real, imag = values[:, :bins], values[:, bins:]
    magnitude = jnp.sqrt(real * real + imag * imag)
    parts = bins // 128
    stacked = jnp.concatenate([magnitude[:, i * 128 : (i + 1) * 128] for i in range(parts)], axis=0)
    high = stacked.astype(jnp.bfloat16)
    low = (stacked - high.astype(jnp.float32)).astype(jnp.bfloat16)
    total = jnp.dot(high, ones, preferred_element_type=jnp.float32) + jnp.dot(
        low, ones, preferred_element_type=jnp.float32
    )
    inverse = 1.0 / (total * (1.0 / BAND) + 1e-06)
    inverse = jnp.concatenate([inverse[i * rows : (i + 1) * rows] for i in range(parts)], axis=1)
    return jnp.concatenate([real * inverse, imag * inverse], axis=1).astype(jnp.bfloat16)


def source_kernel(spectra, ones, out):
    rows = [spectra[w].astype(jnp.float32)[0:1] for w in range(spectra.shape[0])]
    out[...] = whiten_rows(jnp.concatenate(rows, axis=0), ones[...])


def whiten_kernel(spectra, ones, out):
    out[0] = whiten_rows(spectra[0].astype(jnp.float32), ones[...])


def whiten_source(spectra, ones):
    windows, _, width = spectra.shape
    return pl.pallas_call(
        source_kernel,
        out_shape=jax.ShapeDtypeStruct((windows, width), jnp.bfloat16),
        compiler_params=pltpu.CompilerParams(vmem_limit_bytes=VMEM),
        cost_estimate=pl.CostEstimate(flops=10**6, bytes_accessed=2 * 2**20, transcendentals=0),
        name="whiten_source",
    )(spectra, ones)


def whiten_all(spectra, ones):
    windows, channels, width = spectra.shape
    block = pl.BlockSpec((1, channels, width), lambda w: (w, 0, 0))
    return pl.pallas_call(
        whiten_kernel,
        grid=(windows,),
        in_specs=[block, pl.BlockSpec(ones.shape, lambda w: (0, 0))],
        out_specs=block,
        out_shape=jax.ShapeDtypeStruct(spectra.shape, jnp.bfloat16),
        compiler_params=pltpu.CompilerParams(vmem_limit_bytes=VMEM),
        cost_estimate=pl.CostEstimate(flops=10**7, bytes_accessed=4 * 2**20, transcendentals=0),
        name="whiten_all",
    )(spectra, ones)


def tree(terms):
    while len(terms) > 1:
        terms = [terms[i] + terms[i + 1] for i in range(0, len(terms), 2)]
    return terms[0]


def correlate_kernel(groups, scale, parity, *refs):
    own_r, own_i, sib_r, sib_i = refs[:4]
    sources = [(refs[4 + 2 * g], refs[5 + 2 * g]) for g in range(groups)]
    cos, sin, out, acc, prod_r, prod_i, src_r, src_i, src_s = refs[4 + 2 * groups :]
    step = pl.program_id(0)
    windows, half = own_r.shape[0], own_r.shape[1]
    per, chunk = sources[0][0].shape[0], own_r.shape[2]
    for g, (re, im) in enumerate(sources):
        rows = slice(g * per, (g + 1) * per)
        a, b = re[...].astype(jnp.float32), im[...].astype(jnp.float32)
        src_r[rows] = a
        src_i[rows] = b
        src_s[rows] = a + b

    @pl.when(step == 0)
    def _():
        acc[...] = jnp.zeros_like(acc)

    def body(q, carry):
        lanes = pl.ds(pl.multiple_of(q * 128, 128), 128)
        for h, (xr, xi) in enumerate(((own_r, own_i), (sib_r, sib_i))):
            first = pl.multiple_of((parity[0] + h) % 2 * half, half)
            re = [xr[w, :, lanes].astype(jnp.float32) for w in range(windows)]
            im = [xi[w, :, lanes].astype(jnp.float32) for w in range(windows)]
            for s in range(groups * per):
                parts_r, parts_i = [], []
                for t in range(0, half, 8):
                    one, two, three = [], [], []
                    for w in range(windows):
                        x, y = re[w][t : t + 8], im[w][t : t + 8]
                        wide = x.shape
                        one.append(jnp.broadcast_to(src_s[s, w : w + 1, lanes], wide) * x)
                        two.append(jnp.broadcast_to(src_r[s, w : w + 1, lanes], wide) * (x + y))
                        three.append(jnp.broadcast_to(src_i[s, w : w + 1, lanes], wide) * (x - y))
                    base = tree(one)
                    parts_r.append(base - tree(three))
                    parts_i.append(base - tree(two))
                rows = pl.ds(s * 2 * half + first, half)
                prod_r[rows, lanes] = jnp.concatenate(parts_r, axis=0).astype(jnp.bfloat16)
                prod_i[rows, lanes] = jnp.concatenate(parts_i, axis=0).astype(jnp.bfloat16)
        return carry

    lax.fori_loop(0, chunk // 128, body, 0)
    acc[...] += jnp.dot(prod_r[...], cos[...], preferred_element_type=jnp.float32) + jnp.dot(
        prod_i[...], sin[...], preferred_element_type=jnp.float32
    )

    @pl.when(step == pl.num_programs(0) - 1)
    def _():
        out[...] = (acc[...] * scale).reshape(out.shape).astype(out.dtype)


def correlate(parity, own, sibling, sources, table, scale):
    windows, half, width = own.shape
    bins = width // 2
    steps = bins // CHUNK
    groups, per = len(sources), sources[0].shape[0]
    n = groups * per

    def pair(shape):
        lead = (0,) * (len(shape) - 1)
        return [
            pl.BlockSpec(shape, lambda j, lead=lead: lead + (j,)),
            pl.BlockSpec(shape, lambda j, lead=lead: lead + (steps + j,)),
        ]

    x_spec, s_spec = pair((windows, half, CHUNK)), pair((per, windows, CHUNK))
    out_shape = (n, 2 * half, LAGS)
    return pl.pallas_call(
        functools.partial(correlate_kernel, groups, scale),
        grid=(steps,),
        in_specs=[pl.BlockSpec(memory_space=pltpu.SMEM)]
        + x_spec * 2
        + s_spec * groups
        + [
            pl.BlockSpec((CHUNK, LAGS), lambda j: (j, 0)),
            pl.BlockSpec((CHUNK, LAGS), lambda j: (steps + j, 0)),
        ],
        out_specs=pl.BlockSpec(out_shape, lambda j: (0, 0, 0)),
        out_shape=jax.ShapeDtypeStruct(out_shape, jnp.bfloat16),
        scratch_shapes=[
            pltpu.VMEM((n * 2 * half, LAGS), jnp.float32),
            pltpu.VMEM((n * 2 * half, CHUNK), jnp.bfloat16),
            pltpu.VMEM((n * 2 * half, CHUNK), jnp.bfloat16),
            pltpu.VMEM((n, windows, CHUNK), jnp.float32),
            pltpu.VMEM((n, windows, CHUNK), jnp.float32),
            pltpu.VMEM((n, windows, CHUNK), jnp.float32),
        ],
        compiler_params=pltpu.CompilerParams(vmem_limit_bytes=VMEM),
        cost_estimate=pl.CostEstimate(
            flops=n * 10**9, bytes_accessed=8 * 2**20, transcendentals=0
        ),
        name=f"correlate_{n}",
    )(parity, own, own, sibling, sibling, *[s for s in sources for _ in range(2)], table, table)


def chan_shift(block, distance):
    size = lax.axis_size("chan")
    return lax.ppermute(block, "chan", [(i, (i + distance) % size) for i in range(size)])


def chip_shift(block, distance):
    size = lax.axis_size("win")
    return lax.ppermute(block, "win", [(i, (i + 2 * distance) % size) for i in range(size)])


def core_swap(block):
    size = lax.axis_size("win")
    return lax.ppermute(block, "win", [(i, i ^ 1) for i in range(size)])


def on_device(spectra, pair_remote, pair_count):
    windows, channels, width = spectra.shape
    bins = width // 2
    scale = 1.0 / math.sqrt(bins * windows)
    ones = jnp.asarray(band_matrix())
    table = jnp.asarray(lag_table(bins))
    parity = (lax.axis_index("win") % 2).astype(jnp.int32)[None]

    source = whiten_source(spectra, ones)
    near = jnp.stack([chan_shift(source, d) for d in OFFSETS])
    own = whiten_all(spectra, ones)
    sibling = core_swap(own)
    up, down, far = chip_shift(near, 1), chip_shift(near, -1), chip_shift(near, 2)

    args = (table, scale)
    c_own = correlate(parity, own, sibling, [near], *args)
    c_two = correlate(parity, own, sibling, [up, down], *args)
    c_far = correlate(parity, own, sibling, [far], *args)
    c_up, c_down = c_two[: len(OFFSETS)], c_two[len(OFFSETS) :]

    chips = lax.axis_size("win") // 2
    chip = lax.axis_index("win") // 2
    home = [c_own, chip_shift(c_down, 1), chip_shift(c_far, 2), chip_shift(c_up, -1)]
    stacked = jnp.stack(home)
    order = (chip - jnp.arange(chips)) % chips
    stacked = stacked[order]
    blocks = jnp.swapaxes(stacked, 0, 1).reshape(len(OFFSETS), chips * 2 * channels, LAGS)
    back = [chan_shift(blocks[i], -d) for i, d in enumerate(OFFSETS)]

    distance = pair_remote[0] - lax.axis_index("chan")
    live = jnp.arange(pair_remote.shape[1], dtype=jnp.int32) < pair_count[0]
    result = jnp.zeros((pair_remote.shape[1],) + back[0].shape, jnp.float32)
    for block, d in zip(back, OFFSETS):
        chosen = (live & (distance == d))[:, None, None]
        result = jnp.where(chosen, block[None].astype(jnp.float32), result)
    return result[None, None]


def solution(mesh):
    in_specs = (P(None, ("chan", "win"), None), P("chan", None), P("chan"))
    out_specs = P("win", "chan", None, None, None)
    return jax.shard_map(
        on_device, mesh=mesh, in_specs=in_specs, out_specs=out_specs, check_vma=False
    )
```

time: 484 us -> 95.6 us (0.20)
  the two profiles are of different devices: /device:TPU:34 before, /device:TPU:8 now
where the time goes in v1:
time: 95.6 us; the launch traced here: 95.3 us
  starting transfers between devices  37.1 us (39%)
  Pallas kernels  31.1 us (33%)
  waiting for transfers between devices  22.2 us (23%)
  local copies, waits for them, and re-layouts  2.95 us (3%)
  other arithmetic  1.12 us (1%)
    pallas_call x3, Pallas kernels, correlate(): pl.pallas_call(functools.partial(correlate_kernel, groups, scale), grid=(...  28.5 us
    ppermute x6, starting transfers between devices, chip_shift(): lax.ppermute(block, 'win', [(i, (i + 2 * distance) % size) for i in range...  18.9 us
    ppermute x8, starting transfers between devices, chan_shift(): lax.ppermute(block, 'chan', [(i, (i + distance) % size) for i in range(si...  18.1 us
    ppermute x8, waiting for transfers between devices, chan_shift(): lax.ppermute(block, 'chan', [(i, (i + distance) % size) for i in range(si...  11.5 us
    ppermute x6, waiting for transfers between devices, chip_shift(): lax.ppermute(block, 'win', [(i, (i + 2 * distance) % size) for i in range...  10.7 us
    unnamed x6, local copies, waits for them, and re-layouts  2.35 us
    pallas_call x1, Pallas kernels, whiten_all(): pl.pallas_call(whiten_kernel, grid=(windows,), in_specs=[block, pl.BlockS...  2.19 us
  transfers between devices with their start and end apart: 15, of which 9 were waited for; matrix products, arithmetic and copies ran while one was open for 0% of the time, Pallas kernels for 30%

profile of v1, /device:TPU:8, one launch (start us, length us, event | category | flops | bytes accessed | tf_op | source)
XLA Modules:
  0.0 95.3 jit_solution(10050523410254018765)
XLA Ops:
  0.0 0.0 copy-start
  0.0 1.6 %copy-done = bf16[8,16,8192]{2,1,0:T(8,128)(2,1)S(1)} copy-done((bf16[8,16,8192]{2,1,0:T(8,128)(2,1)S(1)}, bf16[8,16,8192]{2,1,0:T(8,128)(2,1)}, u32[]{:S(2)}) %copy-start) | copy-done | bytes 2097176
  1.6 0.0 copy-start.1
  1.6 0.8 copy-done.1
  2.4 2.2 %whiten_all.1.refs_0_.refs_1_ = bf16[8,16,8192]{2,1,0:T(8,128)(2,1)S(1)} custom-call(bf16[8,16,8192]{2,1,0:T(8,128)(2,1)S(1)} %copy-done, bf16[128,128]{1,0:T(8,128)(2,1)S(1)} %copy-done.1), custom_call_target="tpu_custom_call" | custom-call | flops 10000000 | bytes 4194304 | tf_op jit(solution)/shard_map/whiten_all/pallas_call | solution.py:74
  4.5 0.0 copy-start.2
  4.6 0.1 collective-permute-start
  4.7 0.4 whiten_source.1
  5.0 3.1 %collective-permute-start.4 = (bf16[8,8192]{1,0:T(8,128)(2,1)S(1)}, bf16[8,8192]{1,0:T(8,128)(2,1)S(1)}, u32[]{:S(2)}, u32[]{:S(2)}) collective-permute-start(bf16[8,8192]{1,0:T(8,128)(2,1)S(1)} %whiten_source.1), channel_id=1, source_target_pairs={{0,2},{1,3},{2,4},{3,5},{4,6},{5,7},{6,8},{7,9},{8,10},{9,11},{10,... | collective-permute-start | bytes 393224 | tf_op jit(solution)/shard_map/ppermute | solution.py:190
  8.1 0.6 collective-permute-start.3
  8.7 4.8 %collective-permute-start.2 = (bf16[8,8192]{1,0:T(8,128)(2,1)S(1)}, bf16[8,8192]{1,0:T(8,128)(2,1)S(1)}, u32[]{:S(2)}, u32[]{:S(2)}) collective-permute-start(bf16[8,8192]{1,0:T(8,128)(2,1)S(1)} %whiten_source.1), channel_id=1, source_target_pairs={{0,15},{1,0},{2,1},{3,2},{4,3},{5,4},{6,5},{7,6},{8,7},{9,8},{10,9... | collective-permute-start | bytes 393224 | tf_op jit(solution)/shard_map/ppermute | solution.py:190
  13.5 0.8 collective-permute-start.1
  14.3 1.7 %collective-permute-done.4 = bf16[8,8192]{1,0:T(8,128)(2,1)S(1)} collective-permute-done((bf16[8,8192]{1,0:T(8,128)(2,1)S(1)}, bf16[8,8192]{1,0:T(8,128)(2,1)S(1)}, u32[]{:S(2)}, u32[]{:S(2)}) %collective-permute-start.4) | collective-permute-done | bytes 131104 | tf_op jit(solution)/shard_map/ppermute | solution.py:190
  16.0 2.6 %collective-permute-done.3 = bf16[8,8192]{1,0:T(8,128)(2,1)S(1)} collective-permute-done((bf16[8,8192]{1,0:T(8,128)(2,1)S(1)}, bf16[8,8192]{1,0:T(8,128)(2,1)S(1)}, u32[]{:S(2)}, u32[]{:S(2)}) %collective-permute-start.3) | collective-permute-done | bytes 131104 | tf_op jit(solution)/shard_map/ppermute | solution.py:190
  18.6 0.6 collective-permute-done.2
  19.1 0.9 collective-permute-done.1
  20.0 0.1 pad_maximum_fusion.refs_4_.refs_5_
  20.1 1.6 %collective-permute-start.5 = (bf16[4,8,8192]{2,1,0:T(8,128)(2,1)S(1)}, bf16[4,8,8192]{2,1,0:T(8,128)(2,1)S(1)}, u32[]{:S(2)}, u32[]{:S(2)}) collective-permute-start(bf16[4,8,8192]{2,1,0:T(8,128)(2,1)S(1)} %pad_maximum_fusion.refs_4_.refs_5_), channel_id=1, source_target_pairs={{0,32},{16,48},{32,64},{48,80},{64,96},{80,112},{96,0},{112,16},{1... | collective-permute-start | bytes 1572872 | tf_op jit(solution)/shard_map/ppermute | solution.py:195
  21.8 0.5 collective-permute-start.6
  22.9 0.0 copy-done.2
  22.9 2.4 %collective-permute-start.8 = (bf16[4,8,8192]{2,1,0:T(8,128)(2,1)S(1)}, bf16[4,8,8192]{2,1,0:T(8,128)(2,1)S(1)}, u32[]{:S(2)}, u32[]{:S(2)}) collective-permute-start(bf16[4,8,8192]{2,1,0:T(8,128)(2,1)S(1)} %pad_maximum_fusion.refs_4_.refs_5_), channel_id=1, source_target_pairs={{0,64},{16,80},{32,96},{48,112},{64,0},{80,16},{96,32},{112,48},{1... | collective-permute-start | bytes 1572872 | tf_op jit(solution)/shard_map/ppermute | solution.py:195
  25.3 9.7 %collective-permute-done.5.refs_4_.refs_5_ = bf16[4,8,8192]{2,1,0:T(8,128)(2,1)S(1)} collective-permute-done((bf16[4,8,8192]{2,1,0:T(8,128)(2,1)S(1)}, bf16[4,8,8192]{2,1,0:T(8,128)(2,1)S(1)}, u32[]{:S(2)}, u32[]{:S(2)}) %collective-permute-start.5) | collective-permute-done | bytes 524320 | tf_op jit(solution)/shard_map/ppermute | solution.py:195
  35.0 1.0 %collective-permute-done.6.refs_6_.refs_7_ = bf16[4,8,8192]{2,1,0:T(8,128)(2,1)} collective-permute-done((bf16[4,8,8192]{2,1,0:T(8,128)(2,1)S(1)}, bf16[4,8,8192]{2,1,0:T(8,128)(2,1)}, u32[]{:S(2)}, u32[]{:S(2)}) %collective-permute-start.6) | collective-permute-done | bytes 524320 | tf_op jit(solution)/shard_map/ppermute | solution.py:195
  36.0 0.0 collective-permute-done.refs_2_.refs_3_
  36.0 13.0 %correlate_8.1 = bf16[8,32,256]{2,1,0:T(8,128)(2,1)S(1)} custom-call(s32[1]{0:T(128)} %bitcast.2.parity, bf16[8,16,8192]{2,1,0:T(8,128)(2,1)S(1)} %whiten_all.1.refs_0_.refs_1_, bf16[8,16,8192]{2,1,0:T(8,128)(2,1)S(1)} %whiten_all.1.refs_0_.refs_1_, bf16[8,16,8192]{2,1,0:T(8,128)(2,1)} %collective-permute-done.refs_2_.refs_3_, ...), custom_call_target="tpu_custom_call" | custom-call | flops 8000000000 | bytes 8388608 | tf_op jit(solution)/shard_map/correlate_8/pallas_call | solution.py:160
  49.0 9.2 %collective-permute-start.10 = (bf16[4,32,256]{2,1,0:T(8,128)(2,1)S(1)}, bf16[4,32,256]{2,1,0:T(8,128)(2,1)S(1)}, u32[]{:S(2)}, u32[]{:S(2)}) collective-permute-start(bf16[4,32,256]{2,1,0:T(8,128)(2,1)S(1)} %get-tuple-element.12), channel_id=1, source_target_pairs={{0,96},{16,112},{32,0},{48,16},{64,32},{80,48},{96,64},{112,80},{1... | collective-permute-start | bytes 196616 | tf_op jit(solution)/shard_map/ppermute | solution.py:195
  58.2 0.0 collective-permute-done.8.refs_4_.refs_5_
  58.2 7.8 %correlate_4.3 = bf16[4,32,256]{2,1,0:T(8,128)(2,1)S(1)} custom-call(s32[1]{0:T(128)} %bitcast.2.parity, bf16[8,16,8192]{2,1,0:T(8,128)(2,1)S(1)} %whiten_all.1.refs_0_.refs_1_, bf16[8,16,8192]{2,1,0:T(8,128)(2,1)S(1)} %whiten_all.1.refs_0_.refs_1_, bf16[8,16,8192]{2,1,0:T(8,128)(2,1)} %collective-permute-done.refs_2_.refs_3_, ...), custom_call_target="tpu_custom_call" | custom-call | flops 4000000000 | bytes 8388608 | tf_op jit(solution)/shard_map/correlate_4/pallas_call | solution.py:160
  66.0 2.7 %collective-permute-start.9 = (bf16[4,32,256]{2,1,0:T(8,128)(2,1)S(1)}, bf16[4,32,256]{2,1,0:T(8,128)(2,1)S(1)}, u32[]{:S(2)}, u32[]{:S(2)}) collective-permute-start(bf16[4,32,256]{2,1,0:T(8,128)(2,1)S(1)} %correlate_4.3), channel_id=1, source_target_pairs={{0,64},{16,80},{32,96},{48,112},{64,0},{80,16},{96,32},{112,48},{1... | collective-permute-start | bytes 196616 | tf_op jit(solution)/shard_map/ppermute | solution.py:195
  68.7 2.6 %collective-permute-start.7 = (bf16[4,32,256]{2,1,0:T(8,128)(2,1)S(1)}, bf16[4,32,256]{2,1,0:T(8,128)(2,1)S(1)}, u32[]{:S(2)}, u32[]{:S(2)}) collective-permute-start(bf16[4,32,256]{2,1,0:T(8,128)(2,1)S(1)} %get-tuple-element.11), channel_id=1, source_target_pairs={{0,32},{16,48},{32,64},{48,80},{64,96},{80,112},{96,0},{112,16},{1... | collective-permute-start | bytes 196616 | tf_op jit(solution)/shard_map/ppermute | solution.py:195
  71.3 7.8 %correlate_4.2 = bf16[4,32,256]{2,1,0:T(8,128)(2,1)S(1)} custom-call(s32[1]{0:T(128)} %bitcast.2.parity, bf16[8,16,8192]{2,1,0:T(8,128)(2,1)S(1)} %whiten_all.1.refs_0_.refs_1_, bf16[8,16,8192]{2,1,0:T(8,128)(2,1)S(1)} %whiten_all.1.refs_0_.refs_1_, bf16[8,16,8192]{2,1,0:T(8,128)(2,1)} %collective-permute-done.refs_2_.refs_3_, ...), custom_call_target="tpu_custom_call" | custom-call | flops 4000000000 | bytes 8388608 | tf_op jit(solution)/shard_map/correlate_4/pallas_call | solution.py:160
  79.0 0.0 collective-permute-done.10
  79.1 0.0 collective-permute-done.9
  79.1 0.0 collective-permute-done.7
  79.1 0.6 gather_fusion
  79.7 3.5 %collective-permute-start.14 = (bf16[128,256]{1,0:T(8,128)(2,1)S(1)}, bf16[128,256]{1,0:T(8,128)(2,1)S(1)}, u32[]{:S(2)}, u32[]{:S(2)}) collective-permute-start(bf16[128,256]{1,0:T(8,128)(2,1)S(1)} %bitcast.37), channel_id=1, source_target_pairs={{0,2},{1,3},{2,4},{3,5},{4,6},{5,7},{6,8},{7,9},{8,10},{9,11},{10,... | collective-permute-start | bytes 196616 | tf_op jit(solution)/shard_map/ppermute | solution.py:190
  83.3 0.6 collective-permute-start.13
  83.9 4.7 %collective-permute-start.12 = (bf16[128,256]{1,0:T(8,128)(2,1)S(1)}, bf16[128,256]{1,0:T(8,128)(2,1)S(1)}, u32[]{:S(2)}, u32[]{:S(2)}) collective-permute-start(bf16[128,256]{1,0:T(8,128)(2,1)S(1)} %bitcast.34), channel_id=1, source_target_pairs={{0,15},{1,0},{2,1},{3,2},{4,3},{5,4},{6,5},{7,6},{8,7},{9,8},{10,9... | collective-permute-start | bytes 196616 | tf_op jit(solution)/shard_map/ppermute | solution.py:190
  88.6 0.0 collective-permute-start.11
  88.6 0.0 collective-permute-done.14
  88.6 2.2 %collective-permute-done.13 = bf16[128,256]{1,0:T(8,128)(2,1)S(1)} collective-permute-done((bf16[128,256]{1,0:T(8,128)(2,1)S(1)}, bf16[128,256]{1,0:T(8,128)(2,1)S(1)}, u32[]{:S(2)}, u32[]{:S(2)}) %collective-permute-start.13) | collective-permute-done | bytes 65568 | tf_op jit(solution)/shard_map/ppermute | solution.py:190
  90.9 0.3 collective-permute-done.12
  91.1 3.2 %collective-permute-done.11 = bf16[128,256]{1,0:T(8,128)(2,1)S(1)} collective-permute-done((bf16[128,256]{1,0:T(8,128)(2,1)S(1)}, bf16[128,256]{1,0:T(8,128)(2,1)S(1)}, u32[]{:S(2)}, u32[]{:S(2)}) %collective-permute-start.11) | collective-permute-done | bytes 65568 | tf_op jit(solution)/shard_map/ppermute | solution.py:190
  94.4 0.9 select_select_fusion
  (11 shorter events, 0.1 us)
Async XLA Ops:
  0.0 1.6 %copy-start = (bf16[8,16,8192]{2,1,0:T(8,128)(2,1)S(1)}, bf16[8,16,8192]{2,1,0:T(8,128)(2,1)}, u32[]{:S(2)}) copy-start(bf16[8,16,8192]{2,1,0:T(8,128)(2,1)} %spectra.3) | copy-start | bytes 6291460
  1.6 0.8 copy-start.1
  4.5 18.4 %copy-start.2 = (s32[1,4]{1,0:T(1,128)S(1)}, s32[1,4]{1,0:T(1,128)}, u32[]{:S(2)}) copy-start(s32[1,4]{1,0:T(1,128)} %param.6) | copy-start | bytes 52
  4.6 31.4 %collective-permute-start = (bf16[8,16,8192]{2,1,0:T(8,128)(2,1)S(1)}, bf16[8,16,8192]{2,1,0:T(8,128)(2,1)}, u32[]{:S(2)}, u32[]{:S(2)}) collective-permute-start(bf16[8,16,8192]{2,1,0:T(8,128)(2,1)S(1)} %whiten_all.1.refs_0_.refs_1_), channel_id=1, source_target_pairs={{0,16},{16,0},{32,48},{48,32},{64,80},{80,64},{96,112},{112,96},{1... | collective-permute-start | bytes 6291464 | tf_op jit(solution)/shard_map/ppermute | solution.py:200
  5.0 10.9 %collective-permute-start.4 = (bf16[8,8192]{1,0:T(8,128)(2,1)S(1)}, bf16[8,8192]{1,0:T(8,128)(2,1)S(1)}, u32[]{:S(2)}, u32[]{:S(2)}) collective-permute-start(bf16[8,8192]{1,0:T(8,128)(2,1)S(1)} %whiten_source.1), channel_id=1, source_target_pairs={{0,2},{1,3},{2,4},{3,5},{4,6},{5,7},{6,8},{7,9},{8,10},{9,11},{10,... | collective-permute-start | bytes 393224 | tf_op jit(solution)/shard_map/ppermute | solution.py:190
  8.1 10.4 %collective-permute-start.3 = (bf16[8,8192]{1,0:T(8,128)(2,1)S(1)}, bf16[8,8192]{1,0:T(8,128)(2,1)S(1)}, u32[]{:S(2)}, u32[]{:S(2)}) collective-permute-start(bf16[8,8192]{1,0:T(8,128)(2,1)S(1)} %whiten_source.1), channel_id=1, source_target_pairs={{0,1},{1,2},{2,3},{3,4},{4,5},{5,6},{6,7},{7,8},{8,9},{9,10},{10,1... | collective-permute-start | bytes 393224 | tf_op jit(solution)/shard_map/ppermute | solution.py:190
  8.7 10.4 %collective-permute-start.2 = (bf16[8,8192]{1,0:T(8,128)(2,1)S(1)}, bf16[8,8192]{1,0:T(8,128)(2,1)S(1)}, u32[]{:S(2)}, u32[]{:S(2)}) collective-permute-start(bf16[8,8192]{1,0:T(8,128)(2,1)S(1)} %whiten_source.1), channel_id=1, source_target_pairs={{0,15},{1,0},{2,1},{3,2},{4,3},{5,4},{6,5},{7,6},{8,7},{9,8},{10,9... | collective-permute-start | bytes 393224 | tf_op jit(solution)/shard_map/ppermute | solution.py:190
  13.5 6.6 %collective-permute-start.1 = (bf16[8,8192]{1,0:T(8,128)(2,1)S(1)}, bf16[8,8192]{1,0:T(8,128)(2,1)S(1)}, u32[]{:S(2)}, u32[]{:S(2)}) collective-permute-start(bf16[8,8192]{1,0:T(8,128)(2,1)S(1)} %whiten_source.1), channel_id=1, source_target_pairs={{0,14},{1,15},{2,0},{3,1},{4,2},{5,3},{6,4},{7,5},{8,6},{9,7},{10,... | collective-permute-start | bytes 393224 | tf_op jit(solution)/shard_map/ppermute | solution.py:190
  20.1 14.9 %collective-permute-start.5 = (bf16[4,8,8192]{2,1,0:T(8,128)(2,1)S(1)}, bf16[4,8,8192]{2,1,0:T(8,128)(2,1)S(1)}, u32[]{:S(2)}, u32[]{:S(2)}) collective-permute-start(bf16[4,8,8192]{2,1,0:T(8,128)(2,1)S(1)} %pad_maximum_fusion.refs_4_.refs_5_), channel_id=1, source_target_pairs={{0,32},{16,48},{32,64},{48,80},{64,96},{80,112},{96,0},{112,16},{1... | collective-permute-start | bytes 1572872 | tf_op jit(solution)/shard_map/ppermute | solution.py:195
  21.8 14.2 %collective-permute-start.6 = (bf16[4,8,8192]{2,1,0:T(8,128)(2,1)S(1)}, bf16[4,8,8192]{2,1,0:T(8,128)(2,1)}, u32[]{:S(2)}, u32[]{:S(2)}) collective-permute-start(bf16[4,8,8192]{2,1,0:T(8,128)(2,1)S(1)} %pad_maximum_fusion.refs_4_.refs_5_), channel_id=1, source_target_pairs={{0,96},{16,112},{32,0},{48,16},{64,32},{80,48},{96,64},{112,80},{1... | collective-permute-start | bytes 1572872 | tf_op jit(solution)/shard_map/ppermute | solution.py:195
  22.9 35.3 %collective-permute-start.8 = (bf16[4,8,8192]{2,1,0:T(8,128)(2,1)S(1)}, bf16[4,8,8192]{2,1,0:T(8,128)(2,1)S(1)}, u32[]{:S(2)}, u32[]{:S(2)}) collective-permute-start(bf16[4,8,8192]{2,1,0:T(8,128)(2,1)S(1)} %pad_maximum_fusion.refs_4_.refs_5_), channel_id=1, source_target_pairs={{0,64},{16,80},{32,96},{48,112},{64,0},{80,16},{96,32},{112,48},{1... | collective-permute-start | bytes 1572872 | tf_op jit(solution)/shard_map/ppermute | solution.py:195
  49.0 30.0 %collective-permute-start.10 = (bf16[4,32,256]{2,1,0:T(8,128)(2,1)S(1)}, bf16[4,32,256]{2,1,0:T(8,128)(2,1)S(1)}, u32[]{:S(2)}, u32[]{:S(2)}) collective-permute-start(bf16[4,32,256]{2,1,0:T(8,128)(2,1)S(1)} %get-tuple-element.12), channel_id=1, source_target_pairs={{0,96},{16,112},{32,0},{48,16},{64,32},{80,48},{96,64},{112,80},{1... | collective-permute-start | bytes 196616 | tf_op jit(solution)/shard_map/ppermute | solution.py:195
  66.0 13.1 %collective-permute-start.9 = (bf16[4,32,256]{2,1,0:T(8,128)(2,1)S(1)}, bf16[4,32,256]{2,1,0:T(8,128)(2,1)S(1)}, u32[]{:S(2)}, u32[]{:S(2)}) collective-permute-start(bf16[4,32,256]{2,1,0:T(8,128)(2,1)S(1)} %correlate_4.3), channel_id=1, source_target_pairs={{0,64},{16,80},{32,96},{48,112},{64,0},{80,16},{96,32},{112,48},{1... | collective-permute-start | bytes 196616 | tf_op jit(solution)/shard_map/ppermute | solution.py:195
  68.7 10.4 %collective-permute-start.7 = (bf16[4,32,256]{2,1,0:T(8,128)(2,1)S(1)}, bf16[4,32,256]{2,1,0:T(8,128)(2,1)S(1)}, u32[]{:S(2)}, u32[]{:S(2)}) collective-permute-start(bf16[4,32,256]{2,1,0:T(8,128)(2,1)S(1)} %get-tuple-element.11), channel_id=1, source_target_pairs={{0,32},{16,48},{32,64},{48,80},{64,96},{80,112},{96,0},{112,16},{1... | collective-permute-start | bytes 196616 | tf_op jit(solution)/shard_map/ppermute | solution.py:195
  79.7 8.9 %collective-permute-start.14 = (bf16[128,256]{1,0:T(8,128)(2,1)S(1)}, bf16[128,256]{1,0:T(8,128)(2,1)S(1)}, u32[]{:S(2)}, u32[]{:S(2)}) collective-permute-start(bf16[128,256]{1,0:T(8,128)(2,1)S(1)} %bitcast.37), channel_id=1, source_target_pairs={{0,2},{1,3},{2,4},{3,5},{4,6},{5,7},{6,8},{7,9},{8,10},{9,11},{10,... | collective-permute-start | bytes 196616 | tf_op jit(solution)/shard_map/ppermute | solution.py:190
  83.3 7.6 %collective-permute-start.13 = (bf16[128,256]{1,0:T(8,128)(2,1)S(1)}, bf16[128,256]{1,0:T(8,128)(2,1)S(1)}, u32[]{:S(2)}, u32[]{:S(2)}) collective-permute-start(bf16[128,256]{1,0:T(8,128)(2,1)S(1)} %bitcast.36), channel_id=1, source_target_pairs={{0,1},{1,2},{2,3},{3,4},{4,5},{5,6},{6,7},{7,8},{8,9},{9,10},{10,1... | collective-permute-start | bytes 196616 | tf_op jit(solution)/shard_map/ppermute | solution.py:190
  83.9 7.3 %collective-permute-start.12 = (bf16[128,256]{1,0:T(8,128)(2,1)S(1)}, bf16[128,256]{1,0:T(8,128)(2,1)S(1)}, u32[]{:S(2)}, u32[]{:S(2)}) collective-permute-start(bf16[128,256]{1,0:T(8,128)(2,1)S(1)} %bitcast.34), channel_id=1, source_target_pairs={{0,15},{1,0},{2,1},{3,2},{4,3},{5,4},{6,5},{7,6},{8,7},{9,8},{10,9... | collective-permute-start | bytes 196616 | tf_op jit(solution)/shard_map/ppermute | solution.py:190
  88.6 5.8 %collective-permute-start.11 = (bf16[128,256]{1,0:T(8,128)(2,1)S(1)}, bf16[128,256]{1,0:T(8,128)(2,1)S(1)}, u32[]{:S(2)}, u32[]{:S(2)}) collective-permute-start(bf16[128,256]{1,0:T(8,128)(2,1)S(1)} %bitcast.33), channel_id=1, source_target_pairs={{0,14},{1,15},{2,0},{3,1},{4,2},{5,3},{6,4},{7,5},{8,6},{9,7},{10,... | collective-permute-start | bytes 196616 | tf_op jit(solution)/shard_map/ppermute | solution.py:190

commit v2 on v1

v2 whole, which is shorter than its diff:
```python
import functools
import math

import jax
import jax.numpy as jnp
import ml_dtypes
import numpy as np
from jax import lax
from jax.experimental import pallas as pl
from jax.experimental.pallas import tpu as pltpu
from jax.sharding import PartitionSpec as P

BAND = 64
LAGS = 256
REACH = 2
VMEM = 24 * 1024 * 1024
OFFSETS = (-2, -1, 1, 2)


def lag_table(bins):
    t = np.arange(LAGS) - LAGS // 2
    f = np.arange(bins)
    angle = ((f[:, None] * t[None, :]) % (2 * bins)) * (math.pi / bins)
    table = np.concatenate([np.cos(angle), -np.sin(angle)], axis=0)
    return table.astype(np.float32).astype(ml_dtypes.bfloat16)


def band_matrix():
    row = lax.broadcasted_iota(jnp.int32, (128, 128), 0) // BAND
    column = lax.broadcasted_iota(jnp.int32, (128, 128), 1) // BAND
    return jnp.where(row == column, 1.0, 0.0).astype(jnp.bfloat16)


def whiten_rows(values):
    ones = band_matrix()
    rows, width = values.shape
    bins = width // 2
    real, imag = values[:, :bins], values[:, bins:]
    magnitude = jnp.sqrt(real * real + imag * imag)
    parts = bins // 128
    stacked = jnp.concatenate([magnitude[:, i * 128 : (i + 1) * 128] for i in range(parts)], axis=0)
    high = stacked.astype(jnp.bfloat16)
    low = (stacked - high.astype(jnp.float32)).astype(jnp.bfloat16)
    total = jnp.dot(high, ones, preferred_element_type=jnp.float32) + jnp.dot(
        low, ones, preferred_element_type=jnp.float32
    )
    inverse = 1.0 / (total * (1.0 / BAND) + 1e-06)
    inverse = jnp.concatenate([inverse[i * rows : (i + 1) * rows] for i in range(parts)], axis=1)
    return jnp.concatenate([real * inverse, imag * inverse], axis=1).astype(jnp.bfloat16)


def source_kernel(spectra, out):
    rows = [spectra[w].astype(jnp.float32)[0:1] for w in range(spectra.shape[0])]
    out[...] = whiten_rows(jnp.concatenate(rows, axis=0))


def whiten_kernel(own, sibling, own_out, sibling_out):
    own_out[0] = whiten_rows(own[0].astype(jnp.float32))
    sibling_out[0] = whiten_rows(sibling[0].astype(jnp.float32))


def whiten_source(spectra):
    windows, _, width = spectra.shape
    return pl.pallas_call(
        source_kernel,
        out_shape=jax.ShapeDtypeStruct((windows, width), jnp.bfloat16),
        compiler_params=pltpu.CompilerParams(vmem_limit_bytes=VMEM),
        cost_estimate=pl.CostEstimate(flops=10**6, bytes_accessed=2 * 2**20, transcendentals=0),
        name="whiten_source",
    )(spectra)


def whiten_both(own, sibling):
    windows, channels, width = own.shape
    block = pl.BlockSpec((1, channels, width), lambda w: (w, 0, 0))
    shape = jax.ShapeDtypeStruct(own.shape, jnp.bfloat16)
    return pl.pallas_call(
        whiten_kernel,
        grid=(windows,),
        in_specs=[block, block],
        out_specs=[block, block],
        out_shape=[shape, shape],
        compiler_params=pltpu.CompilerParams(vmem_limit_bytes=VMEM),
        cost_estimate=pl.CostEstimate(flops=10**9, bytes_accessed=8 * 2**20, transcendentals=0),
        name="whiten_both",
    )(own, sibling)


def correlate_kernel(groups, scale, parity, *refs):
    own, sib = refs[:2]
    sources = refs[2 : 2 + groups]
    table_hbm, out, prod_r, prod_i, src_r, src_i, src_s, table, done = refs[2 + groups :]
    fetch = pltpu.make_async_copy(table_hbm, table, done)
    fetch.start()
    windows, half, width = own.shape
    bins = width // 2
    per = sources[0].shape[0]
    for g, ref in enumerate(sources):
        rows = slice(g * per, (g + 1) * per)
        a, b = ref[:, :, :bins].astype(jnp.float32), ref[:, :, bins:].astype(jnp.float32)
        src_r[rows] = a
        src_i[rows] = b
        src_s[rows] = a + b

    def body(q, carry):
        lanes = pl.ds(pl.multiple_of(q * 128, 128), 128)
        upper = pl.ds(pl.multiple_of(bins + q * 128, 128), 128)
        for h, ref in enumerate((own, sib)):
            place = (parity[0] + h) % 2
            for t in range(0, half, 8):
                chan = []
                for w in range(windows):
                    x = ref[w, :, lanes].astype(jnp.float32)[t : t + 8]
                    y = ref[w, :, upper].astype(jnp.float32)[t : t + 8]
                    chan.append((x, x + y, x - y))
                for s in range(groups * per):
                    total = None
                    for w in range(windows):
                        terms = [
                            jnp.broadcast_to(r[s, w : w + 1, lanes], (8, 128)) * c
                            for r, c in zip((src_s, src_r, src_i), chan[w])
                        ]
                        total = terms if total is None else [p + q for p, q in zip(total, terms)]
                    tile = (s * 2 + place) * (half // 8) + t // 8
                    prod_r[tile, :, lanes] = (total[0] - total[2]).astype(jnp.bfloat16)
                    prod_i[tile, :, lanes] = (total[0] - total[1]).astype(jnp.bfloat16)
        return carry

    def rows(ref):
        return ref[...].reshape(ref.shape[0] * 8, bins)

    lax.fori_loop(0, bins // 128, body, 0)
    fetch.wait()
    total = jnp.dot(rows(prod_r), table[:bins], preferred_element_type=jnp.float32) + jnp.dot(
        rows(prod_i), table[bins:], preferred_element_type=jnp.float32
    )
    out[...] = (total * scale).reshape(out.shape).astype(out.dtype)


def correlate(parity, own, sibling, sources, table, scale):
    windows, half, width = own.shape
    bins = width // 2
    groups, per = len(sources), sources[0].shape[0]
    n = groups * per
    whole = pl.BlockSpec(memory_space=pltpu.VMEM)
    return pl.pallas_call(
        functools.partial(correlate_kernel, groups, scale),
        in_specs=[pl.BlockSpec(memory_space=pltpu.SMEM)] + [whole] * (2 + groups)
        + [pl.BlockSpec(memory_space=pl.ANY)],
        out_specs=whole,
        out_shape=jax.ShapeDtypeStruct((n, 2 * half, LAGS), jnp.bfloat16),
        scratch_shapes=[
            pltpu.VMEM((n * 2 * half // 8, 8, bins), jnp.bfloat16),
            pltpu.VMEM((n * 2 * half // 8, 8, bins), jnp.bfloat16),
            pltpu.VMEM((n, windows, bins), jnp.float32),
            pltpu.VMEM((n, windows, bins), jnp.float32),
            pltpu.VMEM((n, windows, bins), jnp.float32),
            pltpu.VMEM(table.shape, table.dtype),
            pltpu.SemaphoreType.DMA,
        ],
        compiler_params=pltpu.CompilerParams(vmem_limit_bytes=VMEM),
        cost_estimate=pl.CostEstimate(
            flops=n * 10**9, bytes_accessed=8 * 2**20, transcendentals=0
        ),
        name=f"correlate_{n}",
    )(parity, own, sibling, *sources, table)


def chan_shift(block, distance):
    size = lax.axis_size("chan")
    return lax.ppermute(block, "chan", [(i, (i + distance) % size) for i in range(size)])


def chip_shift(block, distance):
    size = lax.axis_size("win")
    return lax.ppermute(block, "win", [(i, (i + 2 * distance) % size) for i in range(size)])


def core_swap(block):
    size = lax.axis_size("win")
    return lax.ppermute(block, "win", [(i, i ^ 1) for i in range(size)])


def on_device(spectra, pair_remote, pair_count):
    windows, channels, width = spectra.shape
    bins = width // 2
    scale = 1.0 / math.sqrt(bins * windows)
    table = jnp.asarray(lag_table(bins))
    parity = (lax.axis_index("win") % 2).astype(jnp.int32)[None]

    other = core_swap(spectra)
    source = whiten_source(spectra)
    near = jnp.stack([chan_shift(source, d) for d in OFFSETS])
    own, sibling = whiten_both(spectra, other)

    args = (table, scale)
    up, down = chip_shift(near, 1), chip_shift(near, -1)
    part = len(OFFSETS) // 2
    c_first = correlate(parity, own, sibling, [near[:part]], *args)
    near, c_first = lax.optimization_barrier((near, c_first))
    far = chip_shift(near, 2)
    c_two = correlate(parity, own, sibling, [up, down], *args)
    c_up, c_down = c_two[: len(OFFSETS)], c_two[len(OFFSETS) :]
    far, c_up, c_down = lax.optimization_barrier((far, c_up, c_down))
    c_far = correlate(parity, own, sibling, [far], *args)
    last, c_far = lax.optimization_barrier((near[part:], c_far))
    c_own = jnp.concatenate([c_first, correlate(parity, own, sibling, [last], *args)])

    chips = lax.axis_size("win") // 2
    chip = lax.axis_index("win") // 2
    home = [c_own, chip_shift(c_down, 1), chip_shift(c_far, 2), chip_shift(c_up, -1)]
    stacked = jnp.stack(home)
    order = (chip - jnp.arange(chips)) % chips
    stacked = stacked[order]
    blocks = jnp.swapaxes(stacked, 0, 1).reshape(len(OFFSETS), chips * 2 * channels, LAGS)
    back = [chan_shift(blocks[i], -d) for i, d in enumerate(OFFSETS)]

    distance = pair_remote[0] - lax.axis_index("chan")
    live = jnp.arange(pair_remote.shape[1], dtype=jnp.int32) < pair_count[0]
    result = jnp.zeros((pair_remote.shape[1],) + back[0].shape, jnp.float32)
    for block, d in zip(back, OFFSETS):
        chosen = (live & (distance == d))[:, None, None]
        result = jnp.where(chosen, block[None].astype(jnp.float32), result)
    return result[None, None]


def solution(mesh):
    in_specs = (P(None, ("chan", "win"), None), P("chan", None), P("chan"))
    out_specs = P("win", "chan", None, None, None)
    return jax.shard_map(
        on_device, mesh=mesh, in_specs=in_specs, out_specs=out_specs, check_vma=False
    )
```

time: 95.6 us -> 73.5 us (0.77)
  the two profiles are of different devices: /device:TPU:8 before, /device:TPU:0 now
where the time goes in v2:
time: 73.5 us; the launch traced here: 73.3 us
  Pallas kernels  31.9 us (43%)
  starting transfers between devices  26.4 us (36%)
  waiting for transfers between devices  12.3 us (17%)
  other arithmetic  1.15 us (2%)
  between operations  0.87 us (1%)
    pallas_call x4, Pallas kernels, correlate(): pl.pallas_call(functools.partial(correlate_kernel, groups, scale), in_spe...  23.4 us
    ppermute x8, starting transfers between devices, chan_shift(): lax.ppermute(block, 'chan', [(i, (i + distance) % size) for i in range(si...  17.7 us
    ppermute x8, waiting for transfers between devices, chan_shift(): lax.ppermute(block, 'chan', [(i, (i + distance) % size) for i in range(si...  10.5 us
    ppermute x6, starting transfers between devices, chip_shift(): lax.ppermute(block, 'win', [(i, (i + 2 * distance) % size) for i in range...  8.71 us
    pallas_call x1, Pallas kernels, whiten_both(): pl.pallas_call(whiten_kernel, grid=(windows,), in_specs=[block, block], o...  6.58 us
    pallas_call x1, Pallas kernels, whiten_source(): pl.pallas_call(source_kernel, out_shape=jax.ShapeDtypeStruct((windows, wi...  1.99 us
    ppermute x6, waiting for transfers between devices, chip_shift(): lax.ppermute(block, 'win', [(i, (i + 2 * distance) % size) for i in range...  1.79 us
  transfers between devices with their start and end apart: 15, of which 10 were waited for; matrix products, arithmetic and copies ran while one was open for 0% of the time, Pallas kernels for 41%

profile of v2, /device:TPU:0, one launch (start us, length us, event | category | flops | bytes accessed | tf_op | source)
XLA Modules:
  0.0 73.3 jit_solution(12175305319287189953)
XLA Ops:
  0.0 0.0 copy-start.1
  0.0 2.0 %whiten_source.1 = bf16[8,8192]{1,0:T(8,128)(2,1)S(1)} custom-call(bf16[8,16,8192]{2,1,0:T(8,128)(2,1)} %own.1), custom_call_target="tpu_custom_call" | custom-call | flops 1000000 | bytes 2097152 | tf_op jit(solution)/shard_map/whiten_source/pallas_call | solution.py:64
  2.0 3.2 %collective-permute-start.3 = (bf16[8,8192]{1,0:T(8,128)(2,1)S(1)}, bf16[8,8192]{1,0:T(8,128)(2,1)S(1)}, u32[]{:S(2)}, u32[]{:S(2)}) collective-permute-start(bf16[8,8192]{1,0:T(8,128)(2,1)S(1)} %whiten_source.1), channel_id=1, source_target_pairs={{0,2},{1,3},{2,4},{3,5},{4,6},{5,7},{6,8},{7,9},{8,10},{9,11},{10,... | collective-permute-start | bytes 393224 | tf_op jit(solution)/shard_map/ppermute | solution.py:171
  5.2 0.6 collective-permute-start.2
  5.8 4.8 %collective-permute-start.1 = (bf16[8,8192]{1,0:T(8,128)(2,1)S(1)}, bf16[8,8192]{1,0:T(8,128)(2,1)S(1)}, u32[]{:S(2)}, u32[]{:S(2)}) collective-permute-start(bf16[8,8192]{1,0:T(8,128)(2,1)S(1)} %whiten_source.1), channel_id=1, source_target_pairs={{0,15},{1,0},{2,1},{3,2},{4,3},{5,4},{6,5},{7,6},{8,7},{9,8},{10,9... | collective-permute-start | bytes 393224 | tf_op jit(solution)/shard_map/ppermute | solution.py:171
  10.5 0.8 %collective-permute-start = (bf16[8,8192]{1,0:T(8,128)(2,1)S(1)}, bf16[8,8192]{1,0:T(8,128)(2,1)S(1)}, u32[]{:S(2)}, u32[]{:S(2)}) collective-permute-start(bf16[8,8192]{1,0:T(8,128)(2,1)S(1)} %whiten_source.1), channel_id=1, source_target_pairs={{0,14},{1,15},{2,0},{3,1},{4,2},{5,3},{6,4},{7,5},{8,6},{9,7},{10,... | collective-permute-start | bytes 393224 | tf_op jit(solution)/shard_map/ppermute | solution.py:171
  11.3 0.0 collective-permute-start.4
  12.0 0.0 copy-done.1
  12.0 0.9 %collective-permute-done.3 = bf16[8,8192]{1,0:T(8,128)(2,1)S(1)} collective-permute-done((bf16[8,8192]{1,0:T(8,128)(2,1)S(1)}, bf16[8,8192]{1,0:T(8,128)(2,1)S(1)}, u32[]{:S(2)}, u32[]{:S(2)}) %collective-permute-start.3) | collective-permute-done | bytes 131104 | tf_op jit(solution)/shard_map/ppermute | solution.py:171
  13.0 2.0 %collective-permute-done.2 = bf16[8,8192]{1,0:T(8,128)(2,1)S(1)} collective-permute-done((bf16[8,8192]{1,0:T(8,128)(2,1)S(1)}, bf16[8,8192]{1,0:T(8,128)(2,1)S(1)}, u32[]{:S(2)}, u32[]{:S(2)}) %collective-permute-start.2) | collective-permute-done | bytes 131104 | tf_op jit(solution)/shard_map/ppermute | solution.py:171
  15.0 0.6 collective-permute-done.1
  15.5 1.5 %collective-permute-done = bf16[8,8192]{1,0:T(8,128)(2,1)S(1)} collective-permute-done((bf16[8,8192]{1,0:T(8,128)(2,1)S(1)}, bf16[8,8192]{1,0:T(8,128)(2,1)S(1)}, u32[]{:S(2)}, u32[]{:S(2)}) %collective-permute-start) | collective-permute-done | bytes 131104 | tf_op jit(solution)/shard_map/ppermute | solution.py:171
  17.0 0.1 pad_maximum_fusion
  17.1 1.6 %collective-permute-start.6 = (bf16[4,8,8192]{2,1,0:T(8,128)(2,1)S(1)}, bf16[4,8,8192]{2,1,0:T(8,128)(2,1)S(1)}, u32[]{:S(2)}, u32[]{:S(2)}) collective-permute-start(bf16[4,8,8192]{2,1,0:T(8,128)(2,1)S(1)} %pad_maximum_fusion), channel_id=1, source_target_pairs={{0,32},{16,48},{32,64},{48,80},{64,96},{80,112},{96,0},{112,16},{1... | collective-permute-start | bytes 1572872 | tf_op jit(solution)/shard_map/ppermute | solution.py:176
  18.7 1.7 %collective-permute-start.7 = (bf16[4,8,8192]{2,1,0:T(8,128)(2,1)S(1)}, bf16[4,8,8192]{2,1,0:T(8,128)(2,1)S(1)}, u32[]{:S(2)}, u32[]{:S(2)}) collective-permute-start(bf16[4,8,8192]{2,1,0:T(8,128)(2,1)S(1)} %pad_maximum_fusion), channel_id=1, source_target_pairs={{0,96},{16,112},{32,0},{48,16},{64,32},{80,48},{96,64},{112,80},{1... | collective-permute-start | bytes 1572872 | tf_op jit(solution)/shard_map/ppermute | solution.py:176
  20.4 0.0 copy-start
  20.4 0.0 collective-permute-done.4.sibling
  20.4 6.6 %whiten_both.1 = (bf16[8,16,8192]{2,1,0:T(8,128)(2,1)S(1)}, bf16[8,16,8192]{2,1,0:T(8,128)(2,1)S(1)}) custom-call(bf16[8,16,8192]{2,1,0:T(8,128)(2,1)} %own.1, bf16[8,16,8192]{2,1,0:T(8,128)(2,1)S(1)} %collective-permute-done.4.sibling), custom_call_target="tpu_custom_call" | custom-call | flops 1000000000 | bytes 8388608 | tf_op jit(solution)/shard_map/whiten_both/pallas_call | solution.py:77
  27.0 0.0 copy-done
  27.0 3.9 %correlate_2.2 = bf16[2,32,256]{2,1,0:T(8,128)(2,1)S(1)} custom-call(s32[1]{0:T(128)} %bitcast.6.parity, bf16[8,16,8192]{2,1,0:T(8,128)(2,1)S(1)} %get-tuple-element.14.refs_0_, bf16[8,16,8192]{2,1,0:T(8,128)(2,1)S(1)} %get-tuple-element.15.refs_1_, bf16[2,8,8192]{2,1,0:T(8,128)(2,1)S(1)} %pad_maximum_fusion.1.refs_2_, bf16[8192,256]{1,0:T(8,128)(2,1)S(1)} %copy-done), custom_call_target="tpu_custom_call" | custom-call | flops 2000000000 | bytes 8388608 | tf_op jit(solution)/shard_map/correlate_2/pallas_call | solution.py:146
  31.0 2.1 %collective-permute-start.5 = (bf16[4,8,8192]{2,1,0:T(8,128)(2,1)S(1)}, bf16[4,8,8192]{2,1,0:T(8,128)(2,1)S(1)}, u32[]{:S(2)}, u32[]{:S(2)}) collective-permute-start(bf16[4,8,8192]{2,1,0:T(8,128)(2,1)S(1)} %pad_maximum_fusion), channel_id=1, source_target_pairs={{0,64},{16,80},{32,96},{48,112},{64,0},{80,16},{96,32},{112,48},{1... | collective-permute-start | bytes 1572872 | tf_op jit(solution)/shard_map/ppermute | solution.py:176
  33.0 0.0 collective-permute-done.6.refs_2_
  33.0 0.0 collective-permute-done.7.refs_3_
  33.0 10.1 %correlate_8.1 = bf16[8,32,256]{2,1,0:T(8,128)(2,1)S(1)} custom-call(s32[1]{0:T(128)} %bitcast.6.parity, bf16[8,16,8192]{2,1,0:T(8,128)(2,1)S(1)} %get-tuple-element.14.refs_0_, bf16[8,16,8192]{2,1,0:T(8,128)(2,1)S(1)} %get-tuple-element.15.refs_1_, bf16[4,8,8192]{2,1,0:T(8,128)(2,1)S(1)} %collective-permute-done.6.refs_2_, ...), custom_call_target="tpu_custom_call" | custom-call | flops 8000000000 | bytes 8388608 | tf_op jit(solution)/shard_map/correlate_8/pallas_call | solution.py:146
  43.2 0.9 %collective-permute-done.5.refs_2_ = bf16[4,8,8192]{2,1,0:T(8,128)(2,1)S(1)} collective-permute-done((bf16[4,8,8192]{2,1,0:T(8,128)(2,1)S(1)}, bf16[4,8,8192]{2,1,0:T(8,128)(2,1)S(1)}, u32[]{:S(2)}, u32[]{:S(2)}) %collective-permute-start.5) | collective-permute-done | bytes 524320 | tf_op jit(solution)/shard_map/ppermute | solution.py:176
  44.0 1.7 %collective-permute-start.10 = (bf16[4,32,256]{2,1,0:T(8,128)(2,1)S(1)}, bf16[4,32,256]{2,1,0:T(8,128)(2,1)S(1)}, u32[]{:S(2)}, u32[]{:S(2)}) collective-permute-start(bf16[4,32,256]{2,1,0:T(8,128)(2,1)S(1)} %get-tuple-element.22), channel_id=1, source_target_pairs={{0,96},{16,112},{32,0},{48,16},{64,32},{80,48},{96,64},{112,80},{1... | collective-permute-start | bytes 196616 | tf_op jit(solution)/shard_map/ppermute | solution.py:176
  45.7 5.4 %correlate_4.1 = bf16[4,32,256]{2,1,0:T(8,128)(2,1)S(1)} custom-call(s32[1]{0:T(128)} %bitcast.6.parity, bf16[8,16,8192]{2,1,0:T(8,128)(2,1)S(1)} %get-tuple-element.14.refs_0_, bf16[8,16,8192]{2,1,0:T(8,128)(2,1)S(1)} %get-tuple-element.15.refs_1_, bf16[4,8,8192]{2,1,0:T(8,128)(2,1)S(1)} %collective-permute-done.5.refs_2_, bf16[8192,256]{1,0:T(8,128)(2,1)S(1)} %copy-done), custom_call_target="tpu_custom_call" | custom-call | flops 4000000000 | bytes 8388608 | tf_op jit(solution)/shard_map/correlate_4/pallas_call | solution.py:146
  51.1 0.8 %collective-permute-start.9 = (bf16[4,32,256]{2,1,0:T(8,128)(2,1)S(1)}, bf16[4,32,256]{2,1,0:T(8,128)(2,1)S(1)}, u32[]{:S(2)}, u32[]{:S(2)}) collective-permute-start(bf16[4,32,256]{2,1,0:T(8,128)(2,1)S(1)} %correlate_4.1), channel_id=1, source_target_pairs={{0,64},{16,80},{32,96},{48,112},{64,0},{80,16},{96,32},{112,48},{1... | collective-permute-start | bytes 196616 | tf_op jit(solution)/shard_map/ppermute | solution.py:176
  51.9 0.9 %collective-permute-start.8 = (bf16[4,32,256]{2,1,0:T(8,128)(2,1)S(1)}, bf16[4,32,256]{2,1,0:T(8,128)(2,1)S(1)}, u32[]{:S(2)}, u32[]{:S(2)}) collective-permute-start(bf16[4,32,256]{2,1,0:T(8,128)(2,1)S(1)} %get-tuple-element.20), channel_id=1, source_target_pairs={{0,32},{16,48},{32,64},{48,80},{64,96},{80,112},{96,0},{112,16},{1... | collective-permute-start | bytes 196616 | tf_op jit(solution)/shard_map/ppermute | solution.py:176
  52.8 3.9 %correlate_2.3 = bf16[2,32,256]{2,1,0:T(8,128)(2,1)S(1)} custom-call(s32[1]{0:T(128)} %bitcast.6.parity, bf16[8,16,8192]{2,1,0:T(8,128)(2,1)S(1)} %get-tuple-element.14.refs_0_, bf16[8,16,8192]{2,1,0:T(8,128)(2,1)S(1)} %get-tuple-element.15.refs_1_, bf16[2,8,8192]{2,1,0:T(8,128)(2,1)S(1)} %slice.27.refs_2_, bf16[8192,256]{1,0:T(8,128)(2,1)S(1)} %copy-done), custom_call_target="tpu_custom_call" | custom-call | flops 2000000000 | bytes 8388608 | tf_op jit(solution)/shard_map/correlate_2/pallas_call | solution.py:146
  56.8 0.0 collective-permute-done.10
  56.8 0.2 collective-permute-done.9
  57.0 0.7 collective-permute-done.8
  57.7 0.6 gather_fusion
  58.3 2.9 %collective-permute-start.14 = (bf16[128,256]{1,0:T(8,128)(2,1)S(1)}, bf16[128,256]{1,0:T(8,128)(2,1)S(1)}, u32[]{:S(2)}, u32[]{:S(2)}) collective-permute-start(bf16[128,256]{1,0:T(8,128)(2,1)S(1)} %bitcast.40), channel_id=1, source_target_pairs={{0,2},{1,3},{2,4},{3,5},{4,6},{5,7},{6,8},{7,9},{8,10},{9,11},{10,... | collective-permute-start | bytes 196616 | tf_op jit(solution)/shard_map/ppermute | solution.py:171
  61.2 0.6 collective-permute-start.13
  61.8 4.8 %collective-permute-start.12 = (bf16[128,256]{1,0:T(8,128)(2,1)S(1)}, bf16[128,256]{1,0:T(8,128)(2,1)S(1)}, u32[]{:S(2)}, u32[]{:S(2)}) collective-permute-start(bf16[128,256]{1,0:T(8,128)(2,1)S(1)} %bitcast.36), channel_id=1, source_target_pairs={{0,15},{1,0},{2,1},{3,2},{4,3},{5,4},{6,5},{7,6},{8,7},{9,8},{10,9... | collective-permute-start | bytes 196616 | tf_op jit(solution)/shard_map/ppermute | solution.py:171
  66.5 0.2 collective-permute-start.11
  66.7 0.0 collective-permute-done.14
  66.7 2.1 %collective-permute-done.13 = bf16[128,256]{1,0:T(8,128)(2,1)S(1)} collective-permute-done((bf16[128,256]{1,0:T(8,128)(2,1)S(1)}, bf16[128,256]{1,0:T(8,128)(2,1)S(1)}, u32[]{:S(2)}, u32[]{:S(2)}) %collective-permute-start.13) | collective-permute-done | bytes 65568 | tf_op jit(solution)/shard_map/ppermute | solution.py:171
  68.8 0.3 collective-permute-done.12
  69.1 3.2 %collective-permute-done.11 = bf16[128,256]{1,0:T(8,128)(2,1)S(1)} collective-permute-done((bf16[128,256]{1,0:T(8,128)(2,1)S(1)}, bf16[128,256]{1,0:T(8,128)(2,1)S(1)}, u32[]{:S(2)}, u32[]{:S(2)}) %collective-permute-start.11) | collective-permute-done | bytes 65568 | tf_op jit(solution)/shard_map/ppermute | solution.py:171
  72.3 0.9 %select_select_fusion = f32[1,1,4,128,256]{4,3,2,1,0:T(8,128)} fusion(f32[128,256]{1,0:T(8,128)S(1)} %convert_element_type.19, f32[128,256]{1,0:T(8,128)S(1)} %convert_element_type.18, f32[128,256]{1,0:T(8,128)S(1)} %convert_element_type.17, f32[128,256]{1,0:T(8,128)S(1)} %convert_element_type.16, pred[4]{0:T(512)(128)(4,1)S(1)} %get-tuple-element.33, ...), kind=kLoop, calls=%fused_computation.2 | loop fusion | flops 524288 | bytes 1048592 | tf_op jit(solution)/shard_map/jit(_where)/select_n | solution.py:223
  (14 shorter events, 0.2 us)
Async XLA Ops:
  0.0 12.0 %copy-start.1 = (s32[1,4]{1,0:T(1,128)S(1)}, s32[1,4]{1,0:T(1,128)}, u32[]{:S(2)}) copy-start(s32[1,4]{1,0:T(1,128)} %param.5) | copy-start | bytes 52
  2.0 11.0 %collective-permute-start.3 = (bf16[8,8192]{1,0:T(8,128)(2,1)S(1)}, bf16[8,8192]{1,0:T(8,128)(2,1)S(1)}, u32[]{:S(2)}, u32[]{:S(2)}) collective-permute-start(bf16[8,8192]{1,0:T(8,128)(2,1)S(1)} %whiten_source.1), channel_id=1, source_target_pairs={{0,2},{1,3},{2,4},{3,5},{4,6},{5,7},{6,8},{7,9},{8,10},{9,11},{10,... | collective-permute-start | bytes 393224 | tf_op jit(solution)/shard_map/ppermute | solution.py:171
  5.2 9.8 %collective-permute-start.2 = (bf16[8,8192]{1,0:T(8,128)(2,1)S(1)}, bf16[8,8192]{1,0:T(8,128)(2,1)S(1)}, u32[]{:S(2)}, u32[]{:S(2)}) collective-permute-start(bf16[8,8192]{1,0:T(8,128)(2,1)S(1)} %whiten_source.1), channel_id=1, source_target_pairs={{0,1},{1,2},{2,3},{3,4},{4,5},{5,6},{6,7},{7,8},{8,9},{9,10},{10,1... | collective-permute-start | bytes 393224 | tf_op jit(solution)/shard_map/ppermute | solution.py:171
  5.8 9.8 %collective-permute-start.1 = (bf16[8,8192]{1,0:T(8,128)(2,1)S(1)}, bf16[8,8192]{1,0:T(8,128)(2,1)S(1)}, u32[]{:S(2)}, u32[]{:S(2)}) collective-permute-start(bf16[8,8192]{1,0:T(8,128)(2,1)S(1)} %whiten_source.1), channel_id=1, source_target_pairs={{0,15},{1,0},{2,1},{3,2},{4,3},{5,4},{6,5},{7,6},{8,7},{9,8},{10,9... | collective-permute-start | bytes 393224 | tf_op jit(solution)/shard_map/ppermute | solution.py:171
  10.5 6.5 %collective-permute-start = (bf16[8,8192]{1,0:T(8,128)(2,1)S(1)}, bf16[8,8192]{1,0:T(8,128)(2,1)S(1)}, u32[]{:S(2)}, u32[]{:S(2)}) collective-permute-start(bf16[8,8192]{1,0:T(8,128)(2,1)S(1)} %whiten_source.1), channel_id=1, source_target_pairs={{0,14},{1,15},{2,0},{3,1},{4,2},{5,3},{6,4},{7,5},{8,6},{9,7},{10,... | collective-permute-start | bytes 393224 | tf_op jit(solution)/shard_map/ppermute | solution.py:171
  11.3 9.1 %collective-permute-start.4 = (bf16[8,16,8192]{2,1,0:T(8,128)(2,1)}, bf16[8,16,8192]{2,1,0:T(8,128)(2,1)S(1)}, u32[]{:S(2)}, u32[]{:S(2)}) collective-permute-start(bf16[8,16,8192]{2,1,0:T(8,128)(2,1)} %own.1), channel_id=1, source_target_pairs={{0,16},{16,0},{32,48},{48,32},{64,80},{80,64},{96,112},{112,96},{1... | collective-permute-start | bytes 6291464 | tf_op jit(solution)/shard_map/ppermute | solution.py:181
  17.1 16.0 %collective-permute-start.6 = (bf16[4,8,8192]{2,1,0:T(8,128)(2,1)S(1)}, bf16[4,8,8192]{2,1,0:T(8,128)(2,1)S(1)}, u32[]{:S(2)}, u32[]{:S(2)}) collective-permute-start(bf16[4,8,8192]{2,1,0:T(8,128)(2,1)S(1)} %pad_maximum_fusion), channel_id=1, source_target_pairs={{0,32},{16,48},{32,64},{48,80},{64,96},{80,112},{96,0},{112,16},{1... | collective-permute-start | bytes 1572872 | tf_op jit(solution)/shard_map/ppermute | solution.py:176
  18.7 14.3 %collective-permute-start.7 = (bf16[4,8,8192]{2,1,0:T(8,128)(2,1)S(1)}, bf16[4,8,8192]{2,1,0:T(8,128)(2,1)S(1)}, u32[]{:S(2)}, u32[]{:S(2)}) collective-permute-start(bf16[4,8,8192]{2,1,0:T(8,128)(2,1)S(1)} %pad_maximum_fusion), channel_id=1, source_target_pairs={{0,96},{16,112},{32,0},{48,16},{64,32},{80,48},{96,64},{112,80},{1... | collective-permute-start | bytes 1572872 | tf_op jit(solution)/shard_map/ppermute | solution.py:176
  20.4 6.6 %copy-start = (bf16[8192,256]{1,0:T(8,128)(2,1)S(1)}, bf16[8192,256]{1,0:T(8,128)(2,1)}, u32[]{:S(2)}) copy-start(bf16[8192,256]{1,0:T(8,128)(2,1)} %constant.58.clone.refs_3_.refs_4_) | copy-start | bytes 12582916
  31.0 13.1 %collective-permute-start.5 = (bf16[4,8,8192]{2,1,0:T(8,128)(2,1)S(1)}, bf16[4,8,8192]{2,1,0:T(8,128)(2,1)S(1)}, u32[]{:S(2)}, u32[]{:S(2)}) collective-permute-start(bf16[4,8,8192]{2,1,0:T(8,128)(2,1)S(1)} %pad_maximum_fusion), channel_id=1, source_target_pairs={{0,64},{16,80},{32,96},{48,112},{64,0},{80,16},{96,32},{112,48},{1... | collective-permute-start | bytes 1572872 | tf_op jit(solution)/shard_map/ppermute | solution.py:176
  44.0 12.7 %collective-permute-start.10 = (bf16[4,32,256]{2,1,0:T(8,128)(2,1)S(1)}, bf16[4,32,256]{2,1,0:T(8,128)(2,1)S(1)}, u32[]{:S(2)}, u32[]{:S(2)}) collective-permute-start(bf16[4,32,256]{2,1,0:T(8,128)(2,1)S(1)} %get-tuple-element.22), channel_id=1, source_target_pairs={{0,96},{16,112},{32,0},{48,16},{64,32},{80,48},{96,64},{112,80},{1... | collective-permute-start | bytes 196616 | tf_op jit(solution)/shard_map/ppermute | solution.py:176
  51.1 5.9 %collective-permute-start.9 = (bf16[4,32,256]{2,1,0:T(8,128)(2,1)S(1)}, bf16[4,32,256]{2,1,0:T(8,128)(2,1)S(1)}, u32[]{:S(2)}, u32[]{:S(2)}) collective-permute-start(bf16[4,32,256]{2,1,0:T(8,128)(2,1)S(1)} %correlate_4.1), channel_id=1, source_target_pairs={{0,64},{16,80},{32,96},{48,112},{64,0},{80,16},{96,32},{112,48},{1... | collective-permute-start | bytes 196616 | tf_op jit(solution)/shard_map/ppermute | solution.py:176
  51.9 5.8 %collective-permute-start.8 = (bf16[4,32,256]{2,1,0:T(8,128)(2,1)S(1)}, bf16[4,32,256]{2,1,0:T(8,128)(2,1)S(1)}, u32[]{:S(2)}, u32[]{:S(2)}) collective-permute-start(bf16[4,32,256]{2,1,0:T(8,128)(2,1)S(1)} %get-tuple-element.20), channel_id=1, source_target_pairs={{0,32},{16,48},{32,64},{48,80},{64,96},{80,112},{96,0},{112,16},{1... | collective-permute-start | bytes 196616 | tf_op jit(solution)/shard_map/ppermute | solution.py:176
  58.3 8.4 %collective-permute-start.14 = (bf16[128,256]{1,0:T(8,128)(2,1)S(1)}, bf16[128,256]{1,0:T(8,128)(2,1)S(1)}, u32[]{:S(2)}, u32[]{:S(2)}) collective-permute-start(bf16[128,256]{1,0:T(8,128)(2,1)S(1)} %bitcast.40), channel_id=1, source_target_pairs={{0,2},{1,3},{2,4},{3,5},{4,6},{5,7},{6,8},{7,9},{8,10},{9,11},{10,... | collective-permute-start | bytes 196616 | tf_op jit(solution)/shard_map/ppermute | solution.py:171
  61.2 7.6 %collective-permute-start.13 = (bf16[128,256]{1,0:T(8,128)(2,1)S(1)}, bf16[128,256]{1,0:T(8,128)(2,1)S(1)}, u32[]{:S(2)}, u32[]{:S(2)}) collective-permute-start(bf16[128,256]{1,0:T(8,128)(2,1)S(1)} %bitcast.38), channel_id=1, source_target_pairs={{0,1},{1,2},{2,3},{3,4},{4,5},{5,6},{6,7},{7,8},{8,9},{9,10},{10,1... | collective-permute-start | bytes 196616 | tf_op jit(solution)/shard_map/ppermute | solution.py:171
  61.8 7.3 %collective-permute-start.12 = (bf16[128,256]{1,0:T(8,128)(2,1)S(1)}, bf16[128,256]{1,0:T(8,128)(2,1)S(1)}, u32[]{:S(2)}, u32[]{:S(2)}) collective-permute-start(bf16[128,256]{1,0:T(8,128)(2,1)S(1)} %bitcast.36), channel_id=1, source_target_pairs={{0,15},{1,0},{2,1},{3,2},{4,3},{5,4},{6,5},{7,6},{8,7},{9,8},{10,9... | collective-permute-start | bytes 196616 | tf_op jit(solution)/shard_map/ppermute | solution.py:171
  66.5 5.8 %collective-permute-start.11 = (bf16[128,256]{1,0:T(8,128)(2,1)S(1)}, bf16[128,256]{1,0:T(8,128)(2,1)S(1)}, u32[]{:S(2)}, u32[]{:S(2)}) collective-permute-start(bf16[128,256]{1,0:T(8,128)(2,1)S(1)} %bitcast.35), channel_id=1, source_target_pairs={{0,14},{1,15},{2,0},{3,1},{4,2},{5,3},{6,4},{7,5},{8,6},{9,7},{10,... | collective-permute-start | bytes 196616 | tf_op jit(solution)/shard_map/ppermute | solution.py:171

commit v3 on v2

--- a/solution.py
+++ b/solution.py
@@ -13,8 +13,9 @@
 BAND = 64
 LAGS = 256
 REACH = 2
-VMEM = 24 * 1024 * 1024
-OFFSETS = (-2, -1, 1, 2)
+VMEM = 12 * 2**20
+WIDE = 48 * 2**20
+ROUTES = 4
 
 
 def lag_table(bins):
@@ -54,9 +55,21 @@
     out[...] = whiten_rows(jnp.concatenate(rows, axis=0))
 
 
-def whiten_kernel(own, sibling, own_out, sibling_out):
-    own_out[0] = whiten_rows(own[0].astype(jnp.float32))
-    sibling_out[0] = whiten_rows(sibling[0].astype(jnp.float32))
+def whiten_kernel(flag, own, sibling, own_out, sibling_out, flag_out, held, done):
+    windows = own.shape[0]
+    pairs = ((own, own_out), (sibling, sibling_out))
+    copies = [
+        pltpu.make_async_copy(pairs[k][0].at[w], held.at[k, w], done.at[k, w])
+        for w in range(windows)
+        for k in range(2)
+    ]
+    for copy in copies:
+        copy.start()
+    for i, copy in enumerate(copies):
+        w, k = i // 2, i % 2
+        copy.wait()
+        pairs[k][1][w] = whiten_rows(held[k, w].astype(jnp.float32))
+    flag_out[0] = flag[0]
 
 
 def whiten_source(spectra):
@@ -70,20 +83,23 @@
     )(spectra)
 
 
-def whiten_both(own, sibling):
-    windows, channels, width = own.shape
-    block = pl.BlockSpec((1, channels, width), lambda w: (w, 0, 0))
+def whiten_both(own, sibling, flag):
+    windows = own.shape[0]
     shape = jax.ShapeDtypeStruct(own.shape, jnp.bfloat16)
+    scalar, whole = pl.BlockSpec(memory_space=pltpu.SMEM), pl.BlockSpec(memory_space=pltpu.VMEM)
     return pl.pallas_call(
         whiten_kernel,
-        grid=(windows,),
-        in_specs=[block, block],
-        out_specs=[block, block],
-        out_shape=[shape, shape],
+        in_specs=[scalar] + [pl.BlockSpec(memory_space=pltpu.HBM)] * 2,
+        out_specs=[whole, whole, scalar],
+        out_shape=[shape, shape, jax.ShapeDtypeStruct(flag.shape, flag.dtype)],
+        scratch_shapes=[
+            pltpu.VMEM((2,) + own.shape, own.dtype),
+            pltpu.SemaphoreType.DMA((2, windows)),
+        ],
         compiler_params=pltpu.CompilerParams(vmem_limit_bytes=VMEM),
         cost_estimate=pl.CostEstimate(flops=10**9, bytes_accessed=8 * 2**20, transcendentals=0),
         name="whiten_both",
-    )(own, sibling)
+    )(flag, own, sibling)
 
 
 def correlate_kernel(groups, scale, parity, *refs):
@@ -146,7 +162,7 @@
     return pl.pallas_call(
         functools.partial(correlate_kernel, groups, scale),
         in_specs=[pl.BlockSpec(memory_space=pltpu.SMEM)] + [whole] * (2 + groups)
-        + [pl.BlockSpec(memory_space=pl.ANY)],
+        + [pl.BlockSpec(memory_space=pltpu.HBM)],
         out_specs=whole,
         out_shape=jax.ShapeDtypeStruct((n, 2 * half, LAGS), jnp.bfloat16),
         scratch_shapes=[
@@ -158,7 +174,7 @@
             pltpu.VMEM(table.shape, table.dtype),
             pltpu.SemaphoreType.DMA,
         ],
-        compiler_params=pltpu.CompilerParams(vmem_limit_bytes=VMEM),
+        compiler_params=pltpu.CompilerParams(vmem_limit_bytes=WIDE),
         cost_estimate=pl.CostEstimate(
             flops=n * 10**9, bytes_accessed=8 * 2**20, transcendentals=0
         ),
@@ -166,9 +182,25 @@
     )(parity, own, sibling, *sources, table)
 
 
-def chan_shift(block, distance):
-    size = lax.axis_size("chan")
-    return lax.ppermute(block, "chan", [(i, (i + distance) % size) for i in range(size)])
+def routes(blocks):
+    cycle = [min(b + 2, blocks - 1) if b % 2 == 0 else max(b - 2, 0) for b in range(blocks)]
+    inverse = [cycle.index(b) for b in range(blocks)]
+    up = [(b + 1) % blocks for b in range(blocks)]
+    down = [(b - 1) % blocks for b in range(blocks)]
+    return cycle, up, down, inverse
+
+
+def targets(block, blocks):
+    odd, last = block % 2 == 1, blocks - 1
+    cycle = jnp.where(odd, jnp.maximum(block - 2, 0), jnp.minimum(block + 2, last))
+    above = jnp.where(block == last, last - 1, block + 2)
+    below = jnp.where(block == 0, 1, block - 2)
+    return cycle, block + 1, block - 1, jnp.where(odd, above, below)
+
+
+def route_swap(block, index, back=False):
+    pairs = enumerate(routes(lax.axis_size("chan"))[index])
+    return lax.ppermute(block, "chan", [(j, i) if back else (i, j) for i, j in pairs])
 
 
 def chip_shift(block, distance):
@@ -190,21 +222,32 @@
 
     other = core_swap(spectra)
     source = whiten_source(spectra)
-    near = jnp.stack([chan_shift(source, d) for d in OFFSETS])
-    own, sibling = whiten_both(spectra, other)
-
-    args = (table, scale)
-    up, down = chip_shift(near, 1), chip_shift(near, -1)
-    part = len(OFFSETS) // 2
-    c_first = correlate(parity, own, sibling, [near[:part]], *args)
-    near, c_first = lax.optimization_barrier((near, c_first))
-    far = chip_shift(near, 2)
-    c_two = correlate(parity, own, sibling, [up, down], *args)
-    c_up, c_down = c_two[: len(OFFSETS)], c_two[len(OFFSETS) :]
-    far, c_up, c_down = lax.optimization_barrier((far, c_up, c_down))
-    c_far = correlate(parity, own, sibling, [far], *args)
-    last, c_far = lax.optimization_barrier((near[part:], c_far))
-    c_own = jnp.concatenate([c_first, correlate(parity, own, sibling, [last], *args)])
+    arrived = [route_swap(source, i) for i in range(ROUTES)]
+    own, sibling, pair_count = whiten_both(spectra, other, pair_count)
+    arrived, pair_count = lax.optimization_barrier((arrived, pair_count))
+    half = ROUTES // 2
+    first, second = jnp.stack(arrived[:half]), jnp.stack(arrived[half:])
+
+    up_first, down_first = chip_shift(first, 1), chip_shift(first, -1)
+    up_second, down_second = chip_shift(second, 1), chip_shift(second, -1)
+    run = functools.partial(correlate, parity, own, sibling, table=table, scale=scale)
+    own_first = run([first])
+    own_first, up_first, down_first = lax.optimization_barrier((own_first, up_first, down_first))
+    far_first = chip_shift(up_first, 1)
+    near_first = run([up_first, down_first])
+    near_first, up_second, down_second = lax.optimization_barrier(
+        (near_first, up_second, down_second)
+    )
+    far_second = chip_shift(down_second, -1)
+    near_second = run([up_second, down_second])
+    near_second, far_first, far_second = lax.optimization_barrier(
+        (near_second, far_first, far_second)
+    )
+    c_far = run([far_first, far_second])
+    c_far, second = lax.optimization_barrier((c_far, second))
+    c_own = jnp.concatenate([own_first, run([second])])
+    c_up = jnp.concatenate([near_first[:half], near_second[:half]])
+    c_down = jnp.concatenate([near_first[half:], near_second[half:]])
 
     chips = lax.axis_size("win") // 2
     chip = lax.axis_index("win") // 2
@@ -212,14 +255,14 @@
     stacked = jnp.stack(home)
     order = (chip - jnp.arange(chips)) % chips
     stacked = stacked[order]
-    blocks = jnp.swapaxes(stacked, 0, 1).reshape(len(OFFSETS), chips * 2 * channels, LAGS)
-    back = [chan_shift(blocks[i], -d) for i, d in enumerate(OFFSETS)]
-
-    distance = pair_remote[0] - lax.axis_index("chan")
+    blocks = jnp.swapaxes(stacked, 0, 1).reshape(ROUTES, chips * 2 * channels, LAGS)
+    back = [route_swap(blocks[i], i, back=True) for i in range(ROUTES)]
+
+    met = targets(lax.axis_index("chan"), lax.axis_size("chan"))
     live = jnp.arange(pair_remote.shape[1], dtype=jnp.int32) < pair_count[0]
     result = jnp.zeros((pair_remote.shape[1],) + back[0].shape, jnp.float32)
-    for block, d in zip(back, OFFSETS):
-        chosen = (live & (distance == d))[:, None, None]
+    for block, remote in zip(back, met):
+        chosen = (live & (pair_remote[0] == remote))[:, None, None]
         result = jnp.where(chosen, block[None].astype(jnp.float32), result)
     return result[None, None]
 

time: 73.5 us -> 72.6 us (0.988)
  waiting for transfers between devices: 12.3 us -> 8.7 us
  starting transfers between devices: 26.4 us -> 29.4 us
  Pallas kernels: 31.9 us -> 29.4 us
  local copies, waits for them, and re-layouts: 0.62 us -> 2.2 us
    ppermute x6 -> x9, starting transfers between devices: 8.71 us -> 14.5 us  [chip_shift(): lax.ppermute(block, 'win', [(i, (i + 2 * distance) % size) for i in range...]
    ppermute x8, waiting for transfers between devices: 10.5 us -> 6.9 us  [route_swap(): lax.ppermute(block, 'chan', [(j, i) if back else (i, j) for i, j in pairs])]
    ppermute x8, starting transfers between devices: 17.7 us -> 15 us  [route_swap(): lax.ppermute(block, 'chan', [(j, i) if back else (i, j) for i, j in pairs])]
    pallas_call x1, Pallas kernels: 1.99 us -> 0.38 us  [whiten_source(): pl.pallas_call(source_kernel, out_shape=jax.ShapeDtypeStruct((windows, wi...]
    unnamed x4 -> x6, local copies, waits for them, and re-layouts: 0.01 us -> 1.6 us
    pallas_call x4 -> x5, Pallas kernels: 23.4 us -> 22.7 us  [correlate(): pl.pallas_call(functools.partial(correlate_kernel, groups, scale), in_spe...]
    ppermute x6 -> x9, waiting for transfers between devices: 1.79 us -> 1.79 us  [chip_shift(): lax.ppermute(block, 'win', [(i, (i + 2 * distance) % size) for i in range...]
  transfers between devices with their start and end apart: 15 -> 18, of which waited for: 10 -> 6; matrix products, arithmetic and copies ran while one was open for 0% -> 1% of each run, Pallas kernels for 41% -> 41%
where the time goes in v3:
time: 72.6 us; the launch traced here: 72.4 us
  starting transfers between devices  29.4 us (40%)
  Pallas kernels  29.4 us (40%)
  waiting for transfers between devices  8.7 us (12%)
  local copies, waits for them, and re-layouts  2.2 us (3%)
  other arithmetic  1.76 us (2%)
  between operations  0.97 us (1%)
    pallas_call x5, Pallas kernels, correlate(): pl.pallas_call(functools.partial(correlate_kernel, groups, scale), in_spe...  22.7 us
    ppermute x8, starting transfers between devices, route_swap(): lax.ppermute(block, 'chan', [(j, i) if back else (i, j) for i, j in pairs])  15 us
    ppermute x9, starting transfers between devices, chip_shift(): lax.ppermute(block, 'win', [(i, (i + 2 * distance) % size) for i in range...  14.5 us
    ppermute x8, waiting for transfers between devices, route_swap(): lax.ppermute(block, 'chan', [(j, i) if back else (i, j) for i, j in pairs])  6.9 us
    pallas_call x1, Pallas kernels, whiten_both(): pl.pallas_call(whiten_kernel, in_specs=[scalar] + [pl.BlockSpec(memory_sp...  6.24 us
    ppermute x9, waiting for transfers between devices, chip_shift(): lax.ppermute(block, 'win', [(i, (i + 2 * distance) % size) for i in range...  1.79 us
    unnamed x6, local copies, waits for them, and re-layouts  1.6 us
  transfers between devices with their start and end apart: 18, of which 6 were waited for; matrix products, arithmetic and copies ran while one was open for 1% of the time, Pallas kernels for 41%

profile of v3, /device:TPU:0, one launch (start us, length us, event | category | flops | bytes accessed | tf_op | source)
XLA Modules:
  0.0 72.4 jit_solution(10149640984021791406)
XLA Ops:
  0.0 0.0 collective-permute-start.4
  0.0 0.0 copy-start
  0.0 1.6 %copy-done = bf16[8,16,8192]{2,1,0:T(8,128)(2,1)S(1)} copy-done((bf16[8,16,8192]{2,1,0:T(8,128)(2,1)S(1)}, bf16[8,16,8192]{2,1,0:T(8,128)(2,1)}, u32[]{:S(2)}) %copy-start) | copy-done | bytes 2097176
  1.6 0.0 copy-start.1
  1.6 0.4 whiten_source.1
  2.0 3.2 %collective-permute-start = (bf16[8,8192]{1,0:T(8,128)(2,1)S(1)}, bf16[8,8192]{1,0:T(8,128)(2,1)S(1)}, u32[]{:S(2)}, u32[]{:S(2)}) collective-permute-start(bf16[8,8192]{1,0:T(8,128)(2,1)S(1)} %whiten_source.1), channel_id=1, source_target_pairs={{0,2},{1,0},{2,4},{3,1},{4,6},{5,3},{6,8},{7,5},{8,10},{9,7},{10,1... | collective-permute-start | bytes 393224 | tf_op jit(solution)/shard_map/ppermute | solution.py:203
  5.2 0.0 collective-permute-start.1
  5.2 5.3 %collective-permute-start.2 = (bf16[8,8192]{1,0:T(8,128)(2,1)S(1)}, bf16[8,8192]{1,0:T(8,128)(2,1)S(1)}, u32[]{:S(2)}, u32[]{:S(2)}) collective-permute-start(bf16[8,8192]{1,0:T(8,128)(2,1)S(1)} %whiten_source.1), channel_id=1, source_target_pairs={{0,15},{1,0},{2,1},{3,2},{4,3},{5,4},{6,5},{7,6},{8,7},{9,8},{10,9... | collective-permute-start | bytes 393224 | tf_op jit(solution)/shard_map/ppermute | solution.py:203
  10.5 0.0 collective-permute-start.3
  11.2 0.0 collective-permute-done.4.sibling
  11.2 0.0 copy-done.1
  11.2 6.2 %whiten_both.1 = (bf16[8,16,8192]{2,1,0:T(8,128)(2,1)S(1)}, bf16[8,16,8192]{2,1,0:T(8,128)(2,1)S(1)}, s32[1]{0:T(128)}) custom-call(s32[1]{0:T(128)S(6)} %copy.5.flag, bf16[8,16,8192]{2,1,0:T(8,128)(2,1)S(1)} %copy-done.1, bf16[8,16,8192]{2,1,0:T(8,128)(2,1)} %collective-permute-done.4.sibling), custom_call_target="tpu_custom_call" | custom-call | flops 1000000000 | bytes 8388608 | tf_op jit(solution)/shard_map/whiten_both/pallas_call | solution.py:90
  17.5 0.0 collective-permute-done
  17.5 0.0 collective-permute-done.1
  17.5 0.0 collective-permute-done.2
  17.5 0.0 collective-permute-done.3
  17.6 1.6 %collective-permute-start.5 = (bf16[2,8,8192]{2,1,0:T(8,128)(2,1)S(1)}, bf16[2,8,8192]{2,1,0:T(8,128)(2,1)S(1)}, u32[]{:S(2)}, u32[]{:S(2)}) collective-permute-start(bf16[2,8,8192]{2,1,0:T(8,128)(2,1)S(1)} %pad_maximum_fusion.refs_2_), channel_id=1, source_target_pairs={{0,32},{16,48},{32,64},{48,80},{64,96},{80,112},{96,0},{112,16},{1... | collective-permute-start | bytes 786440 | tf_op jit(solution)/shard_map/ppermute | solution.py:208
  19.2 1.7 %collective-permute-start.6 = (bf16[2,8,8192]{2,1,0:T(8,128)(2,1)S(1)}, bf16[2,8,8192]{2,1,0:T(8,128)(2,1)S(1)}, u32[]{:S(2)}, u32[]{:S(2)}) collective-permute-start(bf16[2,8,8192]{2,1,0:T(8,128)(2,1)S(1)} %pad_maximum_fusion.refs_2_), channel_id=1, source_target_pairs={{0,96},{16,112},{32,0},{48,16},{64,32},{80,48},{96,64},{112,80},{1... | collective-permute-start | bytes 786440 | tf_op jit(solution)/shard_map/ppermute | solution.py:208
  20.9 0.4 collective-permute-start.7
  21.3 2.9 %collective-permute-start.8 = (bf16[2,8,8192]{2,1,0:T(8,128)(2,1)S(1)}, bf16[2,8,8192]{2,1,0:T(8,128)(2,1)S(1)}, u32[]{:S(2)}, u32[]{:S(2)}) collective-permute-start(bf16[2,8,8192]{2,1,0:T(8,128)(2,1)S(1)} %pad_maximum_fusion.1.refs_2_), channel_id=1, source_target_pairs={{0,96},{16,112},{32,0},{48,16},{64,32},{80,48},{96,64},{112,80},{1... | collective-permute-start | bytes 786440 | tf_op jit(solution)/shard_map/ppermute | solution.py:208
  24.2 3.6 %correlate_2.2 = bf16[2,32,256]{2,1,0:T(8,128)(2,1)S(1)} custom-call(s32[1]{0:T(128)} %bitcast.2.parity, bf16[8,16,8192]{2,1,0:T(8,128)(2,1)S(1)} %get-tuple-element.26.refs_0_, bf16[8,16,8192]{2,1,0:T(8,128)(2,1)S(1)} %get-tuple-element.27.refs_1_, bf16[2,8,8192]{2,1,0:T(8,128)(2,1)S(1)} %pad_maximum_fusion.refs_2_, ...), custom_call_target="tpu_custom_call" | custom-call | flops 2000000000 | bytes 8388608 | tf_op jit(solution)/shard_map/correlate_2/pallas_call | solution.py:162
  27.9 0.2 collective-permute-done.5.refs_2_
  28.1 0.4 collective-permute-done.6.refs_3_
  28.5 1.6 %collective-permute-start.9 = (bf16[2,8,8192]{2,1,0:T(8,128)(2,1)S(1)}, bf16[2,8,8192]{2,1,0:T(8,128)(2,1)S(1)}, u32[]{:S(2)}, u32[]{:S(2)}) collective-permute-start(bf16[2,8,8192]{2,1,0:T(8,128)(2,1)S(1)} %collective-permute-done.5.refs_2_), channel_id=1, source_target_pairs={{0,32},{16,48},{32,64},{48,80},{64,96},{80,112},{96,0},{112,16},{1... | collective-permute-start | bytes 786440 | tf_op jit(solution)/shard_map/ppermute | solution.py:208
  30.0 5.1 %correlate_4.3 = bf16[4,32,256]{2,1,0:T(8,128)(2,1)S(1)} custom-call(s32[1]{0:T(128)} %bitcast.2.parity, bf16[8,16,8192]{2,1,0:T(8,128)(2,1)S(1)} %get-tuple-element.26.refs_0_, bf16[8,16,8192]{2,1,0:T(8,128)(2,1)S(1)} %get-tuple-element.27.refs_1_, bf16[2,8,8192]{2,1,0:T(8,128)(2,1)S(1)} %collective-permute-done.5.refs_2_, ...), custom_call_target="tpu_custom_call" | custom-call | flops 4000000000 | bytes 8388608 | tf_op jit(solution)/shard_map/correlate_4/pallas_call | solution.py:162
  35.2 0.0 collective-permute-done.7.refs_2_
  35.2 0.0 collective-permute-done.8.refs_3_
  35.2 1.7 %collective-permute-start.10 = (bf16[2,8,8192]{2,1,0:T(8,128)(2,1)S(1)}, bf16[2,8,8192]{2,1,0:T(8,128)(2,1)S(1)}, u32[]{:S(2)}, u32[]{:S(2)}) collective-permute-start(bf16[2,8,8192]{2,1,0:T(8,128)(2,1)S(1)} %collective-permute-done.8.refs_3_), channel_id=1, source_target_pairs={{0,96},{16,112},{32,0},{48,16},{64,32},{80,48},{96,64},{112,80},{1... | collective-permute-start | bytes 786440 | tf_op jit(solution)/shard_map/ppermute | solution.py:208
  36.9 5.1 %correlate_4.4 = bf16[4,32,256]{2,1,0:T(8,128)(2,1)S(1)} custom-call(s32[1]{0:T(128)} %bitcast.2.parity, bf16[8,16,8192]{2,1,0:T(8,128)(2,1)S(1)} %get-tuple-element.26.refs_0_, bf16[8,16,8192]{2,1,0:T(8,128)(2,1)S(1)} %get-tuple-element.27.refs_1_, bf16[2,8,8192]{2,1,0:T(8,128)(2,1)S(1)} %collective-permute-done.7.refs_2_, ...), custom_call_target="tpu_custom_call" | custom-call | flops 4000000000 | bytes 8388608 | tf_op jit(solution)/shard_map/correlate_4/pallas_call | solution.py:162
  42.1 0.0 collective-permute-done.9.refs_2_
  42.1 0.0 collective-permute-done.10.refs_3_
  42.2 2.6 %collective-permute-start.13 = (bf16[4,32,256]{2,1,0:T(8,128)(2,1)S(1)}, bf16[4,32,256]{2,1,0:T(8,128)(2,1)S(1)}, u32[]{:S(2)}, u32[]{:S(2)}) collective-permute-start(bf16[4,32,256]{2,1,0:T(8,128)(2,1)S(1)} %pad_maximum_fusion.4), channel_id=1, source_target_pairs={{0,96},{16,112},{32,0},{48,16},{64,32},{80,48},{96,64},{112,80},{1... | collective-permute-start | bytes 196616 | tf_op jit(solution)/shard_map/ppermute | solution.py:208
  44.8 5.1 %correlate_4.5 = bf16[4,32,256]{2,1,0:T(8,128)(2,1)S(1)} custom-call(s32[1]{0:T(128)} %bitcast.2.parity, bf16[8,16,8192]{2,1,0:T(8,128)(2,1)S(1)} %get-tuple-element.26.refs_0_, bf16[8,16,8192]{2,1,0:T(8,128)(2,1)S(1)} %get-tuple-element.27.refs_1_, bf16[2,8,8192]{2,1,0:T(8,128)(2,1)S(1)} %collective-permute-done.9.refs_2_, ...), custom_call_target="tpu_custom_call" | custom-call | flops 4000000000 | bytes 8388608 | tf_op jit(solution)/shard_map/correlate_4/pallas_call | solution.py:162
  50.0 1.3 %collective-permute-start.12 = (bf16[4,32,256]{2,1,0:T(8,128)(2,1)S(1)}, bf16[4,32,256]{2,1,0:T(8,128)(2,1)S(1)}, u32[]{:S(2)}, u32[]{:S(2)}) collective-permute-start(bf16[4,32,256]{2,1,0:T(8,128)(2,1)S(1)} %correlate_4.5), channel_id=1, source_target_pairs={{0,64},{16,80},{32,96},{48,112},{64,0},{80,16},{96,32},{112,48},{1... | collective-permute-start | bytes 196616 | tf_op jit(solution)/shard_map/ppermute | solution.py:208
  51.2 0.0 copy-start.2
  51.2 0.7 collective-permute-start.11
  51.9 3.7 %correlate_2.3 = bf16[2,32,256]{2,1,0:T(8,128)(2,1)S(1)} custom-call(s32[1]{0:T(128)} %bitcast.2.parity, bf16[8,16,8192]{2,1,0:T(8,128)(2,1)S(1)} %get-tuple-element.26.refs_0_, bf16[8,16,8192]{2,1,0:T(8,128)(2,1)S(1)} %get-tuple-element.27.refs_1_, bf16[2,8,8192]{2,1,0:T(8,128)(2,1)S(1)} %pad_maximum_fusion.1.refs_2_, ...), custom_call_target="tpu_custom_call" | custom-call | flops 2000000000 | bytes 8388608 | tf_op jit(solution)/shard_map/correlate_2/pallas_call | solution.py:162
  55.6 0.0 collective-permute-done.13
  55.6 0.2 collective-permute-done.12
  55.8 1.0 %collective-permute-done.11 = bf16[4,32,256]{2,1,0:T(8,128)(2,1)S(1)} collective-permute-done((bf16[4,32,256]{2,1,0:T(8,128)(2,1)S(1)}, bf16[4,32,256]{2,1,0:T(8,128)(2,1)S(1)}, u32[]{:S(2)}, u32[]{:S(2)}) %collective-permute-start.11) | collective-permute-done | bytes 65568 | tf_op jit(solution)/shard_map/ppermute | solution.py:208
  56.8 0.6 gather_fusion
  57.4 0.2 collective-permute-start.17
  57.6 6.3 %collective-permute-start.16 = (bf16[128,256]{1,0:T(8,128)(2,1)S(1)}, bf16[128,256]{1,0:T(8,128)(2,1)S(1)}, u32[]{:S(2)}, u32[]{:S(2)}) collective-permute-start(bf16[128,256]{1,0:T(8,128)(2,1)S(1)} %bitcast.34), channel_id=1, source_target_pairs={{1,0},{2,1},{3,2},{4,3},{5,4},{6,5},{7,6},{8,7},{9,8},{10,9},{11,1... | collective-permute-start | bytes 196616 | tf_op jit(solution)/shard_map/ppermute | solution.py:203
  63.8 0.0 collective-permute-start.15
  63.8 0.0 collective-permute-start.14
  63.9 0.0 copy-done.2
  63.9 0.6 bitcast_and_fusion.3
  64.5 0.0 collective-permute-done.17
  64.5 1.2 %collective-permute-done.16 = bf16[128,256]{1,0:T(8,128)(2,1)S(1)} collective-permute-done((bf16[128,256]{1,0:T(8,128)(2,1)S(1)}, bf16[128,256]{1,0:T(8,128)(2,1)S(1)}, u32[]{:S(2)}, u32[]{:S(2)}) %collective-permute-start.16) | collective-permute-done | bytes 65568 | tf_op jit(solution)/shard_map/ppermute | solution.py:203
  65.8 5.7 %collective-permute-done.15 = bf16[128,256]{1,0:T(8,128)(2,1)S(1)} collective-permute-done((bf16[128,256]{1,0:T(8,128)(2,1)S(1)}, bf16[128,256]{1,0:T(8,128)(2,1)S(1)}, u32[]{:S(2)}, u32[]{:S(2)}) %collective-permute-start.15) | collective-permute-done | bytes 65568 | tf_op jit(solution)/shard_map/ppermute | solution.py:203
  71.4 0.0 collective-permute-done.14
  71.5 0.9 %select_select_fusion = f32[1,1,4,128,256]{4,3,2,1,0:T(8,128)} fusion(f32[128,256]{1,0:T(8,128)S(1)} %convert_element_type.19, f32[128,256]{1,0:T(8,128)S(1)} %convert_element_type.18, f32[128,256]{1,0:T(8,128)S(1)} %convert_element_type.17, f32[128,256]{1,0:T(8,128)S(1)} %convert_element_type.16, pred[4]{0:T(512)(128)(4,1)S(1)} %get-tuple-element.53, ...), kind=kLoop, calls=%fused_computation.1 | loop fusion | flops 524288 | bytes 1048592 | tf_op jit(solution)/shard_map/jit(_where)/select_n | solution.py:266
  (15 shorter events, 0.2 us)
Async XLA Ops:
  0.0 11.2 %collective-permute-start.4 = (bf16[8,16,8192]{2,1,0:T(8,128)(2,1)}, bf16[8,16,8192]{2,1,0:T(8,128)(2,1)}, u32[]{:S(2)}, u32[]{:S(2)}) collective-permute-start(bf16[8,16,8192]{2,1,0:T(8,128)(2,1)} %own.1), channel_id=1, source_target_pairs={{0,16},{16,0},{32,48},{48,32},{64,80},{80,64},{96,112},{112,96},{1... | collective-permute-start | bytes 6291464 | tf_op jit(solution)/shard_map/ppermute | solution.py:213
  0.0 1.6 %copy-start = (bf16[8,16,8192]{2,1,0:T(8,128)(2,1)S(1)}, bf16[8,16,8192]{2,1,0:T(8,128)(2,1)}, u32[]{:S(2)}) copy-start(bf16[8,16,8192]{2,1,0:T(8,128)(2,1)} %own.1) | copy-start | bytes 6291460
  1.6 9.6 %copy-start.1 = (bf16[8,16,8192]{2,1,0:T(8,128)(2,1)S(1)}, bf16[8,16,8192]{2,1,0:T(8,128)(2,1)}, u32[]{:S(2)}) copy-start(bf16[8,16,8192]{2,1,0:T(8,128)(2,1)} %own.1) | copy-start | bytes 6291460
  2.0 15.5 %collective-permute-start = (bf16[8,8192]{1,0:T(8,128)(2,1)S(1)}, bf16[8,8192]{1,0:T(8,128)(2,1)S(1)}, u32[]{:S(2)}, u32[]{:S(2)}) collective-permute-start(bf16[8,8192]{1,0:T(8,128)(2,1)S(1)} %whiten_source.1), channel_id=1, source_target_pairs={{0,2},{1,0},{2,4},{3,1},{4,6},{5,3},{6,8},{7,5},{8,10},{9,7},{10,1... | collective-permute-start | bytes 393224 | tf_op jit(solution)/shard_map/ppermute | solution.py:203
  5.2 12.3 %collective-permute-start.1 = (bf16[8,8192]{1,0:T(8,128)(2,1)S(1)}, bf16[8,8192]{1,0:T(8,128)(2,1)S(1)}, u32[]{:S(2)}, u32[]{:S(2)}) collective-permute-start(bf16[8,8192]{1,0:T(8,128)(2,1)S(1)} %whiten_source.1), channel_id=1, source_target_pairs={{0,1},{1,2},{2,3},{3,4},{4,5},{5,6},{6,7},{7,8},{8,9},{9,10},{10,1... | collective-permute-start | bytes 393224 | tf_op jit(solution)/shard_map/ppermute | solution.py:203
  5.2 12.4 %collective-permute-start.2 = (bf16[8,8192]{1,0:T(8,128)(2,1)S(1)}, bf16[8,8192]{1,0:T(8,128)(2,1)S(1)}, u32[]{:S(2)}, u32[]{:S(2)}) collective-permute-start(bf16[8,8192]{1,0:T(8,128)(2,1)S(1)} %whiten_source.1), channel_id=1, source_target_pairs={{0,15},{1,0},{2,1},{3,2},{4,3},{5,4},{6,5},{7,6},{8,7},{9,8},{10,9... | collective-permute-start | bytes 393224 | tf_op jit(solution)/shard_map/ppermute | solution.py:203
  10.5 7.0 %collective-permute-start.3 = (bf16[8,8192]{1,0:T(8,128)(2,1)S(1)}, bf16[8,8192]{1,0:T(8,128)(2,1)S(1)}, u32[]{:S(2)}, u32[]{:S(2)}) collective-permute-start(bf16[8,8192]{1,0:T(8,128)(2,1)S(1)} %whiten_source.1), channel_id=1, source_target_pairs={{0,1},{1,3},{2,0},{3,5},{4,2},{5,7},{6,4},{7,9},{8,6},{9,11},{10,8... | collective-permute-start | bytes 393224 | tf_op jit(solution)/shard_map/ppermute | solution.py:203
  17.6 10.5 %collective-permute-start.5 = (bf16[2,8,8192]{2,1,0:T(8,128)(2,1)S(1)}, bf16[2,8,8192]{2,1,0:T(8,128)(2,1)S(1)}, u32[]{:S(2)}, u32[]{:S(2)}) collective-permute-start(bf16[2,8,8192]{2,1,0:T(8,128)(2,1)S(1)} %pad_maximum_fusion.refs_2_), channel_id=1, source_target_pairs={{0,32},{16,48},{32,64},{48,80},{64,96},{80,112},{96,0},{112,16},{1... | collective-permute-start | bytes 786440 | tf_op jit(solution)/shard_map/ppermute | solution.py:208
  19.2 9.2 %collective-permute-start.6 = (bf16[2,8,8192]{2,1,0:T(8,128)(2,1)S(1)}, bf16[2,8,8192]{2,1,0:T(8,128)(2,1)S(1)}, u32[]{:S(2)}, u32[]{:S(2)}) collective-permute-start(bf16[2,8,8192]{2,1,0:T(8,128)(2,1)S(1)} %pad_maximum_fusion.refs_2_), channel_id=1, source_target_pairs={{0,96},{16,112},{32,0},{48,16},{64,32},{80,48},{96,64},{112,80},{1... | collective-permute-start | bytes 786440 | tf_op jit(solution)/shard_map/ppermute | solution.py:208
  20.9 14.3 %collective-permute-start.7 = (bf16[2,8,8192]{2,1,0:T(8,128)(2,1)S(1)}, bf16[2,8,8192]{2,1,0:T(8,128)(2,1)S(1)}, u32[]{:S(2)}, u32[]{:S(2)}) collective-permute-start(bf16[2,8,8192]{2,1,0:T(8,128)(2,1)S(1)} %pad_maximum_fusion.1.refs_2_), channel_id=1, source_target_pairs={{0,32},{16,48},{32,64},{48,80},{64,96},{80,112},{96,0},{112,16},{1... | collective-permute-start | bytes 786440 | tf_op jit(solution)/shard_map/ppermute | solution.py:208
  21.3 13.9 %collective-permute-start.8 = (bf16[2,8,8192]{2,1,0:T(8,128)(2,1)S(1)}, bf16[2,8,8192]{2,1,0:T(8,128)(2,1)S(1)}, u32[]{:S(2)}, u32[]{:S(2)}) collective-permute-start(bf16[2,8,8192]{2,1,0:T(8,128)(2,1)S(1)} %pad_maximum_fusion.1.refs_2_), channel_id=1, source_target_pairs={{0,96},{16,112},{32,0},{48,16},{64,32},{80,48},{96,64},{112,80},{1... | collective-permute-start | bytes 786440 | tf_op jit(solution)/shard_map/ppermute | solution.py:208
  28.5 13.7 %collective-permute-start.9 = (bf16[2,8,8192]{2,1,0:T(8,128)(2,1)S(1)}, bf16[2,8,8192]{2,1,0:T(8,128)(2,1)S(1)}, u32[]{:S(2)}, u32[]{:S(2)}) collective-permute-start(bf16[2,8,8192]{2,1,0:T(8,128)(2,1)S(1)} %collective-permute-done.5.refs_2_), channel_id=1, source_target_pairs={{0,32},{16,48},{32,64},{48,80},{64,96},{80,112},{96,0},{112,16},{1... | collective-permute-start | bytes 786440 | tf_op jit(solution)/shard_map/ppermute | solution.py:208
  35.2 6.9 %collective-permute-start.10 = (bf16[2,8,8192]{2,1,0:T(8,128)(2,1)S(1)}, bf16[2,8,8192]{2,1,0:T(8,128)(2,1)S(1)}, u32[]{:S(2)}, u32[]{:S(2)}) collective-permute-start(bf16[2,8,8192]{2,1,0:T(8,128)(2,1)S(1)} %collective-permute-done.8.refs_3_), channel_id=1, source_target_pairs={{0,96},{16,112},{32,0},{48,16},{64,32},{80,48},{96,64},{112,80},{1... | collective-permute-start | bytes 786440 | tf_op jit(solution)/shard_map/ppermute | solution.py:208
  42.2 13.4 %collective-permute-start.13 = (bf16[4,32,256]{2,1,0:T(8,128)(2,1)S(1)}, bf16[4,32,256]{2,1,0:T(8,128)(2,1)S(1)}, u32[]{:S(2)}, u32[]{:S(2)}) collective-permute-start(bf16[4,32,256]{2,1,0:T(8,128)(2,1)S(1)} %pad_maximum_fusion.4), channel_id=1, source_target_pairs={{0,96},{16,112},{32,0},{48,16},{64,32},{80,48},{96,64},{112,80},{1... | collective-permute-start | bytes 196616 | tf_op jit(solution)/shard_map/ppermute | solution.py:208
  50.0 5.8 %collective-permute-start.12 = (bf16[4,32,256]{2,1,0:T(8,128)(2,1)S(1)}, bf16[4,32,256]{2,1,0:T(8,128)(2,1)S(1)}, u32[]{:S(2)}, u32[]{:S(2)}) collective-permute-start(bf16[4,32,256]{2,1,0:T(8,128)(2,1)S(1)} %correlate_4.5), channel_id=1, source_target_pairs={{0,64},{16,80},{32,96},{48,112},{64,0},{80,16},{96,32},{112,48},{1... | collective-permute-start | bytes 196616 | tf_op jit(solution)/shard_map/ppermute | solution.py:208
  51.2 12.6 %copy-start.2 = (s32[1,4]{1,0:T(1,128)S(1)}, s32[1,4]{1,0:T(1,128)}, u32[]{:S(2)}) copy-start(s32[1,4]{1,0:T(1,128)} %param.5) | copy-start | bytes 52
  51.2 5.5 %collective-permute-start.11 = (bf16[4,32,256]{2,1,0:T(8,128)(2,1)S(1)}, bf16[4,32,256]{2,1,0:T(8,128)(2,1)S(1)}, u32[]{:S(2)}, u32[]{:S(2)}) collective-permute-start(bf16[4,32,256]{2,1,0:T(8,128)(2,1)S(1)} %pad_maximum_fusion.3), channel_id=1, source_target_pairs={{0,32},{16,48},{32,64},{48,80},{64,96},{80,112},{96,0},{112,16},{1... | collective-permute-start | bytes 196616 | tf_op jit(solution)/shard_map/ppermute | solution.py:208
  57.4 7.1 %collective-permute-start.17 = (bf16[128,256]{1,0:T(8,128)(2,1)S(1)}, bf16[128,256]{1,0:T(8,128)(2,1)S(1)}, u32[]{:S(2)}, u32[]{:S(2)}) collective-permute-start(bf16[128,256]{1,0:T(8,128)(2,1)S(1)} %bitcast.36), channel_id=1, source_target_pairs={{2,0},{0,1},{4,2},{1,3},{6,4},{3,5},{8,6},{5,7},{10,8},{7,9},{12,1... | collective-permute-start | bytes 196616 | tf_op jit(solution)/shard_map/ppermute | solution.py:203
  57.6 8.2 %collective-permute-start.16 = (bf16[128,256]{1,0:T(8,128)(2,1)S(1)}, bf16[128,256]{1,0:T(8,128)(2,1)S(1)}, u32[]{:S(2)}, u32[]{:S(2)}) collective-permute-start(bf16[128,256]{1,0:T(8,128)(2,1)S(1)} %bitcast.34), channel_id=1, source_target_pairs={{1,0},{2,1},{3,2},{4,3},{5,4},{6,5},{7,6},{8,7},{9,8},{10,9},{11,1... | collective-permute-start | bytes 196616 | tf_op jit(solution)/shard_map/ppermute | solution.py:203
  63.8 7.6 %collective-permute-start.15 = (bf16[128,256]{1,0:T(8,128)(2,1)S(1)}, bf16[128,256]{1,0:T(8,128)(2,1)S(1)}, u32[]{:S(2)}, u32[]{:S(2)}) collective-permute-start(bf16[128,256]{1,0:T(8,128)(2,1)S(1)} %bitcast.32), channel_id=1, source_target_pairs={{15,0},{0,1},{1,2},{2,3},{3,4},{4,5},{5,6},{6,7},{7,8},{8,9},{9,10... | collective-permute-start | bytes 196616 | tf_op jit(solution)/shard_map/ppermute | solution.py:203
  63.8 7.6 %collective-permute-start.14 = (bf16[128,256]{1,0:T(8,128)(2,1)S(1)}, bf16[128,256]{1,0:T(8,128)(2,1)S(1)}, u32[]{:S(2)}, u32[]{:S(2)}) collective-permute-start(bf16[128,256]{1,0:T(8,128)(2,1)S(1)} %bitcast.31), channel_id=1, source_target_pairs={{1,0},{3,1},{0,2},{5,3},{2,4},{7,5},{4,6},{9,7},{6,8},{11,9},{8,10... | collective-permute-start | bytes 196616 | tf_op jit(solution)/shard_map/ppermute | solution.py:203

commit v4 on v3

--- a/solution.py
+++ b/solution.py
@@ -15,7 +15,8 @@
 REACH = 2
 VMEM = 12 * 2**20
 WIDE = 48 * 2**20
-ROUTES = 4
+MOVES = (2, 1, -1, -2)
+ROUTES = len(MOVES)
 
 
 def lag_table(bins):
@@ -182,25 +183,15 @@
     )(parity, own, sibling, *sources, table)
 
 
-def routes(blocks):
-    cycle = [min(b + 2, blocks - 1) if b % 2 == 0 else max(b - 2, 0) for b in range(blocks)]
-    inverse = [cycle.index(b) for b in range(blocks)]
-    up = [(b + 1) % blocks for b in range(blocks)]
-    down = [(b - 1) % blocks for b in range(blocks)]
-    return cycle, up, down, inverse
-
-
-def targets(block, blocks):
-    odd, last = block % 2 == 1, blocks - 1
-    cycle = jnp.where(odd, jnp.maximum(block - 2, 0), jnp.minimum(block + 2, last))
-    above = jnp.where(block == last, last - 1, block + 2)
-    below = jnp.where(block == 0, 1, block - 2)
-    return cycle, block + 1, block - 1, jnp.where(odd, above, below)
-
-
-def route_swap(block, index, back=False):
-    pairs = enumerate(routes(lax.axis_size("chan"))[index])
-    return lax.ppermute(block, "chan", [(j, i) if back else (i, j) for i, j in pairs])
+def route_swap(block, move, back=False):
+    blocks, size = lax.axis_size("chan"), lax.axis_size("win")
+    pairs = []
+    for w in range(size):
+        for b in range(blocks):
+            to = b - move if w % 2 else b + move
+            inside = 0 <= to < blocks
+            pairs.append((w * blocks + b, w * blocks + to if inside else (w ^ 1) * blocks + b))
+    return lax.ppermute(block, ("win", "chan"), [(j, i) if back else (i, j) for i, j in pairs])
 
 
 def chip_shift(block, distance):
@@ -222,7 +213,7 @@
 
     other = core_swap(spectra)
     source = whiten_source(spectra)
-    arrived = [route_swap(source, i) for i in range(ROUTES)]
+    arrived = [route_swap(source, move) for move in MOVES]
     own, sibling, pair_count = whiten_both(spectra, other, pair_count)
     arrived, pair_count = lax.optimization_barrier((arrived, pair_count))
     half = ROUTES // 2
@@ -256,13 +247,13 @@
     order = (chip - jnp.arange(chips)) % chips
     stacked = stacked[order]
     blocks = jnp.swapaxes(stacked, 0, 1).reshape(ROUTES, chips * 2 * channels, LAGS)
-    back = [route_swap(blocks[i], i, back=True) for i in range(ROUTES)]
-
-    met = targets(lax.axis_index("chan"), lax.axis_size("chan"))
+    back = [route_swap(blocks[i], move, back=True) for i, move in enumerate(MOVES)]
+
+    here, sign = lax.axis_index("chan"), 1 - 2 * parity[0]
     live = jnp.arange(pair_remote.shape[1], dtype=jnp.int32) < pair_count[0]
     result = jnp.zeros((pair_remote.shape[1],) + back[0].shape, jnp.float32)
-    for block, remote in zip(back, met):
-        chosen = (live & (pair_remote[0] == remote))[:, None, None]
+    for block, move in zip(back, MOVES):
+        chosen = (live & (pair_remote[0] == here + move * sign))[:, None, None]
         result = jnp.where(chosen, block[None].astype(jnp.float32), result)
     return result[None, None]
 

time: 72.6 us -> 69 us (0.950)
  the two profiles are of different devices: /device:TPU:0 before, /device:TPU:34 now
where the time goes in v4:
time: 69 us; the launch traced here: 67.7 us
  Pallas kernels  29.4 us (43%)
  starting transfers between devices  28.9 us (42%)
  waiting for transfers between devices  4.48 us (6%)
  local copies, waits for them, and re-layouts  2.2 us (3%)
  other arithmetic  1.76 us (3%)
  between operations  0.98 us (1%)
    pallas_call x5, Pallas kernels, correlate(): pl.pallas_call(functools.partial(correlate_kernel, groups, scale), in_spe...  22.7 us
    ppermute x9, starting transfers between devices, chip_shift(): lax.ppermute(block, 'win', [(i, (i + 2 * distance) % size) for i in range...  14.6 us
    ppermute x8, starting transfers between devices, route_swap(): lax.ppermute(block, ('win', 'chan'), [(j, i) if back else (i, j) for i, j...  14.3 us
    pallas_call x1, Pallas kernels, whiten_both(): pl.pallas_call(whiten_kernel, in_specs=[scalar] + [pl.BlockSpec(memory_sp...  6.24 us
    ppermute x8, waiting for transfers between devices, route_swap(): lax.ppermute(block, ('win', 'chan'), [(j, i) if back else (i, j) for i, j...  2.51 us
    ppermute x9, waiting for transfers between devices, chip_shift(): lax.ppermute(block, 'win', [(i, (i + 2 * distance) % size) for i in range...  1.97 us
    unnamed x6, local copies, waits for them, and re-layouts  1.6 us
  transfers between devices with their start and end apart: 18, of which 4 were waited for; matrix products, arithmetic and copies ran while one was open for 1% of the time, Pallas kernels for 43%

profile of v4, /device:TPU:34, one launch (start us, length us, event | category | flops | bytes accessed | tf_op | source)
XLA Modules:
  0.0 67.7 jit_solution(15200550490564788485)
XLA Ops:
  0.0 0.0 collective-permute-start.4
  0.0 0.0 copy-start
  0.0 1.6 %copy-done = bf16[8,16,8192]{2,1,0:T(8,128)(2,1)S(1)} copy-done((bf16[8,16,8192]{2,1,0:T(8,128)(2,1)S(1)}, bf16[8,16,8192]{2,1,0:T(8,128)(2,1)}, u32[]{:S(2)}) %copy-start) | copy-done | bytes 2097176
  1.6 0.0 copy-start.1
  1.6 0.4 whiten_source.1
  2.0 2.2 %collective-permute-start = (bf16[8,8192]{1,0:T(8,128)(2,1)S(1)}, bf16[8,8192]{1,0:T(8,128)(2,1)S(1)}, u32[]{:S(2)}, u32[]{:S(2)}) collective-permute-start(bf16[8,8192]{1,0:T(8,128)(2,1)S(1)} %whiten_source.1), channel_id=1, source_target_pairs={{0,2},{1,3},{2,4},{3,5},{4,6},{5,7},{6,8},{7,9},{8,10},{9,11},{10,... | collective-permute-start | bytes 393224 | tf_op jit(solution)/shard_map/ppermute | solution.py:194
  4.2 1.2 %collective-permute-start.1 = (bf16[8,8192]{1,0:T(8,128)(2,1)S(1)}, bf16[8,8192]{1,0:T(8,128)(2,1)S(1)}, u32[]{:S(2)}, u32[]{:S(2)}) collective-permute-start(bf16[8,8192]{1,0:T(8,128)(2,1)S(1)} %whiten_source.1), channel_id=1, source_target_pairs={{0,1},{1,2},{2,3},{3,4},{4,5},{5,6},{6,7},{7,8},{8,9},{9,10},{10,1... | collective-permute-start | bytes 393224 | tf_op jit(solution)/shard_map/ppermute | solution.py:194
  5.4 0.8 %collective-permute-start.2 = (bf16[8,8192]{1,0:T(8,128)(2,1)S(1)}, bf16[8,8192]{1,0:T(8,128)(2,1)S(1)}, u32[]{:S(2)}, u32[]{:S(2)}) collective-permute-start(bf16[8,8192]{1,0:T(8,128)(2,1)S(1)} %whiten_source.1), channel_id=1, source_target_pairs={{0,16},{1,0},{2,1},{3,2},{4,3},{5,4},{6,5},{7,6},{8,7},{9,8},{10,9... | collective-permute-start | bytes 393224 | tf_op jit(solution)/shard_map/ppermute | solution.py:194
  6.2 2.4 %collective-permute-start.3 = (bf16[8,8192]{1,0:T(8,128)(2,1)S(1)}, bf16[8,8192]{1,0:T(8,128)(2,1)S(1)}, u32[]{:S(2)}, u32[]{:S(2)}) collective-permute-start(bf16[8,8192]{1,0:T(8,128)(2,1)S(1)} %whiten_source.1), channel_id=1, source_target_pairs={{0,16},{1,17},{2,0},{3,1},{4,2},{5,3},{6,4},{7,5},{8,6},{9,7},{10,... | collective-permute-start | bytes 393224 | tf_op jit(solution)/shard_map/ppermute | solution.py:194
  9.3 0.0 collective-permute-done.4.sibling
  9.3 0.0 copy-done.1
  9.3 6.2 %whiten_both.1 = (bf16[8,16,8192]{2,1,0:T(8,128)(2,1)S(1)}, bf16[8,16,8192]{2,1,0:T(8,128)(2,1)S(1)}, s32[1]{0:T(128)}) custom-call(s32[1]{0:T(128)S(6)} %copy.5.flag, bf16[8,16,8192]{2,1,0:T(8,128)(2,1)S(1)} %copy-done.1, bf16[8,16,8192]{2,1,0:T(8,128)(2,1)} %collective-permute-done.4.sibling), custom_call_target="tpu_custom_call" | custom-call | flops 1000000000 | bytes 8388608 | tf_op jit(solution)/shard_map/whiten_both/pallas_call | solution.py:91
  15.6 0.0 collective-permute-done
  15.6 0.0 collective-permute-done.1
  15.6 0.0 collective-permute-done.2
  15.6 0.0 collective-permute-done.3
  15.6 1.6 %collective-permute-start.5 = (bf16[2,8,8192]{2,1,0:T(8,128)(2,1)S(1)}, bf16[2,8,8192]{2,1,0:T(8,128)(2,1)S(1)}, u32[]{:S(2)}, u32[]{:S(2)}) collective-permute-start(bf16[2,8,8192]{2,1,0:T(8,128)(2,1)S(1)} %pad_maximum_fusion.refs_2_), channel_id=1, source_target_pairs={{0,32},{16,48},{32,64},{48,80},{64,96},{80,112},{96,0},{112,16},{1... | collective-permute-start | bytes 786440 | tf_op jit(solution)/shard_map/ppermute | solution.py:199
  17.3 1.7 %collective-permute-start.6 = (bf16[2,8,8192]{2,1,0:T(8,128)(2,1)S(1)}, bf16[2,8,8192]{2,1,0:T(8,128)(2,1)S(1)}, u32[]{:S(2)}, u32[]{:S(2)}) collective-permute-start(bf16[2,8,8192]{2,1,0:T(8,128)(2,1)S(1)} %pad_maximum_fusion.refs_2_), channel_id=1, source_target_pairs={{0,96},{16,112},{32,0},{48,16},{64,32},{80,48},{96,64},{112,80},{1... | collective-permute-start | bytes 786440 | tf_op jit(solution)/shard_map/ppermute | solution.py:199
  19.0 0.4 collective-permute-start.7
  19.4 2.9 %collective-permute-start.8 = (bf16[2,8,8192]{2,1,0:T(8,128)(2,1)S(1)}, bf16[2,8,8192]{2,1,0:T(8,128)(2,1)S(1)}, u32[]{:S(2)}, u32[]{:S(2)}) collective-permute-start(bf16[2,8,8192]{2,1,0:T(8,128)(2,1)S(1)} %pad_maximum_fusion.1.refs_2_), channel_id=1, source_target_pairs={{0,96},{16,112},{32,0},{48,16},{64,32},{80,48},{96,64},{112,80},{1... | collective-permute-start | bytes 786440 | tf_op jit(solution)/shard_map/ppermute | solution.py:199
  22.3 3.6 %correlate_2.2 = bf16[2,32,256]{2,1,0:T(8,128)(2,1)S(1)} custom-call(s32[1]{0:T(128)} %bitcast.2.parity, bf16[8,16,8192]{2,1,0:T(8,128)(2,1)S(1)} %get-tuple-element.26.refs_0_, bf16[8,16,8192]{2,1,0:T(8,128)(2,1)S(1)} %get-tuple-element.27.refs_1_, bf16[2,8,8192]{2,1,0:T(8,128)(2,1)S(1)} %pad_maximum_fusion.refs_2_, ...), custom_call_target="tpu_custom_call" | custom-call | flops 2000000000 | bytes 8388608 | tf_op jit(solution)/shard_map/correlate_2/pallas_call | solution.py:163
  25.9 0.0 collective-permute-done.5.refs_2_
  26.0 0.4 collective-permute-done.6.refs_3_
  26.4 1.6 %collective-permute-start.9 = (bf16[2,8,8192]{2,1,0:T(8,128)(2,1)S(1)}, bf16[2,8,8192]{2,1,0:T(8,128)(2,1)S(1)}, u32[]{:S(2)}, u32[]{:S(2)}) collective-permute-start(bf16[2,8,8192]{2,1,0:T(8,128)(2,1)S(1)} %collective-permute-done.5.refs_2_), channel_id=1, source_target_pairs={{0,32},{16,48},{32,64},{48,80},{64,96},{80,112},{96,0},{112,16},{1... | collective-permute-start | bytes 786440 | tf_op jit(solution)/shard_map/ppermute | solution.py:199
  28.0 5.1 %correlate_4.3 = bf16[4,32,256]{2,1,0:T(8,128)(2,1)S(1)} custom-call(s32[1]{0:T(128)} %bitcast.2.parity, bf16[8,16,8192]{2,1,0:T(8,128)(2,1)S(1)} %get-tuple-element.26.refs_0_, bf16[8,16,8192]{2,1,0:T(8,128)(2,1)S(1)} %get-tuple-element.27.refs_1_, bf16[2,8,8192]{2,1,0:T(8,128)(2,1)S(1)} %collective-permute-done.5.refs_2_, ...), custom_call_target="tpu_custom_call" | custom-call | flops 4000000000 | bytes 8388608 | tf_op jit(solution)/shard_map/correlate_4/pallas_call | solution.py:163
  33.1 0.0 collective-permute-done.7.refs_2_
  33.2 0.0 collective-permute-done.8.refs_3_
  33.2 1.7 %collective-permute-start.10 = (bf16[2,8,8192]{2,1,0:T(8,128)(2,1)S(1)}, bf16[2,8,8192]{2,1,0:T(8,128)(2,1)S(1)}, u32[]{:S(2)}, u32[]{:S(2)}) collective-permute-start(bf16[2,8,8192]{2,1,0:T(8,128)(2,1)S(1)} %collective-permute-done.8.refs_3_), channel_id=1, source_target_pairs={{0,96},{16,112},{32,0},{48,16},{64,32},{80,48},{96,64},{112,80},{1... | collective-permute-start | bytes 786440 | tf_op jit(solution)/shard_map/ppermute | solution.py:199
  34.9 5.1 %correlate_4.4 = bf16[4,32,256]{2,1,0:T(8,128)(2,1)S(1)} custom-call(s32[1]{0:T(128)} %bitcast.2.parity, bf16[8,16,8192]{2,1,0:T(8,128)(2,1)S(1)} %get-tuple-element.26.refs_0_, bf16[8,16,8192]{2,1,0:T(8,128)(2,1)S(1)} %get-tuple-element.27.refs_1_, bf16[2,8,8192]{2,1,0:T(8,128)(2,1)S(1)} %collective-permute-done.7.refs_2_, ...), custom_call_target="tpu_custom_call" | custom-call | flops 4000000000 | bytes 8388608 | tf_op jit(solution)/shard_map/correlate_4/pallas_call | solution.py:163
  40.1 0.0 collective-permute-done.9.refs_2_
  40.1 0.0 collective-permute-done.10.refs_3_
  40.1 3.5 %collective-permute-start.13 = (bf16[4,32,256]{2,1,0:T(8,128)(2,1)S(1)}, bf16[4,32,256]{2,1,0:T(8,128)(2,1)S(1)}, u32[]{:S(2)}, u32[]{:S(2)}) collective-permute-start(bf16[4,32,256]{2,1,0:T(8,128)(2,1)S(1)} %pad_maximum_fusion.4), channel_id=1, source_target_pairs={{0,96},{16,112},{32,0},{48,16},{64,32},{80,48},{96,64},{112,80},{1... | collective-permute-start | bytes 196616 | tf_op jit(solution)/shard_map/ppermute | solution.py:199
  43.6 5.1 %correlate_4.5 = bf16[4,32,256]{2,1,0:T(8,128)(2,1)S(1)} custom-call(s32[1]{0:T(128)} %bitcast.2.parity, bf16[8,16,8192]{2,1,0:T(8,128)(2,1)S(1)} %get-tuple-element.26.refs_0_, bf16[8,16,8192]{2,1,0:T(8,128)(2,1)S(1)} %get-tuple-element.27.refs_1_, bf16[2,8,8192]{2,1,0:T(8,128)(2,1)S(1)} %collective-permute-done.9.refs_2_, ...), custom_call_target="tpu_custom_call" | custom-call | flops 4000000000 | bytes 8388608 | tf_op jit(solution)/shard_map/correlate_4/pallas_call | solution.py:163
  48.8 0.1 collective-permute-start.12
  48.9 0.0 copy-start.2
  48.9 1.1 %collective-permute-start.11 = (bf16[4,32,256]{2,1,0:T(8,128)(2,1)S(1)}, bf16[4,32,256]{2,1,0:T(8,128)(2,1)S(1)}, u32[]{:S(2)}, u32[]{:S(2)}) collective-permute-start(bf16[4,32,256]{2,1,0:T(8,128)(2,1)S(1)} %pad_maximum_fusion.3), channel_id=1, source_target_pairs={{0,32},{16,48},{32,64},{48,80},{64,96},{80,112},{96,0},{112,16},{1... | collective-permute-start | bytes 196616 | tf_op jit(solution)/shard_map/ppermute | solution.py:199
  50.0 3.7 %correlate_2.3 = bf16[2,32,256]{2,1,0:T(8,128)(2,1)S(1)} custom-call(s32[1]{0:T(128)} %bitcast.2.parity, bf16[8,16,8192]{2,1,0:T(8,128)(2,1)S(1)} %get-tuple-element.26.refs_0_, bf16[8,16,8192]{2,1,0:T(8,128)(2,1)S(1)} %get-tuple-element.27.refs_1_, bf16[2,8,8192]{2,1,0:T(8,128)(2,1)S(1)} %pad_maximum_fusion.1.refs_2_, ...), custom_call_target="tpu_custom_call" | custom-call | flops 2000000000 | bytes 8388608 | tf_op jit(solution)/shard_map/correlate_2/pallas_call | solution.py:163
  53.6 0.0 collective-permute-done.13
  53.6 1.1 %collective-permute-done.12 = bf16[4,32,256]{2,1,0:T(8,128)(2,1)S(1)} collective-permute-done((bf16[4,32,256]{2,1,0:T(8,128)(2,1)S(1)}, bf16[4,32,256]{2,1,0:T(8,128)(2,1)S(1)}, u32[]{:S(2)}, u32[]{:S(2)}) %collective-permute-start.12) | collective-permute-done | bytes 65568 | tf_op jit(solution)/shard_map/ppermute | solution.py:199
  54.7 0.4 collective-permute-done.11
  55.2 0.6 gather_fusion
  55.8 2.3 %collective-permute-start.17 = (bf16[128,256]{1,0:T(8,128)(2,1)S(1)}, bf16[128,256]{1,0:T(8,128)(2,1)S(1)}, u32[]{:S(2)}, u32[]{:S(2)}) collective-permute-start(bf16[128,256]{1,0:T(8,128)(2,1)S(1)} %bitcast.36), channel_id=1, source_target_pairs={{2,0},{3,1},{4,2},{5,3},{6,4},{7,5},{8,6},{9,7},{10,8},{11,9},{12,... | collective-permute-start | bytes 196616 | tf_op jit(solution)/shard_map/ppermute | solution.py:194
  58.0 1.0 %collective-permute-start.16 = (bf16[128,256]{1,0:T(8,128)(2,1)S(1)}, bf16[128,256]{1,0:T(8,128)(2,1)S(1)}, u32[]{:S(2)}, u32[]{:S(2)}) collective-permute-start(bf16[128,256]{1,0:T(8,128)(2,1)S(1)} %bitcast.34), channel_id=1, source_target_pairs={{1,0},{2,1},{3,2},{4,3},{5,4},{6,5},{7,6},{8,7},{9,8},{10,9},{11,1... | collective-permute-start | bytes 196616 | tf_op jit(solution)/shard_map/ppermute | solution.py:194
  59.1 1.0 %collective-permute-start.15 = (bf16[128,256]{1,0:T(8,128)(2,1)S(1)}, bf16[128,256]{1,0:T(8,128)(2,1)S(1)}, u32[]{:S(2)}, u32[]{:S(2)}) collective-permute-start(bf16[128,256]{1,0:T(8,128)(2,1)S(1)} %bitcast.32), channel_id=1, source_target_pairs={{16,0},{0,1},{1,2},{2,3},{3,4},{4,5},{5,6},{6,7},{7,8},{8,9},{9,10... | collective-permute-start | bytes 196616 | tf_op jit(solution)/shard_map/ppermute | solution.py:194
  60.1 3.4 %collective-permute-start.14 = (bf16[128,256]{1,0:T(8,128)(2,1)S(1)}, bf16[128,256]{1,0:T(8,128)(2,1)S(1)}, u32[]{:S(2)}, u32[]{:S(2)}) collective-permute-start(bf16[128,256]{1,0:T(8,128)(2,1)S(1)} %bitcast.31), channel_id=1, source_target_pairs={{16,0},{17,1},{0,2},{1,3},{2,4},{3,5},{4,6},{5,7},{6,8},{7,9},{8,1... | collective-permute-start | bytes 196616 | tf_op jit(solution)/shard_map/ppermute | solution.py:194
  63.5 0.0 copy-done.2
  63.5 0.6 bitcast_and_fusion.3
  64.2 0.0 collective-permute-done.17
  64.2 0.0 collective-permute-done.16
  64.2 0.0 collective-permute-done.15
  64.2 2.5 %collective-permute-done.14 = bf16[128,256]{1,0:T(8,128)(2,1)S(1)} collective-permute-done((bf16[128,256]{1,0:T(8,128)(2,1)S(1)}, bf16[128,256]{1,0:T(8,128)(2,1)S(1)}, u32[]{:S(2)}, u32[]{:S(2)}) %collective-permute-start.14) | collective-permute-done | bytes 65568 | tf_op jit(solution)/shard_map/ppermute | solution.py:194
  66.8 0.9 %select_select_fusion = f32[1,1,4,128,256]{4,3,2,1,0:T(8,128)} fusion(f32[128,256]{1,0:T(8,128)S(1)} %convert_element_type.19, f32[128,256]{1,0:T(8,128)S(1)} %convert_element_type.18, f32[128,256]{1,0:T(8,128)S(1)} %convert_element_type.17, f32[128,256]{1,0:T(8,128)S(1)} %convert_element_type.16, pred[4]{0:T(512)(128)(4,1)S(1)} %get-tuple-element.53, ...), kind=kLoop, calls=%fused_computation.1 | loop fusion | flops 524288 | bytes 1048592 | tf_op jit(solution)/shard_map/jit(_where)/select_n | solution.py:257
  (15 shorter events, 0.2 us)
Async XLA Ops:
  0.0 9.3 %collective-permute-start.4 = (bf16[8,16,8192]{2,1,0:T(8,128)(2,1)}, bf16[8,16,8192]{2,1,0:T(8,128)(2,1)}, u32[]{:S(2)}, u32[]{:S(2)}) collective-permute-start(bf16[8,16,8192]{2,1,0:T(8,128)(2,1)} %own.1), channel_id=1, source_target_pairs={{0,16},{16,0},{32,48},{48,32},{64,80},{80,64},{96,112},{112,96},{1... | collective-permute-start | bytes 6291464 | tf_op jit(solution)/shard_map/ppermute | solution.py:204
  0.0 1.6 %copy-start = (bf16[8,16,8192]{2,1,0:T(8,128)(2,1)S(1)}, bf16[8,16,8192]{2,1,0:T(8,128)(2,1)}, u32[]{:S(2)}) copy-start(bf16[8,16,8192]{2,1,0:T(8,128)(2,1)} %own.1) | copy-start | bytes 6291460
  1.6 7.7 %copy-start.1 = (bf16[8,16,8192]{2,1,0:T(8,128)(2,1)S(1)}, bf16[8,16,8192]{2,1,0:T(8,128)(2,1)}, u32[]{:S(2)}) copy-start(bf16[8,16,8192]{2,1,0:T(8,128)(2,1)} %own.1) | copy-start | bytes 6291460
  2.0 13.6 %collective-permute-start = (bf16[8,8192]{1,0:T(8,128)(2,1)S(1)}, bf16[8,8192]{1,0:T(8,128)(2,1)S(1)}, u32[]{:S(2)}, u32[]{:S(2)}) collective-permute-start(bf16[8,8192]{1,0:T(8,128)(2,1)S(1)} %whiten_source.1), channel_id=1, source_target_pairs={{0,2},{1,3},{2,4},{3,5},{4,6},{5,7},{6,8},{7,9},{8,10},{9,11},{10,... | collective-permute-start | bytes 393224 | tf_op jit(solution)/shard_map/ppermute | solution.py:194
  4.2 11.4 %collective-permute-start.1 = (bf16[8,8192]{1,0:T(8,128)(2,1)S(1)}, bf16[8,8192]{1,0:T(8,128)(2,1)S(1)}, u32[]{:S(2)}, u32[]{:S(2)}) collective-permute-start(bf16[8,8192]{1,0:T(8,128)(2,1)S(1)} %whiten_source.1), channel_id=1, source_target_pairs={{0,1},{1,2},{2,3},{3,4},{4,5},{5,6},{6,7},{7,8},{8,9},{9,10},{10,1... | collective-permute-start | bytes 393224 | tf_op jit(solution)/shard_map/ppermute | solution.py:194
  5.4 10.2 %collective-permute-start.2 = (bf16[8,8192]{1,0:T(8,128)(2,1)S(1)}, bf16[8,8192]{1,0:T(8,128)(2,1)S(1)}, u32[]{:S(2)}, u32[]{:S(2)}) collective-permute-start(bf16[8,8192]{1,0:T(8,128)(2,1)S(1)} %whiten_source.1), channel_id=1, source_target_pairs={{0,16},{1,0},{2,1},{3,2},{4,3},{5,4},{6,5},{7,6},{8,7},{9,8},{10,9... | collective-permute-start | bytes 393224 | tf_op jit(solution)/shard_map/ppermute | solution.py:194
  6.2 9.4 %collective-permute-start.3 = (bf16[8,8192]{1,0:T(8,128)(2,1)S(1)}, bf16[8,8192]{1,0:T(8,128)(2,1)S(1)}, u32[]{:S(2)}, u32[]{:S(2)}) collective-permute-start(bf16[8,8192]{1,0:T(8,128)(2,1)S(1)} %whiten_source.1), channel_id=1, source_target_pairs={{0,16},{1,17},{2,0},{3,1},{4,2},{5,3},{6,4},{7,5},{8,6},{9,7},{10,... | collective-permute-start | bytes 393224 | tf_op jit(solution)/shard_map/ppermute | solution.py:194
  15.6 10.4 %collective-permute-start.5 = (bf16[2,8,8192]{2,1,0:T(8,128)(2,1)S(1)}, bf16[2,8,8192]{2,1,0:T(8,128)(2,1)S(1)}, u32[]{:S(2)}, u32[]{:S(2)}) collective-permute-start(bf16[2,8,8192]{2,1,0:T(8,128)(2,1)S(1)} %pad_maximum_fusion.refs_2_), channel_id=1, source_target_pairs={{0,32},{16,48},{32,64},{48,80},{64,96},{80,112},{96,0},{112,16},{1... | collective-permute-start | bytes 786440 | tf_op jit(solution)/shard_map/ppermute | solution.py:199
  17.3 9.1 %collective-permute-start.6 = (bf16[2,8,8192]{2,1,0:T(8,128)(2,1)S(1)}, bf16[2,8,8192]{2,1,0:T(8,128)(2,1)S(1)}, u32[]{:S(2)}, u32[]{:S(2)}) collective-permute-start(bf16[2,8,8192]{2,1,0:T(8,128)(2,1)S(1)} %pad_maximum_fusion.refs_2_), channel_id=1, source_target_pairs={{0,96},{16,112},{32,0},{48,16},{64,32},{80,48},{96,64},{112,80},{1... | collective-permute-start | bytes 786440 | tf_op jit(solution)/shard_map/ppermute | solution.py:199
  19.0 14.2 %collective-permute-start.7 = (bf16[2,8,8192]{2,1,0:T(8,128)(2,1)S(1)}, bf16[2,8,8192]{2,1,0:T(8,128)(2,1)S(1)}, u32[]{:S(2)}, u32[]{:S(2)}) collective-permute-start(bf16[2,8,8192]{2,1,0:T(8,128)(2,1)S(1)} %pad_maximum_fusion.1.refs_2_), channel_id=1, source_target_pairs={{0,32},{16,48},{32,64},{48,80},{64,96},{80,112},{96,0},{112,16},{1... | collective-permute-start | bytes 786440 | tf_op jit(solution)/shard_map/ppermute | solution.py:199
  19.4 13.8 %collective-permute-start.8 = (bf16[2,8,8192]{2,1,0:T(8,128)(2,1)S(1)}, bf16[2,8,8192]{2,1,0:T(8,128)(2,1)S(1)}, u32[]{:S(2)}, u32[]{:S(2)}) collective-permute-start(bf16[2,8,8192]{2,1,0:T(8,128)(2,1)S(1)} %pad_maximum_fusion.1.refs_2_), channel_id=1, source_target_pairs={{0,96},{16,112},{32,0},{48,16},{64,32},{80,48},{96,64},{112,80},{1... | collective-permute-start | bytes 786440 | tf_op jit(solution)/shard_map/ppermute | solution.py:199
  26.4 13.7 %collective-permute-start.9 = (bf16[2,8,8192]{2,1,0:T(8,128)(2,1)S(1)}, bf16[2,8,8192]{2,1,0:T(8,128)(2,1)S(1)}, u32[]{:S(2)}, u32[]{:S(2)}) collective-permute-start(bf16[2,8,8192]{2,1,0:T(8,128)(2,1)S(1)} %collective-permute-done.5.refs_2_), channel_id=1, source_target_pairs={{0,32},{16,48},{32,64},{48,80},{64,96},{80,112},{96,0},{112,16},{1... | collective-permute-start | bytes 786440 | tf_op jit(solution)/shard_map/ppermute | solution.py:199
  33.2 6.9 %collective-permute-start.10 = (bf16[2,8,8192]{2,1,0:T(8,128)(2,1)S(1)}, bf16[2,8,8192]{2,1,0:T(8,128)(2,1)S(1)}, u32[]{:S(2)}, u32[]{:S(2)}) collective-permute-start(bf16[2,8,8192]{2,1,0:T(8,128)(2,1)S(1)} %collective-permute-done.8.refs_3_), channel_id=1, source_target_pairs={{0,96},{16,112},{32,0},{48,16},{64,32},{80,48},{96,64},{112,80},{1... | collective-permute-start | bytes 786440 | tf_op jit(solution)/shard_map/ppermute | solution.py:199
  40.1 13.5 %collective-permute-start.13 = (bf16[4,32,256]{2,1,0:T(8,128)(2,1)S(1)}, bf16[4,32,256]{2,1,0:T(8,128)(2,1)S(1)}, u32[]{:S(2)}, u32[]{:S(2)}) collective-permute-start(bf16[4,32,256]{2,1,0:T(8,128)(2,1)S(1)} %pad_maximum_fusion.4), channel_id=1, source_target_pairs={{0,96},{16,112},{32,0},{48,16},{64,32},{80,48},{96,64},{112,80},{1... | collective-permute-start | bytes 196616 | tf_op jit(solution)/shard_map/ppermute | solution.py:199
  48.8 6.0 %collective-permute-start.12 = (bf16[4,32,256]{2,1,0:T(8,128)(2,1)S(1)}, bf16[4,32,256]{2,1,0:T(8,128)(2,1)S(1)}, u32[]{:S(2)}, u32[]{:S(2)}) collective-permute-start(bf16[4,32,256]{2,1,0:T(8,128)(2,1)S(1)} %correlate_4.5), channel_id=1, source_target_pairs={{0,64},{16,80},{32,96},{48,112},{64,0},{80,16},{96,32},{112,48},{1... | collective-permute-start | bytes 196616 | tf_op jit(solution)/shard_map/ppermute | solution.py:199
  48.9 14.6 %copy-start.2 = (s32[1,4]{1,0:T(1,128)S(1)}, s32[1,4]{1,0:T(1,128)}, u32[]{:S(2)}) copy-start(s32[1,4]{1,0:T(1,128)} %param.5) | copy-start | bytes 52
  48.9 6.2 %collective-permute-start.11 = (bf16[4,32,256]{2,1,0:T(8,128)(2,1)S(1)}, bf16[4,32,256]{2,1,0:T(8,128)(2,1)S(1)}, u32[]{:S(2)}, u32[]{:S(2)}) collective-permute-start(bf16[4,32,256]{2,1,0:T(8,128)(2,1)S(1)} %pad_maximum_fusion.3), channel_id=1, source_target_pairs={{0,32},{16,48},{32,64},{48,80},{64,96},{80,112},{96,0},{112,16},{1... | collective-permute-start | bytes 196616 | tf_op jit(solution)/shard_map/ppermute | solution.py:199
  55.8 8.4 %collective-permute-start.17 = (bf16[128,256]{1,0:T(8,128)(2,1)S(1)}, bf16[128,256]{1,0:T(8,128)(2,1)S(1)}, u32[]{:S(2)}, u32[]{:S(2)}) collective-permute-start(bf16[128,256]{1,0:T(8,128)(2,1)S(1)} %bitcast.36), channel_id=1, source_target_pairs={{2,0},{3,1},{4,2},{5,3},{6,4},{7,5},{8,6},{9,7},{10,8},{11,9},{12,... | collective-permute-start | bytes 196616 | tf_op jit(solution)/shard_map/ppermute | solution.py:194
  58.0 6.2 %collective-permute-start.16 = (bf16[128,256]{1,0:T(8,128)(2,1)S(1)}, bf16[128,256]{1,0:T(8,128)(2,1)S(1)}, u32[]{:S(2)}, u32[]{:S(2)}) collective-permute-start(bf16[128,256]{1,0:T(8,128)(2,1)S(1)} %bitcast.34), channel_id=1, source_target_pairs={{1,0},{2,1},{3,2},{4,3},{5,4},{6,5},{7,6},{8,7},{9,8},{10,9},{11,1... | collective-permute-start | bytes 196616 | tf_op jit(solution)/shard_map/ppermute | solution.py:194
  59.1 5.2 %collective-permute-start.15 = (bf16[128,256]{1,0:T(8,128)(2,1)S(1)}, bf16[128,256]{1,0:T(8,128)(2,1)S(1)}, u32[]{:S(2)}, u32[]{:S(2)}) collective-permute-start(bf16[128,256]{1,0:T(8,128)(2,1)S(1)} %bitcast.32), channel_id=1, source_target_pairs={{16,0},{0,1},{1,2},{2,3},{3,4},{4,5},{5,6},{6,7},{7,8},{8,9},{9,10... | collective-permute-start | bytes 196616 | tf_op jit(solution)/shard_map/ppermute | solution.py:194
  60.1 6.7 %collective-permute-start.14 = (bf16[128,256]{1,0:T(8,128)(2,1)S(1)}, bf16[128,256]{1,0:T(8,128)(2,1)S(1)}, u32[]{:S(2)}, u32[]{:S(2)}) collective-permute-start(bf16[128,256]{1,0:T(8,128)(2,1)S(1)} %bitcast.31), channel_id=1, source_target_pairs={{16,0},{17,1},{0,2},{1,3},{2,4},{3,5},{4,6},{5,7},{6,8},{7,9},{8,1... | collective-permute-start | bytes 196616 | tf_op jit(solution)/shard_map/ppermute | solution.py:194

commit v5 on v4

--- a/solution.py
+++ b/solution.py
@@ -15,7 +15,7 @@
 REACH = 2
 VMEM = 12 * 2**20
 WIDE = 48 * 2**20
-MOVES = (2, 1, -1, -2)
+MOVES = (1, 2, -1, -2)
 ROUTES = len(MOVES)
 
 
@@ -37,39 +37,57 @@
     ones = band_matrix()
     rows, width = values.shape
     bins = width // 2
-    real, imag = values[:, :bins], values[:, bins:]
-    magnitude = jnp.sqrt(real * real + imag * imag)
     parts = bins // 128
-    stacked = jnp.concatenate([magnitude[:, i * 128 : (i + 1) * 128] for i in range(parts)], axis=0)
+    split = [
+        (values[:, i * 128 : (i + 1) * 128], values[:, bins + i * 128 : bins + (i + 1) * 128])
+        for i in range(parts)
+    ]
+    powers = [re * re + im * im for re, im in split]
+    stacked = jnp.concatenate([p * lax.rsqrt(jnp.maximum(p, 1e-30)) for p in powers], axis=0)
     high = stacked.astype(jnp.bfloat16)
     low = (stacked - high.astype(jnp.float32)).astype(jnp.bfloat16)
-    total = jnp.dot(high, ones, preferred_element_type=jnp.float32) + jnp.dot(
-        low, ones, preferred_element_type=jnp.float32
+    total = jnp.dot(
+        jnp.concatenate([high, low], axis=1),
+        jnp.concatenate([ones, ones], axis=0),
+        preferred_element_type=jnp.float32,
     )
     inverse = 1.0 / (total * (1.0 / BAND) + 1e-06)
-    inverse = jnp.concatenate([inverse[i * rows : (i + 1) * rows] for i in range(parts)], axis=1)
-    return jnp.concatenate([real * inverse, imag * inverse], axis=1).astype(jnp.bfloat16)
-
-
-def source_kernel(spectra, out):
-    rows = [spectra[w].astype(jnp.float32)[0:1] for w in range(spectra.shape[0])]
+    scaled = [inverse[i * rows : (i + 1) * rows] for i in range(parts)]
+    real = [re * k for (re, _), k in zip(split, scaled)]
+    imag = [im * k for (_, im), k in zip(split, scaled)]
+    return jnp.concatenate(real + imag, axis=1).astype(jnp.bfloat16)
+
+
+def source_kernel(spectra, out, held, done):
+    windows = spectra.shape[0]
+    copies = [pltpu.make_async_copy(spectra.at[w], held.at[w], done.at[w]) for w in range(windows)]
+    for copy in copies:
+        copy.start()
+    rows = []
+    for w, copy in enumerate(copies):
+        copy.wait()
+        rows.append(held[w].astype(jnp.float32)[0:1])
     out[...] = whiten_rows(jnp.concatenate(rows, axis=0))
 
 
 def whiten_kernel(flag, own, sibling, own_out, sibling_out, flag_out, held, done):
     windows = own.shape[0]
     pairs = ((own, own_out), (sibling, sibling_out))
-    copies = [
-        pltpu.make_async_copy(pairs[k][0].at[w], held.at[k, w], done.at[k, w])
-        for w in range(windows)
-        for k in range(2)
-    ]
-    for copy in copies:
-        copy.start()
-    for i, copy in enumerate(copies):
-        w, k = i // 2, i % 2
-        copy.wait()
-        pairs[k][1][w] = whiten_rows(held[k, w].astype(jnp.float32))
+
+    def fetch(k, w):
+        return pltpu.make_async_copy(pairs[k][0].at[w], held.at[k, w], done.at[k, w])
+
+    for w in range(windows):
+        for k in range(2):
+            fetch(k, w).start()
+
+    def body(w, carry):
+        for k in range(2):
+            fetch(k, w).wait()
+            pairs[k][1][w] = whiten_rows(held[k, w].astype(jnp.float32))
+        return carry
+
+    lax.fori_loop(0, windows, body, 0)
     flag_out[0] = flag[0]
 
 
@@ -77,6 +95,12 @@
     windows, _, width = spectra.shape
     return pl.pallas_call(
         source_kernel,
+        in_specs=[pl.BlockSpec(memory_space=pltpu.HBM)],
+        out_specs=pl.BlockSpec(memory_space=pltpu.VMEM),
+        scratch_shapes=[
+            pltpu.VMEM(spectra.shape, spectra.dtype),
+            pltpu.SemaphoreType.DMA((windows,)),
+        ],
         out_shape=jax.ShapeDtypeStruct((windows, width), jnp.bfloat16),
         compiler_params=pltpu.CompilerParams(vmem_limit_bytes=VMEM),
         cost_estimate=pl.CostEstimate(flops=10**6, bytes_accessed=2 * 2**20, transcendentals=0),

time: 69 us -> 68.3 us (0.990); the launches traced: 67.7 us -> 68.2 us
  waiting for transfers between devices: 4.48 us -> 6.42 us
  starting transfers between devices: 28.9 us -> 27.6 us
    ppermute x8, waiting for transfers between devices: 2.51 us -> 4.86 us  [route_swap(): lax.ppermute(block, ('win', 'chan'), [(j, i) if back else (i, j) for i, j...]
    ppermute x8, starting transfers between devices: 14.3 us -> 13.1 us  [route_swap(): lax.ppermute(block, ('win', 'chan'), [(j, i) if back else (i, j) for i, j...]
  transfers between devices with their start and end apart: 18 -> 18, of which waited for: 4 -> 5; matrix products, arithmetic and copies ran while one was open for 1% -> 1% of each run, Pallas kernels for 43% -> 43%
where the time goes in v5:
time: 68.3 us; the launch traced here: 68.2 us
  Pallas kernels  29.2 us (43%)
  starting transfers between devices  27.6 us (40%)
  waiting for transfers between devices  6.42 us (9%)
  local copies, waits for them, and re-layouts  2.2 us (3%)
  other arithmetic  1.76 us (3%)
  between operations  0.96 us (1%)
    pallas_call x5, Pallas kernels, correlate(): pl.pallas_call(functools.partial(correlate_kernel, groups, scale), in_spe...  22.7 us
    ppermute x9, starting transfers between devices, chip_shift(): lax.ppermute(block, 'win', [(i, (i + 2 * distance) % size) for i in range...  14.5 us
    ppermute x8, starting transfers between devices, route_swap(): lax.ppermute(block, ('win', 'chan'), [(j, i) if back else (i, j) for i, j...  13.1 us
    pallas_call x1, Pallas kernels, whiten_both(): pl.pallas_call(whiten_kernel, in_specs=[scalar] + [pl.BlockSpec(memory_sp...  5.79 us
    ppermute x8, waiting for transfers between devices, route_swap(): lax.ppermute(block, ('win', 'chan'), [(j, i) if back else (i, j) for i, j...  4.86 us
    unnamed x6, local copies, waits for them, and re-layouts  1.6 us
    ppermute x9, waiting for transfers between devices, chip_shift(): lax.ppermute(block, 'win', [(i, (i + 2 * distance) % size) for i in range...  1.56 us
  transfers between devices with their start and end apart: 18, of which 5 were waited for; matrix products, arithmetic and copies ran while one was open for 1% of the time, Pallas kernels for 43%

profile of v5, /device:TPU:34, one launch (start us, length us, event | category | flops | bytes accessed | tf_op | source)
XLA Modules:
  0.0 68.2 jit_solution(17503704874882368621)
XLA Ops:
  0.0 0.0 collective-permute-start.4
  0.0 0.0 copy-start
  0.0 1.6 %copy-done = bf16[8,16,8192]{2,1,0:T(8,128)(2,1)S(1)} copy-done((bf16[8,16,8192]{2,1,0:T(8,128)(2,1)S(1)}, bf16[8,16,8192]{2,1,0:T(8,128)(2,1)}, u32[]{:S(2)}) %copy-start) | copy-done | bytes 2097176
  1.6 0.0 copy-start.1
  1.6 0.7 whiten_source.1
  2.3 1.6 %collective-permute-start = (bf16[8,8192]{1,0:T(8,128)(2,1)S(1)}, bf16[8,8192]{1,0:T(8,128)(2,1)S(1)}, u32[]{:S(2)}, u32[]{:S(2)}) collective-permute-start(bf16[8,8192]{1,0:T(8,128)(2,1)S(1)} %whiten_source.1), channel_id=1, source_target_pairs={{0,1},{1,2},{2,3},{3,4},{4,5},{5,6},{6,7},{7,8},{8,9},{9,10},{10,1... | collective-permute-start | bytes 393224 | tf_op jit(solution)/shard_map/ppermute | solution.py:218
  3.8 2.5 %collective-permute-start.1 = (bf16[8,8192]{1,0:T(8,128)(2,1)S(1)}, bf16[8,8192]{1,0:T(8,128)(2,1)S(1)}, u32[]{:S(2)}, u32[]{:S(2)}) collective-permute-start(bf16[8,8192]{1,0:T(8,128)(2,1)S(1)} %whiten_source.1), channel_id=1, source_target_pairs={{0,2},{1,3},{2,4},{3,5},{4,6},{5,7},{6,8},{7,9},{8,10},{9,11},{10,... | collective-permute-start | bytes 393224 | tf_op jit(solution)/shard_map/ppermute | solution.py:218
  6.3 0.8 %collective-permute-start.2 = (bf16[8,8192]{1,0:T(8,128)(2,1)S(1)}, bf16[8,8192]{1,0:T(8,128)(2,1)S(1)}, u32[]{:S(2)}, u32[]{:S(2)}) collective-permute-start(bf16[8,8192]{1,0:T(8,128)(2,1)S(1)} %whiten_source.1), channel_id=1, source_target_pairs={{0,16},{1,0},{2,1},{3,2},{4,3},{5,4},{6,5},{7,6},{8,7},{9,8},{10,9... | collective-permute-start | bytes 393224 | tf_op jit(solution)/shard_map/ppermute | solution.py:218
  7.1 1.2 %collective-permute-start.3 = (bf16[8,8192]{1,0:T(8,128)(2,1)S(1)}, bf16[8,8192]{1,0:T(8,128)(2,1)S(1)}, u32[]{:S(2)}, u32[]{:S(2)}) collective-permute-start(bf16[8,8192]{1,0:T(8,128)(2,1)S(1)} %whiten_source.1), channel_id=1, source_target_pairs={{0,16},{1,17},{2,0},{3,1},{4,2},{5,3},{6,4},{7,5},{8,6},{9,7},{10,... | collective-permute-start | bytes 393224 | tf_op jit(solution)/shard_map/ppermute | solution.py:218
  9.0 0.0 collective-permute-done.4.sibling
  9.0 0.0 copy-done.1
  9.0 5.8 %whiten_both.1 = (bf16[8,16,8192]{2,1,0:T(8,128)(2,1)S(1)}, bf16[8,16,8192]{2,1,0:T(8,128)(2,1)S(1)}, s32[1]{0:T(128)}) custom-call(s32[1]{0:T(128)S(6)} %copy.5.flag, bf16[8,16,8192]{2,1,0:T(8,128)(2,1)S(1)} %copy-done.1, bf16[8,16,8192]{2,1,0:T(8,128)(2,1)} %collective-permute-done.4.sibling), custom_call_target="tpu_custom_call" | custom-call | flops 1000000000 | bytes 8388608 | tf_op jit(solution)/shard_map/whiten_both/pallas_call | solution.py:115
  14.8 0.0 collective-permute-done
  14.8 0.0 collective-permute-done.1
  14.8 0.0 collective-permute-done.2
  14.8 1.1 %collective-permute-done.3 = bf16[8,8192]{1,0:T(8,128)(2,1)S(1)} collective-permute-done((bf16[8,8192]{1,0:T(8,128)(2,1)S(1)}, bf16[8,8192]{1,0:T(8,128)(2,1)S(1)}, u32[]{:S(2)}, u32[]{:S(2)}) %collective-permute-start.3) | collective-permute-done | bytes 131104 | tf_op jit(solution)/shard_map/ppermute | solution.py:218
  15.9 1.6 %collective-permute-start.5 = (bf16[2,8,8192]{2,1,0:T(8,128)(2,1)S(1)}, bf16[2,8,8192]{2,1,0:T(8,128)(2,1)S(1)}, u32[]{:S(2)}, u32[]{:S(2)}) collective-permute-start(bf16[2,8,8192]{2,1,0:T(8,128)(2,1)S(1)} %pad_maximum_fusion.refs_2_), channel_id=1, source_target_pairs={{0,32},{16,48},{32,64},{48,80},{64,96},{80,112},{96,0},{112,16},{1... | collective-permute-start | bytes 786440 | tf_op jit(solution)/shard_map/ppermute | solution.py:223
  17.6 1.7 %collective-permute-start.6 = (bf16[2,8,8192]{2,1,0:T(8,128)(2,1)S(1)}, bf16[2,8,8192]{2,1,0:T(8,128)(2,1)S(1)}, u32[]{:S(2)}, u32[]{:S(2)}) collective-permute-start(bf16[2,8,8192]{2,1,0:T(8,128)(2,1)S(1)} %pad_maximum_fusion.refs_2_), channel_id=1, source_target_pairs={{0,96},{16,112},{32,0},{48,16},{64,32},{80,48},{96,64},{112,80},{1... | collective-permute-start | bytes 786440 | tf_op jit(solution)/shard_map/ppermute | solution.py:223
  19.3 0.4 collective-permute-start.7
  19.7 2.9 %collective-permute-start.8 = (bf16[2,8,8192]{2,1,0:T(8,128)(2,1)S(1)}, bf16[2,8,8192]{2,1,0:T(8,128)(2,1)S(1)}, u32[]{:S(2)}, u32[]{:S(2)}) collective-permute-start(bf16[2,8,8192]{2,1,0:T(8,128)(2,1)S(1)} %pad_maximum_fusion.1.refs_2_), channel_id=1, source_target_pairs={{0,96},{16,112},{32,0},{48,16},{64,32},{80,48},{96,64},{112,80},{1... | collective-permute-start | bytes 786440 | tf_op jit(solution)/shard_map/ppermute | solution.py:223
  22.6 3.7 %correlate_2.2 = bf16[2,32,256]{2,1,0:T(8,128)(2,1)S(1)} custom-call(s32[1]{0:T(128)} %bitcast.2.parity, bf16[8,16,8192]{2,1,0:T(8,128)(2,1)S(1)} %get-tuple-element.26.refs_0_, bf16[8,16,8192]{2,1,0:T(8,128)(2,1)S(1)} %get-tuple-element.27.refs_1_, bf16[2,8,8192]{2,1,0:T(8,128)(2,1)S(1)} %pad_maximum_fusion.refs_2_, ...), custom_call_target="tpu_custom_call" | custom-call | flops 2000000000 | bytes 8388608 | tf_op jit(solution)/shard_map/correlate_2/pallas_call | solution.py:187
  26.2 0.2 collective-permute-done.5.refs_2_
  26.5 0.4 collective-permute-done.6.refs_3_
  26.8 1.6 %collective-permute-start.9 = (bf16[2,8,8192]{2,1,0:T(8,128)(2,1)S(1)}, bf16[2,8,8192]{2,1,0:T(8,128)(2,1)S(1)}, u32[]{:S(2)}, u32[]{:S(2)}) collective-permute-start(bf16[2,8,8192]{2,1,0:T(8,128)(2,1)S(1)} %collective-permute-done.5.refs_2_), channel_id=1, source_target_pairs={{0,32},{16,48},{32,64},{48,80},{64,96},{80,112},{96,0},{112,16},{1... | collective-permute-start | bytes 786440 | tf_op jit(solution)/shard_map/ppermute | solution.py:223
  28.4 5.1 %correlate_4.3 = bf16[4,32,256]{2,1,0:T(8,128)(2,1)S(1)} custom-call(s32[1]{0:T(128)} %bitcast.2.parity, bf16[8,16,8192]{2,1,0:T(8,128)(2,1)S(1)} %get-tuple-element.26.refs_0_, bf16[8,16,8192]{2,1,0:T(8,128)(2,1)S(1)} %get-tuple-element.27.refs_1_, bf16[2,8,8192]{2,1,0:T(8,128)(2,1)S(1)} %collective-permute-done.5.refs_2_, ...), custom_call_target="tpu_custom_call" | custom-call | flops 4000000000 | bytes 8388608 | tf_op jit(solution)/shard_map/correlate_4/pallas_call | solution.py:187
  33.6 0.0 collective-permute-done.7.refs_2_
  33.6 0.0 collective-permute-done.8.refs_3_
  33.6 1.7 %collective-permute-start.10 = (bf16[2,8,8192]{2,1,0:T(8,128)(2,1)S(1)}, bf16[2,8,8192]{2,1,0:T(8,128)(2,1)S(1)}, u32[]{:S(2)}, u32[]{:S(2)}) collective-permute-start(bf16[2,8,8192]{2,1,0:T(8,128)(2,1)S(1)} %collective-permute-done.8.refs_3_), channel_id=1, source_target_pairs={{0,96},{16,112},{32,0},{48,16},{64,32},{80,48},{96,64},{112,80},{1... | collective-permute-start | bytes 786440 | tf_op jit(solution)/shard_map/ppermute | solution.py:223
  35.3 5.1 %correlate_4.4 = bf16[4,32,256]{2,1,0:T(8,128)(2,1)S(1)} custom-call(s32[1]{0:T(128)} %bitcast.2.parity, bf16[8,16,8192]{2,1,0:T(8,128)(2,1)S(1)} %get-tuple-element.26.refs_0_, bf16[8,16,8192]{2,1,0:T(8,128)(2,1)S(1)} %get-tuple-element.27.refs_1_, bf16[2,8,8192]{2,1,0:T(8,128)(2,1)S(1)} %collective-permute-done.7.refs_2_, ...), custom_call_target="tpu_custom_call" | custom-call | flops 4000000000 | bytes 8388608 | tf_op jit(solution)/shard_map/correlate_4/pallas_call | solution.py:187
  40.5 0.0 collective-permute-done.9.refs_2_
  40.5 0.0 collective-permute-done.10.refs_3_
  40.5 2.4 %collective-permute-start.13 = (bf16[4,32,256]{2,1,0:T(8,128)(2,1)S(1)}, bf16[4,32,256]{2,1,0:T(8,128)(2,1)S(1)}, u32[]{:S(2)}, u32[]{:S(2)}) collective-permute-start(bf16[4,32,256]{2,1,0:T(8,128)(2,1)S(1)} %pad_maximum_fusion.4), channel_id=1, source_target_pairs={{0,96},{16,112},{32,0},{48,16},{64,32},{80,48},{96,64},{112,80},{1... | collective-permute-start | bytes 196616 | tf_op jit(solution)/shard_map/ppermute | solution.py:223
  43.0 5.1 %correlate_4.5 = bf16[4,32,256]{2,1,0:T(8,128)(2,1)S(1)} custom-call(s32[1]{0:T(128)} %bitcast.2.parity, bf16[8,16,8192]{2,1,0:T(8,128)(2,1)S(1)} %get-tuple-element.26.refs_0_, bf16[8,16,8192]{2,1,0:T(8,128)(2,1)S(1)} %get-tuple-element.27.refs_1_, bf16[2,8,8192]{2,1,0:T(8,128)(2,1)S(1)} %collective-permute-done.9.refs_2_, ...), custom_call_target="tpu_custom_call" | custom-call | flops 4000000000 | bytes 8388608 | tf_op jit(solution)/shard_map/correlate_4/pallas_call | solution.py:187
  48.1 1.3 %collective-permute-start.12 = (bf16[4,32,256]{2,1,0:T(8,128)(2,1)S(1)}, bf16[4,32,256]{2,1,0:T(8,128)(2,1)S(1)}, u32[]{:S(2)}, u32[]{:S(2)}) collective-permute-start(bf16[4,32,256]{2,1,0:T(8,128)(2,1)S(1)} %correlate_4.5), channel_id=1, source_target_pairs={{0,64},{16,80},{32,96},{48,112},{64,0},{80,16},{96,32},{112,48},{1... | collective-permute-start | bytes 196616 | tf_op jit(solution)/shard_map/ppermute | solution.py:223
  49.4 0.0 copy-start.2
  49.4 0.9 %collective-permute-start.11 = (bf16[4,32,256]{2,1,0:T(8,128)(2,1)S(1)}, bf16[4,32,256]{2,1,0:T(8,128)(2,1)S(1)}, u32[]{:S(2)}, u32[]{:S(2)}) collective-permute-start(bf16[4,32,256]{2,1,0:T(8,128)(2,1)S(1)} %pad_maximum_fusion.3), channel_id=1, source_target_pairs={{0,32},{16,48},{32,64},{48,80},{64,96},{80,112},{96,0},{112,16},{1... | collective-permute-start | bytes 196616 | tf_op jit(solution)/shard_map/ppermute | solution.py:223
  50.3 3.6 %correlate_2.3 = bf16[2,32,256]{2,1,0:T(8,128)(2,1)S(1)} custom-call(s32[1]{0:T(128)} %bitcast.2.parity, bf16[8,16,8192]{2,1,0:T(8,128)(2,1)S(1)} %get-tuple-element.26.refs_0_, bf16[8,16,8192]{2,1,0:T(8,128)(2,1)S(1)} %get-tuple-element.27.refs_1_, bf16[2,8,8192]{2,1,0:T(8,128)(2,1)S(1)} %pad_maximum_fusion.1.refs_2_, ...), custom_call_target="tpu_custom_call" | custom-call | flops 2000000000 | bytes 8388608 | tf_op jit(solution)/shard_map/correlate_2/pallas_call | solution.py:187
  54.0 0.0 collective-permute-done.13
  54.0 0.0 collective-permute-done.12
  54.0 1.0 %collective-permute-done.11 = bf16[4,32,256]{2,1,0:T(8,128)(2,1)S(1)} collective-permute-done((bf16[4,32,256]{2,1,0:T(8,128)(2,1)S(1)}, bf16[4,32,256]{2,1,0:T(8,128)(2,1)S(1)}, u32[]{:S(2)}, u32[]{:S(2)}) %collective-permute-start.11) | collective-permute-done | bytes 65568 | tf_op jit(solution)/shard_map/ppermute | solution.py:223
  55.0 0.6 gather_fusion
  55.6 1.2 %collective-permute-start.17 = (bf16[128,256]{1,0:T(8,128)(2,1)S(1)}, bf16[128,256]{1,0:T(8,128)(2,1)S(1)}, u32[]{:S(2)}, u32[]{:S(2)}) collective-permute-start(bf16[128,256]{1,0:T(8,128)(2,1)S(1)} %bitcast.36), channel_id=1, source_target_pairs={{1,0},{2,1},{3,2},{4,3},{5,4},{6,5},{7,6},{8,7},{9,8},{10,9},{11,1... | collective-permute-start | bytes 196616 | tf_op jit(solution)/shard_map/ppermute | solution.py:218
  56.8 1.2 %collective-permute-start.16 = (bf16[128,256]{1,0:T(8,128)(2,1)S(1)}, bf16[128,256]{1,0:T(8,128)(2,1)S(1)}, u32[]{:S(2)}, u32[]{:S(2)}) collective-permute-start(bf16[128,256]{1,0:T(8,128)(2,1)S(1)} %bitcast.34), channel_id=1, source_target_pairs={{2,0},{3,1},{4,2},{5,3},{6,4},{7,5},{8,6},{9,7},{10,8},{11,9},{12,... | collective-permute-start | bytes 196616 | tf_op jit(solution)/shard_map/ppermute | solution.py:218
  58.1 2.5 %collective-permute-start.15 = (bf16[128,256]{1,0:T(8,128)(2,1)S(1)}, bf16[128,256]{1,0:T(8,128)(2,1)S(1)}, u32[]{:S(2)}, u32[]{:S(2)}) collective-permute-start(bf16[128,256]{1,0:T(8,128)(2,1)S(1)} %bitcast.32), channel_id=1, source_target_pairs={{16,0},{0,1},{1,2},{2,3},{3,4},{4,5},{5,6},{6,7},{7,8},{8,9},{9,10... | collective-permute-start | bytes 196616 | tf_op jit(solution)/shard_map/ppermute | solution.py:218
  60.5 2.2 %collective-permute-start.14 = (bf16[128,256]{1,0:T(8,128)(2,1)S(1)}, bf16[128,256]{1,0:T(8,128)(2,1)S(1)}, u32[]{:S(2)}, u32[]{:S(2)}) collective-permute-start(bf16[128,256]{1,0:T(8,128)(2,1)S(1)} %bitcast.31), channel_id=1, source_target_pairs={{16,0},{17,1},{0,2},{1,3},{2,4},{3,5},{4,6},{5,7},{6,8},{7,9},{8,1... | collective-permute-start | bytes 196616 | tf_op jit(solution)/shard_map/ppermute | solution.py:218
  62.7 0.0 copy-done.2
  62.7 0.6 bitcast_and_fusion.3
  63.4 0.0 collective-permute-done.17
  63.4 0.0 collective-permute-done.16
  63.4 0.0 collective-permute-done.15
  63.5 3.7 %collective-permute-done.14 = bf16[128,256]{1,0:T(8,128)(2,1)S(1)} collective-permute-done((bf16[128,256]{1,0:T(8,128)(2,1)S(1)}, bf16[128,256]{1,0:T(8,128)(2,1)S(1)}, u32[]{:S(2)}, u32[]{:S(2)}) %collective-permute-start.14) | collective-permute-done | bytes 65568 | tf_op jit(solution)/shard_map/ppermute | solution.py:218
  67.2 0.9 %select_select_fusion = f32[1,1,4,128,256]{4,3,2,1,0:T(8,128)} fusion(f32[128,256]{1,0:T(8,128)S(1)} %convert_element_type.19, f32[128,256]{1,0:T(8,128)S(1)} %convert_element_type.18, f32[128,256]{1,0:T(8,128)S(1)} %convert_element_type.17, f32[128,256]{1,0:T(8,128)S(1)} %convert_element_type.16, pred[4]{0:T(512)(128)(4,1)S(1)} %get-tuple-element.53, ...), kind=kLoop, calls=%fused_computation.1 | loop fusion | flops 524288 | bytes 1048592 | tf_op jit(solution)/shard_map/jit(_where)/select_n | solution.py:281
  (15 shorter events, 0.2 us)
Async XLA Ops:
  0.0 9.0 %collective-permute-start.4 = (bf16[8,16,8192]{2,1,0:T(8,128)(2,1)}, bf16[8,16,8192]{2,1,0:T(8,128)(2,1)}, u32[]{:S(2)}, u32[]{:S(2)}) collective-permute-start(bf16[8,16,8192]{2,1,0:T(8,128)(2,1)} %own.1), channel_id=1, source_target_pairs={{0,16},{16,0},{32,48},{48,32},{64,80},{80,64},{96,112},{112,96},{1... | collective-permute-start | bytes 6291464 | tf_op jit(solution)/shard_map/ppermute | solution.py:228
  0.0 1.6 %copy-start = (bf16[8,16,8192]{2,1,0:T(8,128)(2,1)S(1)}, bf16[8,16,8192]{2,1,0:T(8,128)(2,1)}, u32[]{:S(2)}) copy-start(bf16[8,16,8192]{2,1,0:T(8,128)(2,1)} %own.1) | copy-start | bytes 6291460
  1.6 7.4 %copy-start.1 = (bf16[8,16,8192]{2,1,0:T(8,128)(2,1)S(1)}, bf16[8,16,8192]{2,1,0:T(8,128)(2,1)}, u32[]{:S(2)}) copy-start(bf16[8,16,8192]{2,1,0:T(8,128)(2,1)} %own.1) | copy-start | bytes 6291460
  2.3 12.5 %collective-permute-start = (bf16[8,8192]{1,0:T(8,128)(2,1)S(1)}, bf16[8,8192]{1,0:T(8,128)(2,1)S(1)}, u32[]{:S(2)}, u32[]{:S(2)}) collective-permute-start(bf16[8,8192]{1,0:T(8,128)(2,1)S(1)} %whiten_source.1), channel_id=1, source_target_pairs={{0,1},{1,2},{2,3},{3,4},{4,5},{5,6},{6,7},{7,8},{8,9},{9,10},{10,1... | collective-permute-start | bytes 393224 | tf_op jit(solution)/shard_map/ppermute | solution.py:218
  3.8 11.0 %collective-permute-start.1 = (bf16[8,8192]{1,0:T(8,128)(2,1)S(1)}, bf16[8,8192]{1,0:T(8,128)(2,1)S(1)}, u32[]{:S(2)}, u32[]{:S(2)}) collective-permute-start(bf16[8,8192]{1,0:T(8,128)(2,1)S(1)} %whiten_source.1), channel_id=1, source_target_pairs={{0,2},{1,3},{2,4},{3,5},{4,6},{5,7},{6,8},{7,9},{8,10},{9,11},{10,... | collective-permute-start | bytes 393224 | tf_op jit(solution)/shard_map/ppermute | solution.py:218
  6.3 8.5 %collective-permute-start.2 = (bf16[8,8192]{1,0:T(8,128)(2,1)S(1)}, bf16[8,8192]{1,0:T(8,128)(2,1)S(1)}, u32[]{:S(2)}, u32[]{:S(2)}) collective-permute-start(bf16[8,8192]{1,0:T(8,128)(2,1)S(1)} %whiten_source.1), channel_id=1, source_target_pairs={{0,16},{1,0},{2,1},{3,2},{4,3},{5,4},{6,5},{7,6},{8,7},{9,8},{10,9... | collective-permute-start | bytes 393224 | tf_op jit(solution)/shard_map/ppermute | solution.py:218
  7.1 8.8 %collective-permute-start.3 = (bf16[8,8192]{1,0:T(8,128)(2,1)S(1)}, bf16[8,8192]{1,0:T(8,128)(2,1)S(1)}, u32[]{:S(2)}, u32[]{:S(2)}) collective-permute-start(bf16[8,8192]{1,0:T(8,128)(2,1)S(1)} %whiten_source.1), channel_id=1, source_target_pairs={{0,16},{1,17},{2,0},{3,1},{4,2},{5,3},{6,4},{7,5},{8,6},{9,7},{10,... | collective-permute-start | bytes 393224 | tf_op jit(solution)/shard_map/ppermute | solution.py:218
  15.9 10.5 %collective-permute-start.5 = (bf16[2,8,8192]{2,1,0:T(8,128)(2,1)S(1)}, bf16[2,8,8192]{2,1,0:T(8,128)(2,1)S(1)}, u32[]{:S(2)}, u32[]{:S(2)}) collective-permute-start(bf16[2,8,8192]{2,1,0:T(8,128)(2,1)S(1)} %pad_maximum_fusion.refs_2_), channel_id=1, source_target_pairs={{0,32},{16,48},{32,64},{48,80},{64,96},{80,112},{96,0},{112,16},{1... | collective-permute-start | bytes 786440 | tf_op jit(solution)/shard_map/ppermute | solution.py:223
  17.6 9.2 %collective-permute-start.6 = (bf16[2,8,8192]{2,1,0:T(8,128)(2,1)S(1)}, bf16[2,8,8192]{2,1,0:T(8,128)(2,1)S(1)}, u32[]{:S(2)}, u32[]{:S(2)}) collective-permute-start(bf16[2,8,8192]{2,1,0:T(8,128)(2,1)S(1)} %pad_maximum_fusion.refs_2_), channel_id=1, source_target_pairs={{0,96},{16,112},{32,0},{48,16},{64,32},{80,48},{96,64},{112,80},{1... | collective-permute-start | bytes 786440 | tf_op jit(solution)/shard_map/ppermute | solution.py:223
  19.3 14.3 %collective-permute-start.7 = (bf16[2,8,8192]{2,1,0:T(8,128)(2,1)S(1)}, bf16[2,8,8192]{2,1,0:T(8,128)(2,1)S(1)}, u32[]{:S(2)}, u32[]{:S(2)}) collective-permute-start(bf16[2,8,8192]{2,1,0:T(8,128)(2,1)S(1)} %pad_maximum_fusion.1.refs_2_), channel_id=1, source_target_pairs={{0,32},{16,48},{32,64},{48,80},{64,96},{80,112},{96,0},{112,16},{1... | collective-permute-start | bytes 786440 | tf_op jit(solution)/shard_map/ppermute | solution.py:223
  19.7 13.9 %collective-permute-start.8 = (bf16[2,8,8192]{2,1,0:T(8,128)(2,1)S(1)}, bf16[2,8,8192]{2,1,0:T(8,128)(2,1)S(1)}, u32[]{:S(2)}, u32[]{:S(2)}) collective-permute-start(bf16[2,8,8192]{2,1,0:T(8,128)(2,1)S(1)} %pad_maximum_fusion.1.refs_2_), channel_id=1, source_target_pairs={{0,96},{16,112},{32,0},{48,16},{64,32},{80,48},{96,64},{112,80},{1... | collective-permute-start | bytes 786440 | tf_op jit(solution)/shard_map/ppermute | solution.py:223
  26.8 13.7 %collective-permute-start.9 = (bf16[2,8,8192]{2,1,0:T(8,128)(2,1)S(1)}, bf16[2,8,8192]{2,1,0:T(8,128)(2,1)S(1)}, u32[]{:S(2)}, u32[]{:S(2)}) collective-permute-start(bf16[2,8,8192]{2,1,0:T(8,128)(2,1)S(1)} %collective-permute-done.5.refs_2_), channel_id=1, source_target_pairs={{0,32},{16,48},{32,64},{48,80},{64,96},{80,112},{96,0},{112,16},{1... | collective-permute-start | bytes 786440 | tf_op jit(solution)/shard_map/ppermute | solution.py:223
  33.6 6.9 %collective-permute-start.10 = (bf16[2,8,8192]{2,1,0:T(8,128)(2,1)S(1)}, bf16[2,8,8192]{2,1,0:T(8,128)(2,1)S(1)}, u32[]{:S(2)}, u32[]{:S(2)}) collective-permute-start(bf16[2,8,8192]{2,1,0:T(8,128)(2,1)S(1)} %collective-permute-done.8.refs_3_), channel_id=1, source_target_pairs={{0,96},{16,112},{32,0},{48,16},{64,32},{80,48},{96,64},{112,80},{1... | collective-permute-start | bytes 786440 | tf_op jit(solution)/shard_map/ppermute | solution.py:223
  40.5 13.5 %collective-permute-start.13 = (bf16[4,32,256]{2,1,0:T(8,128)(2,1)S(1)}, bf16[4,32,256]{2,1,0:T(8,128)(2,1)S(1)}, u32[]{:S(2)}, u32[]{:S(2)}) collective-permute-start(bf16[4,32,256]{2,1,0:T(8,128)(2,1)S(1)} %pad_maximum_fusion.4), channel_id=1, source_target_pairs={{0,96},{16,112},{32,0},{48,16},{64,32},{80,48},{96,64},{112,80},{1... | collective-permute-start | bytes 196616 | tf_op jit(solution)/shard_map/ppermute | solution.py:223
  48.1 5.9 %collective-permute-start.12 = (bf16[4,32,256]{2,1,0:T(8,128)(2,1)S(1)}, bf16[4,32,256]{2,1,0:T(8,128)(2,1)S(1)}, u32[]{:S(2)}, u32[]{:S(2)}) collective-permute-start(bf16[4,32,256]{2,1,0:T(8,128)(2,1)S(1)} %correlate_4.5), channel_id=1, source_target_pairs={{0,64},{16,80},{32,96},{48,112},{64,0},{80,16},{96,32},{112,48},{1... | collective-permute-start | bytes 196616 | tf_op jit(solution)/shard_map/ppermute | solution.py:223
  49.4 13.3 %copy-start.2 = (s32[1,4]{1,0:T(1,128)S(1)}, s32[1,4]{1,0:T(1,128)}, u32[]{:S(2)}) copy-start(s32[1,4]{1,0:T(1,128)} %param.5) | copy-start | bytes 52
  49.4 5.5 %collective-permute-start.11 = (bf16[4,32,256]{2,1,0:T(8,128)(2,1)S(1)}, bf16[4,32,256]{2,1,0:T(8,128)(2,1)S(1)}, u32[]{:S(2)}, u32[]{:S(2)}) collective-permute-start(bf16[4,32,256]{2,1,0:T(8,128)(2,1)S(1)} %pad_maximum_fusion.3), channel_id=1, source_target_pairs={{0,32},{16,48},{32,64},{48,80},{64,96},{80,112},{96,0},{112,16},{1... | collective-permute-start | bytes 196616 | tf_op jit(solution)/shard_map/ppermute | solution.py:223
  55.6 7.8 %collective-permute-start.17 = (bf16[128,256]{1,0:T(8,128)(2,1)S(1)}, bf16[128,256]{1,0:T(8,128)(2,1)S(1)}, u32[]{:S(2)}, u32[]{:S(2)}) collective-permute-start(bf16[128,256]{1,0:T(8,128)(2,1)S(1)} %bitcast.36), channel_id=1, source_target_pairs={{1,0},{2,1},{3,2},{4,3},{5,4},{6,5},{7,6},{8,7},{9,8},{10,9},{11,1... | collective-permute-start | bytes 196616 | tf_op jit(solution)/shard_map/ppermute | solution.py:218
  56.8 6.6 %collective-permute-start.16 = (bf16[128,256]{1,0:T(8,128)(2,1)S(1)}, bf16[128,256]{1,0:T(8,128)(2,1)S(1)}, u32[]{:S(2)}, u32[]{:S(2)}) collective-permute-start(bf16[128,256]{1,0:T(8,128)(2,1)S(1)} %bitcast.34), channel_id=1, source_target_pairs={{2,0},{3,1},{4,2},{5,3},{6,4},{7,5},{8,6},{9,7},{10,8},{11,9},{12,... | collective-permute-start | bytes 196616 | tf_op jit(solution)/shard_map/ppermute | solution.py:218
  58.1 5.4 %collective-permute-start.15 = (bf16[128,256]{1,0:T(8,128)(2,1)S(1)}, bf16[128,256]{1,0:T(8,128)(2,1)S(1)}, u32[]{:S(2)}, u32[]{:S(2)}) collective-permute-start(bf16[128,256]{1,0:T(8,128)(2,1)S(1)} %bitcast.32), channel_id=1, source_target_pairs={{16,0},{0,1},{1,2},{2,3},{3,4},{4,5},{5,6},{6,7},{7,8},{8,9},{9,10... | collective-permute-start | bytes 196616 | tf_op jit(solution)/shard_map/ppermute | solution.py:218
  60.5 6.7 %collective-permute-start.14 = (bf16[128,256]{1,0:T(8,128)(2,1)S(1)}, bf16[128,256]{1,0:T(8,128)(2,1)S(1)}, u32[]{:S(2)}, u32[]{:S(2)}) collective-permute-start(bf16[128,256]{1,0:T(8,128)(2,1)S(1)} %bitcast.31), channel_id=1, source_target_pairs={{16,0},{17,1},{0,2},{1,3},{2,4},{3,5},{4,6},{5,7},{6,8},{7,9},{8,1... | collective-permute-start | bytes 196616 | tf_op jit(solution)/shard_map/ppermute | solution.py:218

commit v6 on v5

--- a/solution.py
+++ b/solution.py
@@ -244,9 +244,10 @@
     first, second = jnp.stack(arrived[:half]), jnp.stack(arrived[half:])
 
     up_first, down_first = chip_shift(first, 1), chip_shift(first, -1)
-    up_second, down_second = chip_shift(second, 1), chip_shift(second, -1)
     run = functools.partial(correlate, parity, own, sibling, table=table, scale=scale)
     own_first = run([first])
+    own_first, second = lax.optimization_barrier((own_first, second))
+    up_second, down_second = chip_shift(second, 1), chip_shift(second, -1)
     own_first, up_first, down_first = lax.optimization_barrier((own_first, up_first, down_first))
     far_first = chip_shift(up_first, 1)
     near_first = run([up_first, down_first])

time: 68.3 us -> 67.5 us (0.988)
  starting transfers between devices: 27.6 us -> 25.1 us
  waiting for transfers between devices: 6.42 us -> 8.15 us
    ppermute x9, starting transfers between devices: 14.5 us -> 11.9 us  [chip_shift(): lax.ppermute(block, 'win', [(i, (i + 2 * distance) % size) for i in range...]
    ppermute x9, waiting for transfers between devices: 1.56 us -> 3.3 us  [chip_shift(): lax.ppermute(block, 'win', [(i, (i + 2 * distance) % size) for i in range...]
where the time goes in v6:
time: 67.5 us; the launch traced here: 67.3 us
  Pallas kernels  29.2 us (43%)
  starting transfers between devices  25.1 us (37%)
  waiting for transfers between devices  8.15 us (12%)
  local copies, waits for them, and re-layouts  2.2 us (3%)
  other arithmetic  1.76 us (3%)
  between operations  0.94 us (1%)
    pallas_call x5, Pallas kernels, correlate(): pl.pallas_call(functools.partial(correlate_kernel, groups, scale), in_spe...  22.8 us
    ppermute x8, starting transfers between devices, route_swap(): lax.ppermute(block, ('win', 'chan'), [(j, i) if back else (i, j) for i, j...  13.1 us
    ppermute x9, starting transfers between devices, chip_shift(): lax.ppermute(block, 'win', [(i, (i + 2 * distance) % size) for i in range...  11.9 us
    pallas_call x1, Pallas kernels, whiten_both(): pl.pallas_call(whiten_kernel, in_specs=[scalar] + [pl.BlockSpec(memory_sp...  5.79 us
    ppermute x8, waiting for transfers between devices, route_swap(): lax.ppermute(block, ('win', 'chan'), [(j, i) if back else (i, j) for i, j...  4.85 us
    ppermute x9, waiting for transfers between devices, chip_shift(): lax.ppermute(block, 'win', [(i, (i + 2 * distance) % size) for i in range...  3.3 us
    unnamed x6, local copies, waits for them, and re-layouts  1.6 us
  transfers between devices with their start and end apart: 18, of which 5 were waited for; matrix products, arithmetic and copies ran while one was open for 1% of the time, Pallas kernels for 43%

profile of v6, /device:TPU:34, one launch (start us, length us, event | category | flops | bytes accessed | tf_op | source)
XLA Modules:
  0.0 67.3 jit_solution(11300448990624586564)
XLA Ops:
  0.0 0.0 collective-permute-start.4
  0.0 0.0 copy-start
  0.0 1.6 %copy-done = bf16[8,16,8192]{2,1,0:T(8,128)(2,1)S(1)} copy-done((bf16[8,16,8192]{2,1,0:T(8,128)(2,1)S(1)}, bf16[8,16,8192]{2,1,0:T(8,128)(2,1)}, u32[]{:S(2)}) %copy-start) | copy-done | bytes 2097176
  1.6 0.0 copy-start.1
  1.6 0.7 whiten_source.1
  2.3 1.6 %collective-permute-start = (bf16[8,8192]{1,0:T(8,128)(2,1)S(1)}, bf16[8,8192]{1,0:T(8,128)(2,1)S(1)}, u32[]{:S(2)}, u32[]{:S(2)}) collective-permute-start(bf16[8,8192]{1,0:T(8,128)(2,1)S(1)} %whiten_source.1), channel_id=1, source_target_pairs={{0,1},{1,2},{2,3},{3,4},{4,5},{5,6},{6,7},{7,8},{8,9},{9,10},{10,1... | collective-permute-start | bytes 393224 | tf_op jit(solution)/shard_map/ppermute | solution.py:218
  3.8 2.5 %collective-permute-start.1 = (bf16[8,8192]{1,0:T(8,128)(2,1)S(1)}, bf16[8,8192]{1,0:T(8,128)(2,1)S(1)}, u32[]{:S(2)}, u32[]{:S(2)}) collective-permute-start(bf16[8,8192]{1,0:T(8,128)(2,1)S(1)} %whiten_source.1), channel_id=1, source_target_pairs={{0,2},{1,3},{2,4},{3,5},{4,6},{5,7},{6,8},{7,9},{8,10},{9,11},{10,... | collective-permute-start | bytes 393224 | tf_op jit(solution)/shard_map/ppermute | solution.py:218
  6.3 0.8 %collective-permute-start.2 = (bf16[8,8192]{1,0:T(8,128)(2,1)S(1)}, bf16[8,8192]{1,0:T(8,128)(2,1)S(1)}, u32[]{:S(2)}, u32[]{:S(2)}) collective-permute-start(bf16[8,8192]{1,0:T(8,128)(2,1)S(1)} %whiten_source.1), channel_id=1, source_target_pairs={{0,16},{1,0},{2,1},{3,2},{4,3},{5,4},{6,5},{7,6},{8,7},{9,8},{10,9... | collective-permute-start | bytes 393224 | tf_op jit(solution)/shard_map/ppermute | solution.py:218
  7.1 1.2 %collective-permute-start.3 = (bf16[8,8192]{1,0:T(8,128)(2,1)S(1)}, bf16[8,8192]{1,0:T(8,128)(2,1)S(1)}, u32[]{:S(2)}, u32[]{:S(2)}) collective-permute-start(bf16[8,8192]{1,0:T(8,128)(2,1)S(1)} %whiten_source.1), channel_id=1, source_target_pairs={{0,16},{1,17},{2,0},{3,1},{4,2},{5,3},{6,4},{7,5},{8,6},{9,7},{10,... | collective-permute-start | bytes 393224 | tf_op jit(solution)/shard_map/ppermute | solution.py:218
  9.0 0.0 collective-permute-done.4.sibling
  9.0 0.0 copy-done.1
  9.0 5.8 %whiten_both.1 = (bf16[8,16,8192]{2,1,0:T(8,128)(2,1)S(1)}, bf16[8,16,8192]{2,1,0:T(8,128)(2,1)S(1)}, s32[1]{0:T(128)}) custom-call(s32[1]{0:T(128)S(6)} %copy.5.flag, bf16[8,16,8192]{2,1,0:T(8,128)(2,1)S(1)} %copy-done.1, bf16[8,16,8192]{2,1,0:T(8,128)(2,1)} %collective-permute-done.4.sibling), custom_call_target="tpu_custom_call" | custom-call | flops 1000000000 | bytes 8388608 | tf_op jit(solution)/shard_map/whiten_both/pallas_call | solution.py:115
  14.8 0.0 collective-permute-done
  14.8 0.0 collective-permute-done.1
  14.8 0.0 collective-permute-done.2
  14.8 1.1 %collective-permute-done.3 = bf16[8,8192]{1,0:T(8,128)(2,1)S(1)} collective-permute-done((bf16[8,8192]{1,0:T(8,128)(2,1)S(1)}, bf16[8,8192]{1,0:T(8,128)(2,1)S(1)}, u32[]{:S(2)}, u32[]{:S(2)}) %collective-permute-start.3) | collective-permute-done | bytes 131104 | tf_op jit(solution)/shard_map/ppermute | solution.py:218
  15.9 1.6 %collective-permute-start.5 = (bf16[2,8,8192]{2,1,0:T(8,128)(2,1)S(1)}, bf16[2,8,8192]{2,1,0:T(8,128)(2,1)S(1)}, u32[]{:S(2)}, u32[]{:S(2)}) collective-permute-start(bf16[2,8,8192]{2,1,0:T(8,128)(2,1)S(1)} %pad_maximum_fusion.refs_2_), channel_id=1, source_target_pairs={{0,32},{16,48},{32,64},{48,80},{64,96},{80,112},{96,0},{112,16},{1... | collective-permute-start | bytes 786440 | tf_op jit(solution)/shard_map/ppermute | solution.py:223
  17.6 1.7 %collective-permute-start.6 = (bf16[2,8,8192]{2,1,0:T(8,128)(2,1)S(1)}, bf16[2,8,8192]{2,1,0:T(8,128)(2,1)S(1)}, u32[]{:S(2)}, u32[]{:S(2)}) collective-permute-start(bf16[2,8,8192]{2,1,0:T(8,128)(2,1)S(1)} %pad_maximum_fusion.refs_2_), channel_id=1, source_target_pairs={{0,96},{16,112},{32,0},{48,16},{64,32},{80,48},{96,64},{112,80},{1... | collective-permute-start | bytes 786440 | tf_op jit(solution)/shard_map/ppermute | solution.py:223
  19.3 3.7 %correlate_2.2 = bf16[2,32,256]{2,1,0:T(8,128)(2,1)S(1)} custom-call(s32[1]{0:T(128)} %bitcast.2.parity, bf16[8,16,8192]{2,1,0:T(8,128)(2,1)S(1)} %get-tuple-element.28.refs_0_, bf16[8,16,8192]{2,1,0:T(8,128)(2,1)S(1)} %get-tuple-element.29.refs_1_, bf16[2,8,8192]{2,1,0:T(8,128)(2,1)S(1)} %pad_maximum_fusion.refs_2_, ...), custom_call_target="tpu_custom_call" | custom-call | flops 2000000000 | bytes 8388608 | tf_op jit(solution)/shard_map/correlate_2/pallas_call | solution.py:187
  22.9 0.4 collective-permute-start.7
  23.4 2.9 %collective-permute-start.8 = (bf16[2,8,8192]{2,1,0:T(8,128)(2,1)S(1)}, bf16[2,8,8192]{2,1,0:T(8,128)(2,1)S(1)}, u32[]{:S(2)}, u32[]{:S(2)}) collective-permute-start(bf16[2,8,8192]{2,1,0:T(8,128)(2,1)S(1)} %pad_maximum_fusion.1.refs_2_), channel_id=1, source_target_pairs={{0,96},{16,112},{32,0},{48,16},{64,32},{80,48},{96,64},{112,80},{1... | collective-permute-start | bytes 786440 | tf_op jit(solution)/shard_map/ppermute | solution.py:223
  26.2 0.0 collective-permute-done.5.refs_2_
  26.3 0.0 collective-permute-done.6.refs_3_
  26.3 0.6 collective-permute-start.9
  26.8 5.1 %correlate_4.3 = bf16[4,32,256]{2,1,0:T(8,128)(2,1)S(1)} custom-call(s32[1]{0:T(128)} %bitcast.2.parity, bf16[8,16,8192]{2,1,0:T(8,128)(2,1)S(1)} %get-tuple-element.28.refs_0_, bf16[8,16,8192]{2,1,0:T(8,128)(2,1)S(1)} %get-tuple-element.29.refs_1_, bf16[2,8,8192]{2,1,0:T(8,128)(2,1)S(1)} %collective-permute-done.5.refs_2_, ...), custom_call_target="tpu_custom_call" | custom-call | flops 4000000000 | bytes 8388608 | tf_op jit(solution)/shard_map/correlate_4/pallas_call | solution.py:187
  32.0 1.5 %collective-permute-done.7.refs_2_ = bf16[2,8,8192]{2,1,0:T(8,128)(2,1)S(1)} collective-permute-done((bf16[2,8,8192]{2,1,0:T(8,128)(2,1)S(1)}, bf16[2,8,8192]{2,1,0:T(8,128)(2,1)S(1)}, u32[]{:S(2)}, u32[]{:S(2)}) %collective-permute-start.7) | collective-permute-done | bytes 262176 | tf_op jit(solution)/shard_map/ppermute | solution.py:223
  33.5 0.0 collective-permute-done.8.refs_3_
  33.5 1.3 %collective-permute-start.10 = (bf16[2,8,8192]{2,1,0:T(8,128)(2,1)S(1)}, bf16[2,8,8192]{2,1,0:T(8,128)(2,1)S(1)}, u32[]{:S(2)}, u32[]{:S(2)}) collective-permute-start(bf16[2,8,8192]{2,1,0:T(8,128)(2,1)S(1)} %collective-permute-done.8.refs_3_), channel_id=1, source_target_pairs={{0,96},{16,112},{32,0},{48,16},{64,32},{80,48},{96,64},{112,80},{1... | collective-permute-start | bytes 786440 | tf_op jit(solution)/shard_map/ppermute | solution.py:223
  34.7 5.1 %correlate_4.4 = bf16[4,32,256]{2,1,0:T(8,128)(2,1)S(1)} custom-call(s32[1]{0:T(128)} %bitcast.2.parity, bf16[8,16,8192]{2,1,0:T(8,128)(2,1)S(1)} %get-tuple-element.28.refs_0_, bf16[8,16,8192]{2,1,0:T(8,128)(2,1)S(1)} %get-tuple-element.29.refs_1_, bf16[2,8,8192]{2,1,0:T(8,128)(2,1)S(1)} %collective-permute-done.7.refs_2_, ...), custom_call_target="tpu_custom_call" | custom-call | flops 4000000000 | bytes 8388608 | tf_op jit(solution)/shard_map/correlate_4/pallas_call | solution.py:187
  39.9 0.0 collective-permute-done.9.refs_2_
  39.9 0.0 collective-permute-done.10.refs_3_
  40.0 2.5 %collective-permute-start.13 = (bf16[4,32,256]{2,1,0:T(8,128)(2,1)S(1)}, bf16[4,32,256]{2,1,0:T(8,128)(2,1)S(1)}, u32[]{:S(2)}, u32[]{:S(2)}) collective-permute-start(bf16[4,32,256]{2,1,0:T(8,128)(2,1)S(1)} %pad_maximum_fusion.4), channel_id=1, source_target_pairs={{0,96},{16,112},{32,0},{48,16},{64,32},{80,48},{96,64},{112,80},{1... | collective-permute-start | bytes 196616 | tf_op jit(solution)/shard_map/ppermute | solution.py:223
  42.4 5.2 %correlate_4.5 = bf16[4,32,256]{2,1,0:T(8,128)(2,1)S(1)} custom-call(s32[1]{0:T(128)} %bitcast.2.parity, bf16[8,16,8192]{2,1,0:T(8,128)(2,1)S(1)} %get-tuple-element.28.refs_0_, bf16[8,16,8192]{2,1,0:T(8,128)(2,1)S(1)} %get-tuple-element.29.refs_1_, bf16[2,8,8192]{2,1,0:T(8,128)(2,1)S(1)} %collective-permute-done.9.refs_2_, ...), custom_call_target="tpu_custom_call" | custom-call | flops 4000000000 | bytes 8388608 | tf_op jit(solution)/shard_map/correlate_4/pallas_call | solution.py:187
  47.6 0.5 collective-permute-start.12
  48.1 0.0 copy-start.2
  48.1 0.5 collective-permute-start.11
  48.6 3.6 %correlate_2.3 = bf16[2,32,256]{2,1,0:T(8,128)(2,1)S(1)} custom-call(s32[1]{0:T(128)} %bitcast.2.parity, bf16[8,16,8192]{2,1,0:T(8,128)(2,1)S(1)} %get-tuple-element.28.refs_0_, bf16[8,16,8192]{2,1,0:T(8,128)(2,1)S(1)} %get-tuple-element.29.refs_1_, bf16[2,8,8192]{2,1,0:T(8,128)(2,1)S(1)} %pad_maximum_fusion.1.refs_2_, ...), custom_call_target="tpu_custom_call" | custom-call | flops 2000000000 | bytes 8388608 | tf_op jit(solution)/shard_map/correlate_2/pallas_call | solution.py:187
  52.3 0.0 collective-permute-done.13
  52.3 1.2 %collective-permute-done.12 = bf16[4,32,256]{2,1,0:T(8,128)(2,1)S(1)} collective-permute-done((bf16[4,32,256]{2,1,0:T(8,128)(2,1)S(1)}, bf16[4,32,256]{2,1,0:T(8,128)(2,1)S(1)}, u32[]{:S(2)}, u32[]{:S(2)}) %collective-permute-start.12) | collective-permute-done | bytes 65568 | tf_op jit(solution)/shard_map/ppermute | solution.py:223
  53.5 0.7 collective-permute-done.11
  54.2 0.6 gather_fusion
  54.8 1.2 %collective-permute-start.17 = (bf16[128,256]{1,0:T(8,128)(2,1)S(1)}, bf16[128,256]{1,0:T(8,128)(2,1)S(1)}, u32[]{:S(2)}, u32[]{:S(2)}) collective-permute-start(bf16[128,256]{1,0:T(8,128)(2,1)S(1)} %bitcast.36), channel_id=1, source_target_pairs={{1,0},{2,1},{3,2},{4,3},{5,4},{6,5},{7,6},{8,7},{9,8},{10,9},{11,1... | collective-permute-start | bytes 196616 | tf_op jit(solution)/shard_map/ppermute | solution.py:218
  56.0 1.2 %collective-permute-start.16 = (bf16[128,256]{1,0:T(8,128)(2,1)S(1)}, bf16[128,256]{1,0:T(8,128)(2,1)S(1)}, u32[]{:S(2)}, u32[]{:S(2)}) collective-permute-start(bf16[128,256]{1,0:T(8,128)(2,1)S(1)} %bitcast.34), channel_id=1, source_target_pairs={{2,0},{3,1},{4,2},{5,3},{6,4},{7,5},{8,6},{9,7},{10,8},{11,9},{12,... | collective-permute-start | bytes 196616 | tf_op jit(solution)/shard_map/ppermute | solution.py:218
  57.2 2.5 %collective-permute-start.15 = (bf16[128,256]{1,0:T(8,128)(2,1)S(1)}, bf16[128,256]{1,0:T(8,128)(2,1)S(1)}, u32[]{:S(2)}, u32[]{:S(2)}) collective-permute-start(bf16[128,256]{1,0:T(8,128)(2,1)S(1)} %bitcast.32), channel_id=1, source_target_pairs={{16,0},{0,1},{1,2},{2,3},{3,4},{4,5},{5,6},{6,7},{7,8},{8,9},{9,10... | collective-permute-start | bytes 196616 | tf_op jit(solution)/shard_map/ppermute | solution.py:218
  59.7 2.2 %collective-permute-start.14 = (bf16[128,256]{1,0:T(8,128)(2,1)S(1)}, bf16[128,256]{1,0:T(8,128)(2,1)S(1)}, u32[]{:S(2)}, u32[]{:S(2)}) collective-permute-start(bf16[128,256]{1,0:T(8,128)(2,1)S(1)} %bitcast.31), channel_id=1, source_target_pairs={{16,0},{17,1},{0,2},{1,3},{2,4},{3,5},{4,6},{5,7},{6,8},{7,9},{8,1... | collective-permute-start | bytes 196616 | tf_op jit(solution)/shard_map/ppermute | solution.py:218
  61.9 0.0 copy-done.2
  61.9 0.6 bitcast_and_fusion.3
  62.5 0.0 collective-permute-done.17
  62.6 0.0 collective-permute-done.16
  62.6 0.0 collective-permute-done.15
  62.6 3.7 %collective-permute-done.14 = bf16[128,256]{1,0:T(8,128)(2,1)S(1)} collective-permute-done((bf16[128,256]{1,0:T(8,128)(2,1)S(1)}, bf16[128,256]{1,0:T(8,128)(2,1)S(1)}, u32[]{:S(2)}, u32[]{:S(2)}) %collective-permute-start.14) | collective-permute-done | bytes 65568 | tf_op jit(solution)/shard_map/ppermute | solution.py:218
  66.4 0.9 %select_select_fusion = f32[1,1,4,128,256]{4,3,2,1,0:T(8,128)} fusion(f32[128,256]{1,0:T(8,128)S(1)} %convert_element_type.19, f32[128,256]{1,0:T(8,128)S(1)} %convert_element_type.18, f32[128,256]{1,0:T(8,128)S(1)} %convert_element_type.17, f32[128,256]{1,0:T(8,128)S(1)} %convert_element_type.16, pred[4]{0:T(512)(128)(4,1)S(1)} %get-tuple-element.57, ...), kind=kLoop, calls=%fused_computation.1 | loop fusion | flops 524288 | bytes 1048592 | tf_op jit(solution)/shard_map/jit(_where)/select_n | solution.py:282
  (15 shorter events, 0.2 us)
Async XLA Ops:
  0.0 9.0 %collective-permute-start.4 = (bf16[8,16,8192]{2,1,0:T(8,128)(2,1)}, bf16[8,16,8192]{2,1,0:T(8,128)(2,1)}, u32[]{:S(2)}, u32[]{:S(2)}) collective-permute-start(bf16[8,16,8192]{2,1,0:T(8,128)(2,1)} %own.1), channel_id=1, source_target_pairs={{0,16},{16,0},{32,48},{48,32},{64,80},{80,64},{96,112},{112,96},{1... | collective-permute-start | bytes 6291464 | tf_op jit(solution)/shard_map/ppermute | solution.py:228
  0.0 1.6 %copy-start = (bf16[8,16,8192]{2,1,0:T(8,128)(2,1)S(1)}, bf16[8,16,8192]{2,1,0:T(8,128)(2,1)}, u32[]{:S(2)}) copy-start(bf16[8,16,8192]{2,1,0:T(8,128)(2,1)} %own.1) | copy-start | bytes 6291460
  1.6 7.4 %copy-start.1 = (bf16[8,16,8192]{2,1,0:T(8,128)(2,1)S(1)}, bf16[8,16,8192]{2,1,0:T(8,128)(2,1)}, u32[]{:S(2)}) copy-start(bf16[8,16,8192]{2,1,0:T(8,128)(2,1)} %own.1) | copy-start | bytes 6291460
  2.3 12.5 %collective-permute-start = (bf16[8,8192]{1,0:T(8,128)(2,1)S(1)}, bf16[8,8192]{1,0:T(8,128)(2,1)S(1)}, u32[]{:S(2)}, u32[]{:S(2)}) collective-permute-start(bf16[8,8192]{1,0:T(8,128)(2,1)S(1)} %whiten_source.1), channel_id=1, source_target_pairs={{0,1},{1,2},{2,3},{3,4},{4,5},{5,6},{6,7},{7,8},{8,9},{9,10},{10,1... | collective-permute-start | bytes 393224 | tf_op jit(solution)/shard_map/ppermute | solution.py:218
  3.8 11.0 %collective-permute-start.1 = (bf16[8,8192]{1,0:T(8,128)(2,1)S(1)}, bf16[8,8192]{1,0:T(8,128)(2,1)S(1)}, u32[]{:S(2)}, u32[]{:S(2)}) collective-permute-start(bf16[8,8192]{1,0:T(8,128)(2,1)S(1)} %whiten_source.1), channel_id=1, source_target_pairs={{0,2},{1,3},{2,4},{3,5},{4,6},{5,7},{6,8},{7,9},{8,10},{9,11},{10,... | collective-permute-start | bytes 393224 | tf_op jit(solution)/shard_map/ppermute | solution.py:218
  6.3 8.5 %collective-permute-start.2 = (bf16[8,8192]{1,0:T(8,128)(2,1)S(1)}, bf16[8,8192]{1,0:T(8,128)(2,1)S(1)}, u32[]{:S(2)}, u32[]{:S(2)}) collective-permute-start(bf16[8,8192]{1,0:T(8,128)(2,1)S(1)} %whiten_source.1), channel_id=1, source_target_pairs={{0,16},{1,0},{2,1},{3,2},{4,3},{5,4},{6,5},{7,6},{8,7},{9,8},{10,9... | collective-permute-start | bytes 393224 | tf_op jit(solution)/shard_map/ppermute | solution.py:218
  7.1 8.8 %collective-permute-start.3 = (bf16[8,8192]{1,0:T(8,128)(2,1)S(1)}, bf16[8,8192]{1,0:T(8,128)(2,1)S(1)}, u32[]{:S(2)}, u32[]{:S(2)}) collective-permute-start(bf16[8,8192]{1,0:T(8,128)(2,1)S(1)} %whiten_source.1), channel_id=1, source_target_pairs={{0,16},{1,17},{2,0},{3,1},{4,2},{5,3},{6,4},{7,5},{8,6},{9,7},{10,... | collective-permute-start | bytes 393224 | tf_op jit(solution)/shard_map/ppermute | solution.py:218
  15.9 10.3 %collective-permute-start.5 = (bf16[2,8,8192]{2,1,0:T(8,128)(2,1)S(1)}, bf16[2,8,8192]{2,1,0:T(8,128)(2,1)S(1)}, u32[]{:S(2)}, u32[]{:S(2)}) collective-permute-start(bf16[2,8,8192]{2,1,0:T(8,128)(2,1)S(1)} %pad_maximum_fusion.refs_2_), channel_id=1, source_target_pairs={{0,32},{16,48},{32,64},{48,80},{64,96},{80,112},{96,0},{112,16},{1... | collective-permute-start | bytes 786440 | tf_op jit(solution)/shard_map/ppermute | solution.py:223
  17.6 8.7 %collective-permute-start.6 = (bf16[2,8,8192]{2,1,0:T(8,128)(2,1)S(1)}, bf16[2,8,8192]{2,1,0:T(8,128)(2,1)S(1)}, u32[]{:S(2)}, u32[]{:S(2)}) collective-permute-start(bf16[2,8,8192]{2,1,0:T(8,128)(2,1)S(1)} %pad_maximum_fusion.refs_2_), channel_id=1, source_target_pairs={{0,96},{16,112},{32,0},{48,16},{64,32},{80,48},{96,64},{112,80},{1... | collective-permute-start | bytes 786440 | tf_op jit(solution)/shard_map/ppermute | solution.py:223
  22.9 10.5 %collective-permute-start.7 = (bf16[2,8,8192]{2,1,0:T(8,128)(2,1)S(1)}, bf16[2,8,8192]{2,1,0:T(8,128)(2,1)S(1)}, u32[]{:S(2)}, u32[]{:S(2)}) collective-permute-start(bf16[2,8,8192]{2,1,0:T(8,128)(2,1)S(1)} %pad_maximum_fusion.1.refs_2_), channel_id=1, source_target_pairs={{0,32},{16,48},{32,64},{48,80},{64,96},{80,112},{96,0},{112,16},{1... | collective-permute-start | bytes 786440 | tf_op jit(solution)/shard_map/ppermute | solution.py:223
  23.4 10.1 %collective-permute-start.8 = (bf16[2,8,8192]{2,1,0:T(8,128)(2,1)S(1)}, bf16[2,8,8192]{2,1,0:T(8,128)(2,1)S(1)}, u32[]{:S(2)}, u32[]{:S(2)}) collective-permute-start(bf16[2,8,8192]{2,1,0:T(8,128)(2,1)S(1)} %pad_maximum_fusion.1.refs_2_), channel_id=1, source_target_pairs={{0,96},{16,112},{32,0},{48,16},{64,32},{80,48},{96,64},{112,80},{1... | collective-permute-start | bytes 786440 | tf_op jit(solution)/shard_map/ppermute | solution.py:223
  26.3 13.7 %collective-permute-start.9 = (bf16[2,8,8192]{2,1,0:T(8,128)(2,1)S(1)}, bf16[2,8,8192]{2,1,0:T(8,128)(2,1)S(1)}, u32[]{:S(2)}, u32[]{:S(2)}) collective-permute-start(bf16[2,8,8192]{2,1,0:T(8,128)(2,1)S(1)} %collective-permute-done.5.refs_2_), channel_id=1, source_target_pairs={{0,32},{16,48},{32,64},{48,80},{64,96},{80,112},{96,0},{112,16},{1... | collective-permute-start | bytes 786440 | tf_op jit(solution)/shard_map/ppermute | solution.py:223
  33.5 6.5 %collective-permute-start.10 = (bf16[2,8,8192]{2,1,0:T(8,128)(2,1)S(1)}, bf16[2,8,8192]{2,1,0:T(8,128)(2,1)S(1)}, u32[]{:S(2)}, u32[]{:S(2)}) collective-permute-start(bf16[2,8,8192]{2,1,0:T(8,128)(2,1)S(1)} %collective-permute-done.8.refs_3_), channel_id=1, source_target_pairs={{0,96},{16,112},{32,0},{48,16},{64,32},{80,48},{96,64},{112,80},{1... | collective-permute-start | bytes 786440 | tf_op jit(solution)/shard_map/ppermute | solution.py:223
  40.0 12.3 %collective-permute-start.13 = (bf16[4,32,256]{2,1,0:T(8,128)(2,1)S(1)}, bf16[4,32,256]{2,1,0:T(8,128)(2,1)S(1)}, u32[]{:S(2)}, u32[]{:S(2)}) collective-permute-start(bf16[4,32,256]{2,1,0:T(8,128)(2,1)S(1)} %pad_maximum_fusion.4), channel_id=1, source_target_pairs={{0,96},{16,112},{32,0},{48,16},{64,32},{80,48},{96,64},{112,80},{1... | collective-permute-start | bytes 196616 | tf_op jit(solution)/shard_map/ppermute | solution.py:223
  47.6 5.9 %collective-permute-start.12 = (bf16[4,32,256]{2,1,0:T(8,128)(2,1)S(1)}, bf16[4,32,256]{2,1,0:T(8,128)(2,1)S(1)}, u32[]{:S(2)}, u32[]{:S(2)}) collective-permute-start(bf16[4,32,256]{2,1,0:T(8,128)(2,1)S(1)} %correlate_4.5), channel_id=1, source_target_pairs={{0,64},{16,80},{32,96},{48,112},{64,0},{80,16},{96,32},{112,48},{1... | collective-permute-start | bytes 196616 | tf_op jit(solution)/shard_map/ppermute | solution.py:223
  48.1 13.8 %copy-start.2 = (s32[1,4]{1,0:T(1,128)S(1)}, s32[1,4]{1,0:T(1,128)}, u32[]{:S(2)}) copy-start(s32[1,4]{1,0:T(1,128)} %param.5) | copy-start | bytes 52
  48.1 6.0 %collective-permute-start.11 = (bf16[4,32,256]{2,1,0:T(8,128)(2,1)S(1)}, bf16[4,32,256]{2,1,0:T(8,128)(2,1)S(1)}, u32[]{:S(2)}, u32[]{:S(2)}) collective-permute-start(bf16[4,32,256]{2,1,0:T(8,128)(2,1)S(1)} %pad_maximum_fusion.3), channel_id=1, source_target_pairs={{0,32},{16,48},{32,64},{48,80},{64,96},{80,112},{96,0},{112,16},{1... | collective-permute-start | bytes 196616 | tf_op jit(solution)/shard_map/ppermute | solution.py:223
  54.8 7.8 %collective-permute-start.17 = (bf16[128,256]{1,0:T(8,128)(2,1)S(1)}, bf16[128,256]{1,0:T(8,128)(2,1)S(1)}, u32[]{:S(2)}, u32[]{:S(2)}) collective-permute-start(bf16[128,256]{1,0:T(8,128)(2,1)S(1)} %bitcast.36), channel_id=1, source_target_pairs={{1,0},{2,1},{3,2},{4,3},{5,4},{6,5},{7,6},{8,7},{9,8},{10,9},{11,1... | collective-permute-start | bytes 196616 | tf_op jit(solution)/shard_map/ppermute | solution.py:218
  56.0 6.6 %collective-permute-start.16 = (bf16[128,256]{1,0:T(8,128)(2,1)S(1)}, bf16[128,256]{1,0:T(8,128)(2,1)S(1)}, u32[]{:S(2)}, u32[]{:S(2)}) collective-permute-start(bf16[128,256]{1,0:T(8,128)(2,1)S(1)} %bitcast.34), channel_id=1, source_target_pairs={{2,0},{3,1},{4,2},{5,3},{6,4},{7,5},{8,6},{9,7},{10,8},{11,9},{12,... | collective-permute-start | bytes 196616 | tf_op jit(solution)/shard_map/ppermute | solution.py:218
  57.2 5.5 %collective-permute-start.15 = (bf16[128,256]{1,0:T(8,128)(2,1)S(1)}, bf16[128,256]{1,0:T(8,128)(2,1)S(1)}, u32[]{:S(2)}, u32[]{:S(2)}) collective-permute-start(bf16[128,256]{1,0:T(8,128)(2,1)S(1)} %bitcast.32), channel_id=1, source_target_pairs={{16,0},{0,1},{1,2},{2,3},{3,4},{4,5},{5,6},{6,7},{7,8},{8,9},{9,10... | collective-permute-start | bytes 196616 | tf_op jit(solution)/shard_map/ppermute | solution.py:218
  59.7 6.7 %collective-permute-start.14 = (bf16[128,256]{1,0:T(8,128)(2,1)S(1)}, bf16[128,256]{1,0:T(8,128)(2,1)S(1)}, u32[]{:S(2)}, u32[]{:S(2)}) collective-permute-start(bf16[128,256]{1,0:T(8,128)(2,1)S(1)} %bitcast.31), channel_id=1, source_target_pairs={{16,0},{17,1},{0,2},{1,3},{2,4},{3,5},{4,6},{5,7},{6,8},{7,9},{8,1... | collective-permute-start | bytes 196616 | tf_op jit(solution)/shard_map/ppermute | solution.py:218

commit v7 on v6

--- a/solution.py
+++ b/solution.py
@@ -249,18 +249,20 @@
     own_first, second = lax.optimization_barrier((own_first, second))
     up_second, down_second = chip_shift(second, 1), chip_shift(second, -1)
     own_first, up_first, down_first = lax.optimization_barrier((own_first, up_first, down_first))
+    near_first = run([up_first, down_first])
+    near_first, up_first, up_second, down_second = lax.optimization_barrier(
+        (near_first, up_first, up_second, down_second)
+    )
     far_first = chip_shift(up_first, 1)
-    near_first = run([up_first, down_first])
-    near_first, up_second, down_second = lax.optimization_barrier(
-        (near_first, up_second, down_second)
-    )
     far_second = chip_shift(down_second, -1)
     near_second = run([up_second, down_second])
     near_second, far_first, far_second = lax.optimization_barrier(
         (near_second, far_first, far_second)
     )
     c_far = run([far_first, far_second])
-    c_far, second = lax.optimization_barrier((c_far, second))
+    c_far, second, near_first, near_second = lax.optimization_barrier(
+        (c_far, second, near_first, near_second)
+    )
     c_own = jnp.concatenate([own_first, run([second])])
     c_up = jnp.concatenate([near_first[:half], near_second[:half]])
     c_down = jnp.concatenate([near_first[half:], near_second[half:]])

time: 67.5 us -> 67.2 us (level)
  waiting for transfers between devices: 8.15 us -> 6.02 us
  starting transfers between devices: 25.1 us -> 26.9 us
    ppermute x9, waiting for transfers between devices: 3.3 us -> 1.21 us  [chip_shift(): lax.ppermute(block, 'win', [(i, (i + 2 * distance) % size) for i in range...]
    ppermute x9, starting transfers between devices: 11.9 us -> 13.8 us  [chip_shift(): lax.ppermute(block, 'win', [(i, (i + 2 * distance) % size) for i in range...]
  transfers between devices with their start and end apart: 18 -> 18, of which waited for: 5 -> 4; matrix products, arithmetic and copies ran while one was open for 1% -> 1% of each run, Pallas kernels for 43% -> 36%
where the time goes in v7:
time: 67.2 us; the launch traced here: 67.1 us
  Pallas kernels  29.2 us (43%)
  starting transfers between devices  26.9 us (40%)
  waiting for transfers between devices  6.02 us (9%)
  local copies, waits for them, and re-layouts  2.2 us (3%)
  other arithmetic  1.81 us (3%)
  between operations  0.93 us (1%)
    pallas_call x5, Pallas kernels, correlate(): pl.pallas_call(functools.partial(correlate_kernel, groups, scale), in_spe...  22.8 us
    ppermute x9, starting transfers between devices, chip_shift(): lax.ppermute(block, 'win', [(i, (i + 2 * distance) % size) for i in range...  13.8 us
    ppermute x8, starting transfers between devices, route_swap(): lax.ppermute(block, ('win', 'chan'), [(j, i) if back else (i, j) for i, j...  13.1 us
    pallas_call x1, Pallas kernels, whiten_both(): pl.pallas_call(whiten_kernel, in_specs=[scalar] + [pl.BlockSpec(memory_sp...  5.79 us
    ppermute x8, waiting for transfers between devices, route_swap(): lax.ppermute(block, ('win', 'chan'), [(j, i) if back else (i, j) for i, j...  4.8 us
    unnamed x6, local copies, waits for them, and re-layouts  1.6 us
  transfers between devices with their start and end apart: 18, of which 4 were waited for; matrix products, arithmetic and copies ran while one was open for 1% of the time, Pallas kernels for 36%

profile of v7, /device:TPU:34, one launch (start us, length us, event | category | flops | bytes accessed | tf_op | source)
XLA Modules:
  0.0 67.1 jit_solution(10147004468912460056)
XLA Ops:
  0.0 0.0 collective-permute-start.4
  0.0 0.0 copy-start
  0.0 1.6 %copy-done = bf16[8,16,8192]{2,1,0:T(8,128)(2,1)S(1)} copy-done((bf16[8,16,8192]{2,1,0:T(8,128)(2,1)S(1)}, bf16[8,16,8192]{2,1,0:T(8,128)(2,1)}, u32[]{:S(2)}) %copy-start) | copy-done | bytes 2097176
  1.6 0.0 copy-start.1
  1.6 0.7 whiten_source.1
  2.3 1.6 %collective-permute-start = (bf16[8,8192]{1,0:T(8,128)(2,1)S(1)}, bf16[8,8192]{1,0:T(8,128)(2,1)S(1)}, u32[]{:S(2)}, u32[]{:S(2)}) collective-permute-start(bf16[8,8192]{1,0:T(8,128)(2,1)S(1)} %whiten_source.1), channel_id=1, source_target_pairs={{0,1},{1,2},{2,3},{3,4},{4,5},{5,6},{6,7},{7,8},{8,9},{9,10},{10,1... | collective-permute-start | bytes 393224 | tf_op jit(solution)/shard_map/ppermute | solution.py:218
  3.8 2.5 %collective-permute-start.1 = (bf16[8,8192]{1,0:T(8,128)(2,1)S(1)}, bf16[8,8192]{1,0:T(8,128)(2,1)S(1)}, u32[]{:S(2)}, u32[]{:S(2)}) collective-permute-start(bf16[8,8192]{1,0:T(8,128)(2,1)S(1)} %whiten_source.1), channel_id=1, source_target_pairs={{0,2},{1,3},{2,4},{3,5},{4,6},{5,7},{6,8},{7,9},{8,10},{9,11},{10,... | collective-permute-start | bytes 393224 | tf_op jit(solution)/shard_map/ppermute | solution.py:218
  6.3 0.8 %collective-permute-start.2 = (bf16[8,8192]{1,0:T(8,128)(2,1)S(1)}, bf16[8,8192]{1,0:T(8,128)(2,1)S(1)}, u32[]{:S(2)}, u32[]{:S(2)}) collective-permute-start(bf16[8,8192]{1,0:T(8,128)(2,1)S(1)} %whiten_source.1), channel_id=1, source_target_pairs={{0,16},{1,0},{2,1},{3,2},{4,3},{5,4},{6,5},{7,6},{8,7},{9,8},{10,9... | collective-permute-start | bytes 393224 | tf_op jit(solution)/shard_map/ppermute | solution.py:218
  7.1 1.2 %collective-permute-start.3 = (bf16[8,8192]{1,0:T(8,128)(2,1)S(1)}, bf16[8,8192]{1,0:T(8,128)(2,1)S(1)}, u32[]{:S(2)}, u32[]{:S(2)}) collective-permute-start(bf16[8,8192]{1,0:T(8,128)(2,1)S(1)} %whiten_source.1), channel_id=1, source_target_pairs={{0,16},{1,17},{2,0},{3,1},{4,2},{5,3},{6,4},{7,5},{8,6},{9,7},{10,... | collective-permute-start | bytes 393224 | tf_op jit(solution)/shard_map/ppermute | solution.py:218
  9.0 0.0 collective-permute-done.4.sibling
  9.0 0.0 copy-done.1
  9.0 5.8 %whiten_both.1 = (bf16[8,16,8192]{2,1,0:T(8,128)(2,1)S(1)}, bf16[8,16,8192]{2,1,0:T(8,128)(2,1)S(1)}, s32[1]{0:T(128)}) custom-call(s32[1]{0:T(128)S(6)} %copy.5.flag, bf16[8,16,8192]{2,1,0:T(8,128)(2,1)S(1)} %copy-done.1, bf16[8,16,8192]{2,1,0:T(8,128)(2,1)} %collective-permute-done.4.sibling), custom_call_target="tpu_custom_call" | custom-call | flops 1000000000 | bytes 8388608 | tf_op jit(solution)/shard_map/whiten_both/pallas_call | solution.py:115
  14.8 0.0 collective-permute-done
  14.8 0.0 collective-permute-done.1
  14.8 0.0 collective-permute-done.2
  14.8 1.1 %collective-permute-done.3 = bf16[8,8192]{1,0:T(8,128)(2,1)S(1)} collective-permute-done((bf16[8,8192]{1,0:T(8,128)(2,1)S(1)}, bf16[8,8192]{1,0:T(8,128)(2,1)S(1)}, u32[]{:S(2)}, u32[]{:S(2)}) %collective-permute-start.3) | collective-permute-done | bytes 131104 | tf_op jit(solution)/shard_map/ppermute | solution.py:218
  15.9 1.6 %collective-permute-start.5 = (bf16[2,8,8192]{2,1,0:T(8,128)(2,1)S(1)}, bf16[2,8,8192]{2,1,0:T(8,128)(2,1)S(1)}, u32[]{:S(2)}, u32[]{:S(2)}) collective-permute-start(bf16[2,8,8192]{2,1,0:T(8,128)(2,1)S(1)} %pad_maximum_fusion.refs_2_), channel_id=1, source_target_pairs={{0,32},{16,48},{32,64},{48,80},{64,96},{80,112},{96,0},{112,16},{1... | collective-permute-start | bytes 786440 | tf_op jit(solution)/shard_map/ppermute | solution.py:223
  17.6 1.7 %collective-permute-start.6 = (bf16[2,8,8192]{2,1,0:T(8,128)(2,1)S(1)}, bf16[2,8,8192]{2,1,0:T(8,128)(2,1)S(1)}, u32[]{:S(2)}, u32[]{:S(2)}) collective-permute-start(bf16[2,8,8192]{2,1,0:T(8,128)(2,1)S(1)} %pad_maximum_fusion.refs_2_), channel_id=1, source_target_pairs={{0,96},{16,112},{32,0},{48,16},{64,32},{80,48},{96,64},{112,80},{1... | collective-permute-start | bytes 786440 | tf_op jit(solution)/shard_map/ppermute | solution.py:223
  19.3 3.7 %correlate_2.2 = bf16[2,32,256]{2,1,0:T(8,128)(2,1)S(1)} custom-call(s32[1]{0:T(128)} %bitcast.2.parity, bf16[8,16,8192]{2,1,0:T(8,128)(2,1)S(1)} %get-tuple-element.31.refs_0_, bf16[8,16,8192]{2,1,0:T(8,128)(2,1)S(1)} %get-tuple-element.32.refs_1_, bf16[2,8,8192]{2,1,0:T(8,128)(2,1)S(1)} %pad_maximum_fusion.refs_2_, ...), custom_call_target="tpu_custom_call" | custom-call | flops 2000000000 | bytes 8388608 | tf_op jit(solution)/shard_map/correlate_2/pallas_call | solution.py:187
  22.9 0.4 collective-permute-start.7
  23.4 2.9 %collective-permute-start.8 = (bf16[2,8,8192]{2,1,0:T(8,128)(2,1)S(1)}, bf16[2,8,8192]{2,1,0:T(8,128)(2,1)S(1)}, u32[]{:S(2)}, u32[]{:S(2)}) collective-permute-start(bf16[2,8,8192]{2,1,0:T(8,128)(2,1)S(1)} %pad_maximum_fusion.1.refs_2_), channel_id=1, source_target_pairs={{0,96},{16,112},{32,0},{48,16},{64,32},{80,48},{96,64},{112,80},{1... | collective-permute-start | bytes 786440 | tf_op jit(solution)/shard_map/ppermute | solution.py:223
  26.2 0.0 collective-permute-done.5.refs_2_
  26.3 0.0 collective-permute-done.6.refs_3_
  26.3 5.2 %correlate_4.3 = bf16[4,32,256]{2,1,0:T(8,128)(2,1)S(1)} custom-call(s32[1]{0:T(128)} %bitcast.2.parity, bf16[8,16,8192]{2,1,0:T(8,128)(2,1)S(1)} %get-tuple-element.31.refs_0_, bf16[8,16,8192]{2,1,0:T(8,128)(2,1)S(1)} %get-tuple-element.32.refs_1_, bf16[2,8,8192]{2,1,0:T(8,128)(2,1)S(1)} %collective-permute-done.5.refs_2_, ...), custom_call_target="tpu_custom_call" | custom-call | flops 4000000000 | bytes 8388608 | tf_op jit(solution)/shard_map/correlate_4/pallas_call | solution.py:187
  31.4 0.0 collective-permute-done.7.refs_2_
  31.4 0.0 collective-permute-done.8.refs_3_
  31.4 0.7 %collective-permute-start.9 = (bf16[2,8,8192]{2,1,0:T(8,128)(2,1)S(1)}, bf16[2,8,8192]{2,1,0:T(8,128)(2,1)S(1)}, u32[]{:S(2)}, u32[]{:S(2)}) collective-permute-start(bf16[2,8,8192]{2,1,0:T(8,128)(2,1)S(1)} %collective-permute-done.5.refs_2_), channel_id=1, source_target_pairs={{0,32},{16,48},{32,64},{48,80},{64,96},{80,112},{96,0},{112,16},{1... | collective-permute-start | bytes 786440 | tf_op jit(solution)/shard_map/ppermute | solution.py:223
  32.1 2.6 %collective-permute-start.10 = (bf16[2,8,8192]{2,1,0:T(8,128)(2,1)S(1)}, bf16[2,8,8192]{2,1,0:T(8,128)(2,1)S(1)}, u32[]{:S(2)}, u32[]{:S(2)}) collective-permute-start(bf16[2,8,8192]{2,1,0:T(8,128)(2,1)S(1)} %collective-permute-done.8.refs_3_), channel_id=1, source_target_pairs={{0,96},{16,112},{32,0},{48,16},{64,32},{80,48},{96,64},{112,80},{1... | collective-permute-start | bytes 786440 | tf_op jit(solution)/shard_map/ppermute | solution.py:223
  34.7 5.1 %correlate_4.4 = bf16[4,32,256]{2,1,0:T(8,128)(2,1)S(1)} custom-call(s32[1]{0:T(128)} %bitcast.2.parity, bf16[8,16,8192]{2,1,0:T(8,128)(2,1)S(1)} %get-tuple-element.31.refs_0_, bf16[8,16,8192]{2,1,0:T(8,128)(2,1)S(1)} %get-tuple-element.32.refs_1_, bf16[2,8,8192]{2,1,0:T(8,128)(2,1)S(1)} %collective-permute-done.7.refs_2_, ...), custom_call_target="tpu_custom_call" | custom-call | flops 4000000000 | bytes 8388608 | tf_op jit(solution)/shard_map/correlate_4/pallas_call | solution.py:187
  39.9 0.0 collective-permute-done.9.refs_2_
  39.9 0.0 collective-permute-done.10.refs_3_
  39.9 5.2 %correlate_4.5 = bf16[4,32,256]{2,1,0:T(8,128)(2,1)S(1)} custom-call(s32[1]{0:T(128)} %bitcast.2.parity, bf16[8,16,8192]{2,1,0:T(8,128)(2,1)S(1)} %get-tuple-element.31.refs_0_, bf16[8,16,8192]{2,1,0:T(8,128)(2,1)S(1)} %get-tuple-element.32.refs_1_, bf16[2,8,8192]{2,1,0:T(8,128)(2,1)S(1)} %collective-permute-done.9.refs_2_, ...), custom_call_target="tpu_custom_call" | custom-call | flops 4000000000 | bytes 8388608 | tf_op jit(solution)/shard_map/correlate_4/pallas_call | solution.py:187
  45.1 2.5 %collective-permute-start.13 = (bf16[4,32,256]{2,1,0:T(8,128)(2,1)S(1)}, bf16[4,32,256]{2,1,0:T(8,128)(2,1)S(1)}, u32[]{:S(2)}, u32[]{:S(2)}) collective-permute-start(bf16[4,32,256]{2,1,0:T(8,128)(2,1)S(1)} %pad_maximum_fusion.4), channel_id=1, source_target_pairs={{0,96},{16,112},{32,0},{48,16},{64,32},{80,48},{96,64},{112,80},{1... | collective-permute-start | bytes 196616 | tf_op jit(solution)/shard_map/ppermute | solution.py:223
  47.6 0.0 collective-permute-start.12
  47.6 0.0 copy-start.2
  47.6 1.4 %collective-permute-start.11 = (bf16[4,32,256]{2,1,0:T(8,128)(2,1)S(1)}, bf16[4,32,256]{2,1,0:T(8,128)(2,1)S(1)}, u32[]{:S(2)}, u32[]{:S(2)}) collective-permute-start(bf16[4,32,256]{2,1,0:T(8,128)(2,1)S(1)} %pad_maximum_fusion.3), channel_id=1, source_target_pairs={{0,32},{16,48},{32,64},{48,80},{64,96},{80,112},{96,0},{112,16},{1... | collective-permute-start | bytes 196616 | tf_op jit(solution)/shard_map/ppermute | solution.py:223
  49.0 3.6 %correlate_2.3 = bf16[2,32,256]{2,1,0:T(8,128)(2,1)S(1)} custom-call(s32[1]{0:T(128)} %bitcast.2.parity, bf16[8,16,8192]{2,1,0:T(8,128)(2,1)S(1)} %get-tuple-element.31.refs_0_, bf16[8,16,8192]{2,1,0:T(8,128)(2,1)S(1)} %get-tuple-element.32.refs_1_, bf16[2,8,8192]{2,1,0:T(8,128)(2,1)S(1)} %pad_maximum_fusion.1.refs_2_, ...), custom_call_target="tpu_custom_call" | custom-call | flops 2000000000 | bytes 8388608 | tf_op jit(solution)/shard_map/correlate_2/pallas_call | solution.py:187
  52.7 0.0 collective-permute-done.13
  52.7 0.8 %collective-permute-done.12 = bf16[4,32,256]{2,1,0:T(8,128)(2,1)S(1)} collective-permute-done((bf16[4,32,256]{2,1,0:T(8,128)(2,1)S(1)}, bf16[4,32,256]{2,1,0:T(8,128)(2,1)S(1)}, u32[]{:S(2)}, u32[]{:S(2)}) %collective-permute-start.12) | collective-permute-done | bytes 65568 | tf_op jit(solution)/shard_map/ppermute | solution.py:223
  53.5 0.4 collective-permute-done.11
  53.9 0.6 gather_fusion
  54.5 1.2 %collective-permute-start.17 = (bf16[128,256]{1,0:T(8,128)(2,1)S(1)}, bf16[128,256]{1,0:T(8,128)(2,1)S(1)}, u32[]{:S(2)}, u32[]{:S(2)}) collective-permute-start(bf16[128,256]{1,0:T(8,128)(2,1)S(1)} %bitcast.36), channel_id=1, source_target_pairs={{1,0},{2,1},{3,2},{4,3},{5,4},{6,5},{7,6},{8,7},{9,8},{10,9},{11,1... | collective-permute-start | bytes 196616 | tf_op jit(solution)/shard_map/ppermute | solution.py:218
  55.7 1.2 %collective-permute-start.16 = (bf16[128,256]{1,0:T(8,128)(2,1)S(1)}, bf16[128,256]{1,0:T(8,128)(2,1)S(1)}, u32[]{:S(2)}, u32[]{:S(2)}) collective-permute-start(bf16[128,256]{1,0:T(8,128)(2,1)S(1)} %bitcast.33), channel_id=1, source_target_pairs={{2,0},{3,1},{4,2},{5,3},{6,4},{7,5},{8,6},{9,7},{10,8},{11,9},{12,... | collective-permute-start | bytes 196616 | tf_op jit(solution)/shard_map/ppermute | solution.py:218
  56.9 2.5 %collective-permute-start.15 = (bf16[128,256]{1,0:T(8,128)(2,1)S(1)}, bf16[128,256]{1,0:T(8,128)(2,1)S(1)}, u32[]{:S(2)}, u32[]{:S(2)}) collective-permute-start(bf16[128,256]{1,0:T(8,128)(2,1)S(1)} %bitcast.32), channel_id=1, source_target_pairs={{16,0},{0,1},{1,2},{2,3},{3,4},{4,5},{5,6},{6,7},{7,8},{8,9},{9,10... | collective-permute-start | bytes 196616 | tf_op jit(solution)/shard_map/ppermute | solution.py:218
  59.4 2.2 %collective-permute-start.14 = (bf16[128,256]{1,0:T(8,128)(2,1)S(1)}, bf16[128,256]{1,0:T(8,128)(2,1)S(1)}, u32[]{:S(2)}, u32[]{:S(2)}) collective-permute-start(bf16[128,256]{1,0:T(8,128)(2,1)S(1)} %bitcast.31), channel_id=1, source_target_pairs={{16,0},{17,1},{0,2},{1,3},{2,4},{3,5},{4,6},{5,7},{6,8},{7,9},{8,1... | collective-permute-start | bytes 196616 | tf_op jit(solution)/shard_map/ppermute | solution.py:218
  61.6 0.0 copy-done.2
  61.6 0.7 %bitcast_and_fusion.3 = (pred[4]{0:T(512)(128)(4,1)S(1)}, pred[4]{0:T(512)(128)(4,1)S(1)}, pred[4]{0:T(512)(128)(4,1)S(1)}, pred[4]{0:T(512)(128)(4,1)S(1)}) fusion(s32[1,4]{1,0:T(1,128)S(1)} %copy-done.2, s32[]{:T(128)S(6)} %add.41, s32[]{:T(128)} %bitcast, s32[]{:T(128)S(6)} %add.44, s32[]{:T(128)S(6)} %add.46, s32[]{:T(128)S(6)} %add.45), kind=kLoop, calls=%fused_computation.15 | loop fusion | flops 36 | bytes 52 | tf_op jit(solution)/shard_map/and | solution.py:283
  62.3 0.0 collective-permute-done.17
  62.4 0.0 collective-permute-done.16
  62.4 0.0 collective-permute-done.15
  62.4 3.7 %collective-permute-done.14 = bf16[128,256]{1,0:T(8,128)(2,1)S(1)} collective-permute-done((bf16[128,256]{1,0:T(8,128)(2,1)S(1)}, bf16[128,256]{1,0:T(8,128)(2,1)S(1)}, u32[]{:S(2)}, u32[]{:S(2)}) %collective-permute-start.14) | collective-permute-done | bytes 65568 | tf_op jit(solution)/shard_map/ppermute | solution.py:218
  66.1 0.9 %select_select_fusion = f32[1,1,4,128,256]{4,3,2,1,0:T(8,128)} fusion(f32[128,256]{1,0:T(8,128)S(1)} %convert_element_type.19, f32[128,256]{1,0:T(8,128)S(1)} %convert_element_type.18, f32[128,256]{1,0:T(8,128)S(1)} %convert_element_type.17, f32[128,256]{1,0:T(8,128)S(1)} %convert_element_type.16, pred[4]{0:T(512)(128)(4,1)S(1)} %get-tuple-element.63, ...), kind=kLoop, calls=%fused_computation.1 | loop fusion | flops 524288 | bytes 1048592 | tf_op jit(solution)/shard_map/jit(_where)/select_n | solution.py:284
  (14 shorter events, 0.2 us)
Async XLA Ops:
  0.0 9.0 %collective-permute-start.4 = (bf16[8,16,8192]{2,1,0:T(8,128)(2,1)}, bf16[8,16,8192]{2,1,0:T(8,128)(2,1)}, u32[]{:S(2)}, u32[]{:S(2)}) collective-permute-start(bf16[8,16,8192]{2,1,0:T(8,128)(2,1)} %own.1), channel_id=1, source_target_pairs={{0,16},{16,0},{32,48},{48,32},{64,80},{80,64},{96,112},{112,96},{1... | collective-permute-start | bytes 6291464 | tf_op jit(solution)/shard_map/ppermute | solution.py:228
  0.0 1.6 %copy-start = (bf16[8,16,8192]{2,1,0:T(8,128)(2,1)S(1)}, bf16[8,16,8192]{2,1,0:T(8,128)(2,1)}, u32[]{:S(2)}) copy-start(bf16[8,16,8192]{2,1,0:T(8,128)(2,1)} %own.1) | copy-start | bytes 6291460
  1.6 7.4 %copy-start.1 = (bf16[8,16,8192]{2,1,0:T(8,128)(2,1)S(1)}, bf16[8,16,8192]{2,1,0:T(8,128)(2,1)}, u32[]{:S(2)}) copy-start(bf16[8,16,8192]{2,1,0:T(8,128)(2,1)} %own.1) | copy-start | bytes 6291460
  2.3 12.5 %collective-permute-start = (bf16[8,8192]{1,0:T(8,128)(2,1)S(1)}, bf16[8,8192]{1,0:T(8,128)(2,1)S(1)}, u32[]{:S(2)}, u32[]{:S(2)}) collective-permute-start(bf16[8,8192]{1,0:T(8,128)(2,1)S(1)} %whiten_source.1), channel_id=1, source_target_pairs={{0,1},{1,2},{2,3},{3,4},{4,5},{5,6},{6,7},{7,8},{8,9},{9,10},{10,1... | collective-permute-start | bytes 393224 | tf_op jit(solution)/shard_map/ppermute | solution.py:218
  3.8 11.0 %collective-permute-start.1 = (bf16[8,8192]{1,0:T(8,128)(2,1)S(1)}, bf16[8,8192]{1,0:T(8,128)(2,1)S(1)}, u32[]{:S(2)}, u32[]{:S(2)}) collective-permute-start(bf16[8,8192]{1,0:T(8,128)(2,1)S(1)} %whiten_source.1), channel_id=1, source_target_pairs={{0,2},{1,3},{2,4},{3,5},{4,6},{5,7},{6,8},{7,9},{8,10},{9,11},{10,... | collective-permute-start | bytes 393224 | tf_op jit(solution)/shard_map/ppermute | solution.py:218
  6.3 8.5 %collective-permute-start.2 = (bf16[8,8192]{1,0:T(8,128)(2,1)S(1)}, bf16[8,8192]{1,0:T(8,128)(2,1)S(1)}, u32[]{:S(2)}, u32[]{:S(2)}) collective-permute-start(bf16[8,8192]{1,0:T(8,128)(2,1)S(1)} %whiten_source.1), channel_id=1, source_target_pairs={{0,16},{1,0},{2,1},{3,2},{4,3},{5,4},{6,5},{7,6},{8,7},{9,8},{10,9... | collective-permute-start | bytes 393224 | tf_op jit(solution)/shard_map/ppermute | solution.py:218
  7.1 8.8 %collective-permute-start.3 = (bf16[8,8192]{1,0:T(8,128)(2,1)S(1)}, bf16[8,8192]{1,0:T(8,128)(2,1)S(1)}, u32[]{:S(2)}, u32[]{:S(2)}) collective-permute-start(bf16[8,8192]{1,0:T(8,128)(2,1)S(1)} %whiten_source.1), channel_id=1, source_target_pairs={{0,16},{1,17},{2,0},{3,1},{4,2},{5,3},{6,4},{7,5},{8,6},{9,7},{10,... | collective-permute-start | bytes 393224 | tf_op jit(solution)/shard_map/ppermute | solution.py:218
  15.9 10.3 %collective-permute-start.5 = (bf16[2,8,8192]{2,1,0:T(8,128)(2,1)S(1)}, bf16[2,8,8192]{2,1,0:T(8,128)(2,1)S(1)}, u32[]{:S(2)}, u32[]{:S(2)}) collective-permute-start(bf16[2,8,8192]{2,1,0:T(8,128)(2,1)S(1)} %pad_maximum_fusion.refs_2_), channel_id=1, source_target_pairs={{0,32},{16,48},{32,64},{48,80},{64,96},{80,112},{96,0},{112,16},{1... | collective-permute-start | bytes 786440 | tf_op jit(solution)/shard_map/ppermute | solution.py:223
  17.6 8.7 %collective-permute-start.6 = (bf16[2,8,8192]{2,1,0:T(8,128)(2,1)S(1)}, bf16[2,8,8192]{2,1,0:T(8,128)(2,1)S(1)}, u32[]{:S(2)}, u32[]{:S(2)}) collective-permute-start(bf16[2,8,8192]{2,1,0:T(8,128)(2,1)S(1)} %pad_maximum_fusion.refs_2_), channel_id=1, source_target_pairs={{0,96},{16,112},{32,0},{48,16},{64,32},{80,48},{96,64},{112,80},{1... | collective-permute-start | bytes 786440 | tf_op jit(solution)/shard_map/ppermute | solution.py:223
  22.9 8.5 %collective-permute-start.7 = (bf16[2,8,8192]{2,1,0:T(8,128)(2,1)S(1)}, bf16[2,8,8192]{2,1,0:T(8,128)(2,1)S(1)}, u32[]{:S(2)}, u32[]{:S(2)}) collective-permute-start(bf16[2,8,8192]{2,1,0:T(8,128)(2,1)S(1)} %pad_maximum_fusion.1.refs_2_), channel_id=1, source_target_pairs={{0,32},{16,48},{32,64},{48,80},{64,96},{80,112},{96,0},{112,16},{1... | collective-permute-start | bytes 786440 | tf_op jit(solution)/shard_map/ppermute | solution.py:223
  23.4 8.1 %collective-permute-start.8 = (bf16[2,8,8192]{2,1,0:T(8,128)(2,1)S(1)}, bf16[2,8,8192]{2,1,0:T(8,128)(2,1)S(1)}, u32[]{:S(2)}, u32[]{:S(2)}) collective-permute-start(bf16[2,8,8192]{2,1,0:T(8,128)(2,1)S(1)} %pad_maximum_fusion.1.refs_2_), channel_id=1, source_target_pairs={{0,96},{16,112},{32,0},{48,16},{64,32},{80,48},{96,64},{112,80},{1... | collective-permute-start | bytes 786440 | tf_op jit(solution)/shard_map/ppermute | solution.py:223
  31.4 8.5 %collective-permute-start.9 = (bf16[2,8,8192]{2,1,0:T(8,128)(2,1)S(1)}, bf16[2,8,8192]{2,1,0:T(8,128)(2,1)S(1)}, u32[]{:S(2)}, u32[]{:S(2)}) collective-permute-start(bf16[2,8,8192]{2,1,0:T(8,128)(2,1)S(1)} %collective-permute-done.5.refs_2_), channel_id=1, source_target_pairs={{0,32},{16,48},{32,64},{48,80},{64,96},{80,112},{96,0},{112,16},{1... | collective-permute-start | bytes 786440 | tf_op jit(solution)/shard_map/ppermute | solution.py:223
  32.1 7.8 %collective-permute-start.10 = (bf16[2,8,8192]{2,1,0:T(8,128)(2,1)S(1)}, bf16[2,8,8192]{2,1,0:T(8,128)(2,1)S(1)}, u32[]{:S(2)}, u32[]{:S(2)}) collective-permute-start(bf16[2,8,8192]{2,1,0:T(8,128)(2,1)S(1)} %collective-permute-done.8.refs_3_), channel_id=1, source_target_pairs={{0,96},{16,112},{32,0},{48,16},{64,32},{80,48},{96,64},{112,80},{1... | collective-permute-start | bytes 786440 | tf_op jit(solution)/shard_map/ppermute | solution.py:223
  45.1 7.6 %collective-permute-start.13 = (bf16[4,32,256]{2,1,0:T(8,128)(2,1)S(1)}, bf16[4,32,256]{2,1,0:T(8,128)(2,1)S(1)}, u32[]{:S(2)}, u32[]{:S(2)}) collective-permute-start(bf16[4,32,256]{2,1,0:T(8,128)(2,1)S(1)} %pad_maximum_fusion.4), channel_id=1, source_target_pairs={{0,96},{16,112},{32,0},{48,16},{64,32},{80,48},{96,64},{112,80},{1... | collective-permute-start | bytes 196616 | tf_op jit(solution)/shard_map/ppermute | solution.py:223
  47.6 5.9 %collective-permute-start.12 = (bf16[4,32,256]{2,1,0:T(8,128)(2,1)S(1)}, bf16[4,32,256]{2,1,0:T(8,128)(2,1)S(1)}, u32[]{:S(2)}, u32[]{:S(2)}) collective-permute-start(bf16[4,32,256]{2,1,0:T(8,128)(2,1)S(1)} %correlate_4.5), channel_id=1, source_target_pairs={{0,64},{16,80},{32,96},{48,112},{64,0},{80,16},{96,32},{112,48},{1... | collective-permute-start | bytes 196616 | tf_op jit(solution)/shard_map/ppermute | solution.py:223
  47.6 14.0 %copy-start.2 = (s32[1,4]{1,0:T(1,128)S(1)}, s32[1,4]{1,0:T(1,128)}, u32[]{:S(2)}) copy-start(s32[1,4]{1,0:T(1,128)} %param.5) | copy-start | bytes 52
  47.6 6.2 %collective-permute-start.11 = (bf16[4,32,256]{2,1,0:T(8,128)(2,1)S(1)}, bf16[4,32,256]{2,1,0:T(8,128)(2,1)S(1)}, u32[]{:S(2)}, u32[]{:S(2)}) collective-permute-start(bf16[4,32,256]{2,1,0:T(8,128)(2,1)S(1)} %pad_maximum_fusion.3), channel_id=1, source_target_pairs={{0,32},{16,48},{32,64},{48,80},{64,96},{80,112},{96,0},{112,16},{1... | collective-permute-start | bytes 196616 | tf_op jit(solution)/shard_map/ppermute | solution.py:223
  54.5 7.8 %collective-permute-start.17 = (bf16[128,256]{1,0:T(8,128)(2,1)S(1)}, bf16[128,256]{1,0:T(8,128)(2,1)S(1)}, u32[]{:S(2)}, u32[]{:S(2)}) collective-permute-start(bf16[128,256]{1,0:T(8,128)(2,1)S(1)} %bitcast.36), channel_id=1, source_target_pairs={{1,0},{2,1},{3,2},{4,3},{5,4},{6,5},{7,6},{8,7},{9,8},{10,9},{11,1... | collective-permute-start | bytes 196616 | tf_op jit(solution)/shard_map/ppermute | solution.py:218
  55.7 6.7 %collective-permute-start.16 = (bf16[128,256]{1,0:T(8,128)(2,1)S(1)}, bf16[128,256]{1,0:T(8,128)(2,1)S(1)}, u32[]{:S(2)}, u32[]{:S(2)}) collective-permute-start(bf16[128,256]{1,0:T(8,128)(2,1)S(1)} %bitcast.33), channel_id=1, source_target_pairs={{2,0},{3,1},{4,2},{5,3},{6,4},{7,5},{8,6},{9,7},{10,8},{11,9},{12,... | collective-permute-start | bytes 196616 | tf_op jit(solution)/shard_map/ppermute | solution.py:218
  56.9 5.5 %collective-permute-start.15 = (bf16[128,256]{1,0:T(8,128)(2,1)S(1)}, bf16[128,256]{1,0:T(8,128)(2,1)S(1)}, u32[]{:S(2)}, u32[]{:S(2)}) collective-permute-start(bf16[128,256]{1,0:T(8,128)(2,1)S(1)} %bitcast.32), channel_id=1, source_target_pairs={{16,0},{0,1},{1,2},{2,3},{3,4},{4,5},{5,6},{6,7},{7,8},{8,9},{9,10... | collective-permute-start | bytes 196616 | tf_op jit(solution)/shard_map/ppermute | solution.py:218
  59.4 6.7 %collective-permute-start.14 = (bf16[128,256]{1,0:T(8,128)(2,1)S(1)}, bf16[128,256]{1,0:T(8,128)(2,1)S(1)}, u32[]{:S(2)}, u32[]{:S(2)}) collective-permute-start(bf16[128,256]{1,0:T(8,128)(2,1)S(1)} %bitcast.31), channel_id=1, source_target_pairs={{16,0},{17,1},{0,2},{1,3},{2,4},{3,5},{4,6},{5,7},{6,8},{7,9},{8,1... | collective-permute-start | bytes 196616 | tf_op jit(solution)/shard_map/ppermute | solution.py:218

commit v8 on v7

--- a/solution.py
+++ b/solution.py
@@ -250,11 +250,11 @@
     up_second, down_second = chip_shift(second, 1), chip_shift(second, -1)
     own_first, up_first, down_first = lax.optimization_barrier((own_first, up_first, down_first))
     near_first = run([up_first, down_first])
-    near_first, up_first, up_second, down_second = lax.optimization_barrier(
-        (near_first, up_first, up_second, down_second)
-    )
-    far_first = chip_shift(up_first, 1)
-    far_second = chip_shift(down_second, -1)
+    near_first, down_first, up_second, down_second = lax.optimization_barrier(
+        (near_first, down_first, up_second, down_second)
+    )
+    far_first = chip_shift(down_first, -1)
+    far_second = chip_shift(up_second, 1)
     near_second = run([up_second, down_second])
     near_second, far_first, far_second = lax.optimization_barrier(
         (near_second, far_first, far_second)

time: 67.2 us -> 67.7 us (level)
  waiting for transfers between devices: 6.02 us -> 8.21 us
  starting transfers between devices: 26.9 us -> 24.9 us
    ppermute x9, waiting for transfers between devices: 1.21 us -> 3.96 us  [chip_shift(): lax.ppermute(block, 'win', [(i, (i + 2 * distance) % size) for i in range...]
    ppermute x9, starting transfers between devices: 13.8 us -> 11.7 us  [chip_shift(): lax.ppermute(block, 'win', [(i, (i + 2 * distance) % size) for i in range...]
  transfers between devices with their start and end apart: 18 -> 18, of which waited for: 4 -> 5; matrix products, arithmetic and copies ran while one was open for 1% -> 1% of each run, Pallas kernels for 36% -> 36%
where the time goes in v8:
time: 67.7 us; the launch traced here: 67.2 us
  Pallas kernels  29.2 us (43%)
  starting transfers between devices  24.9 us (37%)
  waiting for transfers between devices  8.21 us (12%)
  local copies, waits for them, and re-layouts  2.2 us (3%)
  other arithmetic  1.81 us (3%)
  between operations  0.92 us (1%)
    pallas_call x5, Pallas kernels, correlate(): pl.pallas_call(functools.partial(correlate_kernel, groups, scale), in_spe...  22.8 us
    ppermute x8, starting transfers between devices, route_swap(): lax.ppermute(block, ('win', 'chan'), [(j, i) if back else (i, j) for i, j...  13.1 us
    ppermute x9, starting transfers between devices, chip_shift(): lax.ppermute(block, 'win', [(i, (i + 2 * distance) % size) for i in range...  11.7 us
    pallas_call x1, Pallas kernels, whiten_both(): pl.pallas_call(whiten_kernel, in_specs=[scalar] + [pl.BlockSpec(memory_sp...  5.79 us
    ppermute x8, waiting for transfers between devices, route_swap(): lax.ppermute(block, ('win', 'chan'), [(j, i) if back else (i, j) for i, j...  4.25 us
    ppermute x9, waiting for transfers between devices, chip_shift(): lax.ppermute(block, 'win', [(i, (i + 2 * distance) % size) for i in range...  3.96 us
    unnamed x6, local copies, waits for them, and re-layouts  1.6 us
  transfers between devices with their start and end apart: 18, of which 5 were waited for; matrix products, arithmetic and copies ran while one was open for 1% of the time, Pallas kernels for 36%

profile of v8, /device:TPU:34, one launch (start us, length us, event | category | flops | bytes accessed | tf_op | source)
XLA Modules:
  0.0 67.2 jit_solution(15566925054325391163)
XLA Ops:
  0.0 0.0 collective-permute-start.4
  0.0 0.0 copy-start
  0.0 1.6 %copy-done = bf16[8,16,8192]{2,1,0:T(8,128)(2,1)S(1)} copy-done((bf16[8,16,8192]{2,1,0:T(8,128)(2,1)S(1)}, bf16[8,16,8192]{2,1,0:T(8,128)(2,1)}, u32[]{:S(2)}) %copy-start) | copy-done | bytes 2097176
  1.6 0.0 copy-start.1
  1.6 0.7 whiten_source.1
  2.3 1.6 %collective-permute-start = (bf16[8,8192]{1,0:T(8,128)(2,1)S(1)}, bf16[8,8192]{1,0:T(8,128)(2,1)S(1)}, u32[]{:S(2)}, u32[]{:S(2)}) collective-permute-start(bf16[8,8192]{1,0:T(8,128)(2,1)S(1)} %whiten_source.1), channel_id=1, source_target_pairs={{0,1},{1,2},{2,3},{3,4},{4,5},{5,6},{6,7},{7,8},{8,9},{9,10},{10,1... | collective-permute-start | bytes 393224 | tf_op jit(solution)/shard_map/ppermute | solution.py:218
  3.8 2.5 %collective-permute-start.1 = (bf16[8,8192]{1,0:T(8,128)(2,1)S(1)}, bf16[8,8192]{1,0:T(8,128)(2,1)S(1)}, u32[]{:S(2)}, u32[]{:S(2)}) collective-permute-start(bf16[8,8192]{1,0:T(8,128)(2,1)S(1)} %whiten_source.1), channel_id=1, source_target_pairs={{0,2},{1,3},{2,4},{3,5},{4,6},{5,7},{6,8},{7,9},{8,10},{9,11},{10,... | collective-permute-start | bytes 393224 | tf_op jit(solution)/shard_map/ppermute | solution.py:218
  6.3 0.8 %collective-permute-start.2 = (bf16[8,8192]{1,0:T(8,128)(2,1)S(1)}, bf16[8,8192]{1,0:T(8,128)(2,1)S(1)}, u32[]{:S(2)}, u32[]{:S(2)}) collective-permute-start(bf16[8,8192]{1,0:T(8,128)(2,1)S(1)} %whiten_source.1), channel_id=1, source_target_pairs={{0,16},{1,0},{2,1},{3,2},{4,3},{5,4},{6,5},{7,6},{8,7},{9,8},{10,9... | collective-permute-start | bytes 393224 | tf_op jit(solution)/shard_map/ppermute | solution.py:218
  7.1 1.2 %collective-permute-start.3 = (bf16[8,8192]{1,0:T(8,128)(2,1)S(1)}, bf16[8,8192]{1,0:T(8,128)(2,1)S(1)}, u32[]{:S(2)}, u32[]{:S(2)}) collective-permute-start(bf16[8,8192]{1,0:T(8,128)(2,1)S(1)} %whiten_source.1), channel_id=1, source_target_pairs={{0,16},{1,17},{2,0},{3,1},{4,2},{5,3},{6,4},{7,5},{8,6},{9,7},{10,... | collective-permute-start | bytes 393224 | tf_op jit(solution)/shard_map/ppermute | solution.py:218
  9.0 0.0 collective-permute-done.4.sibling
  9.0 0.0 copy-done.1
  9.0 5.8 %whiten_both.1 = (bf16[8,16,8192]{2,1,0:T(8,128)(2,1)S(1)}, bf16[8,16,8192]{2,1,0:T(8,128)(2,1)S(1)}, s32[1]{0:T(128)}) custom-call(s32[1]{0:T(128)S(6)} %copy.5.flag, bf16[8,16,8192]{2,1,0:T(8,128)(2,1)S(1)} %copy-done.1, bf16[8,16,8192]{2,1,0:T(8,128)(2,1)} %collective-permute-done.4.sibling), custom_call_target="tpu_custom_call" | custom-call | flops 1000000000 | bytes 8388608 | tf_op jit(solution)/shard_map/whiten_both/pallas_call | solution.py:115
  14.8 0.0 collective-permute-done
  14.8 0.0 collective-permute-done.1
  14.8 0.0 collective-permute-done.2
  14.8 1.1 %collective-permute-done.3 = bf16[8,8192]{1,0:T(8,128)(2,1)S(1)} collective-permute-done((bf16[8,8192]{1,0:T(8,128)(2,1)S(1)}, bf16[8,8192]{1,0:T(8,128)(2,1)S(1)}, u32[]{:S(2)}, u32[]{:S(2)}) %collective-permute-start.3) | collective-permute-done | bytes 131104 | tf_op jit(solution)/shard_map/ppermute | solution.py:218
  15.9 1.6 %collective-permute-start.5 = (bf16[2,8,8192]{2,1,0:T(8,128)(2,1)S(1)}, bf16[2,8,8192]{2,1,0:T(8,128)(2,1)S(1)}, u32[]{:S(2)}, u32[]{:S(2)}) collective-permute-start(bf16[2,8,8192]{2,1,0:T(8,128)(2,1)S(1)} %pad_maximum_fusion.refs_2_), channel_id=1, source_target_pairs={{0,32},{16,48},{32,64},{48,80},{64,96},{80,112},{96,0},{112,16},{1... | collective-permute-start | bytes 786440 | tf_op jit(solution)/shard_map/ppermute | solution.py:223
  17.6 1.7 %collective-permute-start.6 = (bf16[2,8,8192]{2,1,0:T(8,128)(2,1)S(1)}, bf16[2,8,8192]{2,1,0:T(8,128)(2,1)S(1)}, u32[]{:S(2)}, u32[]{:S(2)}) collective-permute-start(bf16[2,8,8192]{2,1,0:T(8,128)(2,1)S(1)} %pad_maximum_fusion.refs_2_), channel_id=1, source_target_pairs={{0,96},{16,112},{32,0},{48,16},{64,32},{80,48},{96,64},{112,80},{1... | collective-permute-start | bytes 786440 | tf_op jit(solution)/shard_map/ppermute | solution.py:223
  19.3 3.7 %correlate_2.2 = bf16[2,32,256]{2,1,0:T(8,128)(2,1)S(1)} custom-call(s32[1]{0:T(128)} %bitcast.2.parity, bf16[8,16,8192]{2,1,0:T(8,128)(2,1)S(1)} %get-tuple-element.31.refs_0_, bf16[8,16,8192]{2,1,0:T(8,128)(2,1)S(1)} %get-tuple-element.32.refs_1_, bf16[2,8,8192]{2,1,0:T(8,128)(2,1)S(1)} %pad_maximum_fusion.refs_2_, ...), custom_call_target="tpu_custom_call" | custom-call | flops 2000000000 | bytes 8388608 | tf_op jit(solution)/shard_map/correlate_2/pallas_call | solution.py:187
  22.9 0.4 collective-permute-start.7
  23.4 2.9 %collective-permute-start.8 = (bf16[2,8,8192]{2,1,0:T(8,128)(2,1)S(1)}, bf16[2,8,8192]{2,1,0:T(8,128)(2,1)S(1)}, u32[]{:S(2)}, u32[]{:S(2)}) collective-permute-start(bf16[2,8,8192]{2,1,0:T(8,128)(2,1)S(1)} %pad_maximum_fusion.1.refs_2_), channel_id=1, source_target_pairs={{0,96},{16,112},{32,0},{48,16},{64,32},{80,48},{96,64},{112,80},{1... | collective-permute-start | bytes 786440 | tf_op jit(solution)/shard_map/ppermute | solution.py:223
  26.2 0.0 collective-permute-done.5.refs_2_
  26.3 0.0 collective-permute-done.6.refs_3_
  26.3 5.2 %correlate_4.3 = bf16[4,32,256]{2,1,0:T(8,128)(2,1)S(1)} custom-call(s32[1]{0:T(128)} %bitcast.2.parity, bf16[8,16,8192]{2,1,0:T(8,128)(2,1)S(1)} %get-tuple-element.31.refs_0_, bf16[8,16,8192]{2,1,0:T(8,128)(2,1)S(1)} %get-tuple-element.32.refs_1_, bf16[2,8,8192]{2,1,0:T(8,128)(2,1)S(1)} %collective-permute-done.5.refs_2_, ...), custom_call_target="tpu_custom_call" | custom-call | flops 4000000000 | bytes 8388608 | tf_op jit(solution)/shard_map/correlate_4/pallas_call | solution.py:187
  31.4 0.0 collective-permute-done.7.refs_2_
  31.4 0.0 collective-permute-done.8.refs_3_
  31.4 3.0 %collective-permute-start.9 = (bf16[2,8,8192]{2,1,0:T(8,128)(2,1)S(1)}, bf16[2,8,8192]{2,1,0:T(8,128)(2,1)S(1)}, u32[]{:S(2)}, u32[]{:S(2)}) collective-permute-start(bf16[2,8,8192]{2,1,0:T(8,128)(2,1)S(1)} %collective-permute-done.6.refs_3_), channel_id=1, source_target_pairs={{0,96},{16,112},{32,0},{48,16},{64,32},{80,48},{96,64},{112,80},{1... | collective-permute-start | bytes 786440 | tf_op jit(solution)/shard_map/ppermute | solution.py:223
  34.4 0.0 collective-permute-start.10
  34.4 5.1 %correlate_4.4 = bf16[4,32,256]{2,1,0:T(8,128)(2,1)S(1)} custom-call(s32[1]{0:T(128)} %bitcast.2.parity, bf16[8,16,8192]{2,1,0:T(8,128)(2,1)S(1)} %get-tuple-element.31.refs_0_, bf16[8,16,8192]{2,1,0:T(8,128)(2,1)S(1)} %get-tuple-element.32.refs_1_, bf16[2,8,8192]{2,1,0:T(8,128)(2,1)S(1)} %collective-permute-done.7.refs_2_, ...), custom_call_target="tpu_custom_call" | custom-call | flops 4000000000 | bytes 8388608 | tf_op jit(solution)/shard_map/correlate_4/pallas_call | solution.py:187
  39.6 0.0 collective-permute-done.9.refs_2_
  39.6 2.4 %collective-permute-done.10.refs_3_ = bf16[2,8,8192]{2,1,0:T(8,128)(2,1)S(1)} collective-permute-done((bf16[2,8,8192]{2,1,0:T(8,128)(2,1)S(1)}, bf16[2,8,8192]{2,1,0:T(8,128)(2,1)S(1)}, u32[]{:S(2)}, u32[]{:S(2)}) %collective-permute-start.10) | collective-permute-done | bytes 262176 | tf_op jit(solution)/shard_map/ppermute | solution.py:223
  42.0 5.1 %correlate_4.5 = bf16[4,32,256]{2,1,0:T(8,128)(2,1)S(1)} custom-call(s32[1]{0:T(128)} %bitcast.2.parity, bf16[8,16,8192]{2,1,0:T(8,128)(2,1)S(1)} %get-tuple-element.31.refs_0_, bf16[8,16,8192]{2,1,0:T(8,128)(2,1)S(1)} %get-tuple-element.32.refs_1_, bf16[2,8,8192]{2,1,0:T(8,128)(2,1)S(1)} %collective-permute-done.9.refs_2_, ...), custom_call_target="tpu_custom_call" | custom-call | flops 4000000000 | bytes 8388608 | tf_op jit(solution)/shard_map/correlate_4/pallas_call | solution.py:187
  47.2 0.9 %collective-permute-start.13 = (bf16[4,32,256]{2,1,0:T(8,128)(2,1)S(1)}, bf16[4,32,256]{2,1,0:T(8,128)(2,1)S(1)}, u32[]{:S(2)}, u32[]{:S(2)}) collective-permute-start(bf16[4,32,256]{2,1,0:T(8,128)(2,1)S(1)} %pad_maximum_fusion.4), channel_id=1, source_target_pairs={{0,96},{16,112},{32,0},{48,16},{64,32},{80,48},{96,64},{112,80},{1... | collective-permute-start | bytes 196616 | tf_op jit(solution)/shard_map/ppermute | solution.py:223
  48.1 0.0 collective-permute-start.12
  48.1 0.0 copy-start.2
  48.1 1.2 %collective-permute-start.11 = (bf16[4,32,256]{2,1,0:T(8,128)(2,1)S(1)}, bf16[4,32,256]{2,1,0:T(8,128)(2,1)S(1)}, u32[]{:S(2)}, u32[]{:S(2)}) collective-permute-start(bf16[4,32,256]{2,1,0:T(8,128)(2,1)S(1)} %pad_maximum_fusion.3), channel_id=1, source_target_pairs={{0,32},{16,48},{32,64},{48,80},{64,96},{80,112},{96,0},{112,16},{1... | collective-permute-start | bytes 196616 | tf_op jit(solution)/shard_map/ppermute | solution.py:223
  49.4 3.6 %correlate_2.3 = bf16[2,32,256]{2,1,0:T(8,128)(2,1)S(1)} custom-call(s32[1]{0:T(128)} %bitcast.2.parity, bf16[8,16,8192]{2,1,0:T(8,128)(2,1)S(1)} %get-tuple-element.31.refs_0_, bf16[8,16,8192]{2,1,0:T(8,128)(2,1)S(1)} %get-tuple-element.32.refs_1_, bf16[2,8,8192]{2,1,0:T(8,128)(2,1)S(1)} %pad_maximum_fusion.1.refs_2_, ...), custom_call_target="tpu_custom_call" | custom-call | flops 2000000000 | bytes 8388608 | tf_op jit(solution)/shard_map/correlate_2/pallas_call | solution.py:187
  53.0 0.0 collective-permute-done.13
  53.0 0.8 %collective-permute-done.12 = bf16[4,32,256]{2,1,0:T(8,128)(2,1)S(1)} collective-permute-done((bf16[4,32,256]{2,1,0:T(8,128)(2,1)S(1)}, bf16[4,32,256]{2,1,0:T(8,128)(2,1)S(1)}, u32[]{:S(2)}, u32[]{:S(2)}) %collective-permute-start.12) | collective-permute-done | bytes 65568 | tf_op jit(solution)/shard_map/ppermute | solution.py:223
  53.9 0.7 %collective-permute-done.11 = bf16[4,32,256]{2,1,0:T(8,128)(2,1)S(1)} collective-permute-done((bf16[4,32,256]{2,1,0:T(8,128)(2,1)S(1)}, bf16[4,32,256]{2,1,0:T(8,128)(2,1)S(1)}, u32[]{:S(2)}, u32[]{:S(2)}) %collective-permute-start.11) | collective-permute-done | bytes 65568 | tf_op jit(solution)/shard_map/ppermute | solution.py:223
  54.6 0.6 gather_fusion
  55.2 1.1 %collective-permute-start.17 = (bf16[128,256]{1,0:T(8,128)(2,1)S(1)}, bf16[128,256]{1,0:T(8,128)(2,1)S(1)}, u32[]{:S(2)}, u32[]{:S(2)}) collective-permute-start(bf16[128,256]{1,0:T(8,128)(2,1)S(1)} %bitcast.36), channel_id=1, source_target_pairs={{1,0},{2,1},{3,2},{4,3},{5,4},{6,5},{7,6},{8,7},{9,8},{10,9},{11,1... | collective-permute-start | bytes 196616 | tf_op jit(solution)/shard_map/ppermute | solution.py:218
  56.3 0.7 %collective-permute-start.16 = (bf16[128,256]{1,0:T(8,128)(2,1)S(1)}, bf16[128,256]{1,0:T(8,128)(2,1)S(1)}, u32[]{:S(2)}, u32[]{:S(2)}) collective-permute-start(bf16[128,256]{1,0:T(8,128)(2,1)S(1)} %bitcast.33), channel_id=1, source_target_pairs={{2,0},{3,1},{4,2},{5,3},{6,4},{7,5},{8,6},{9,7},{10,8},{11,9},{12,... | collective-permute-start | bytes 196616 | tf_op jit(solution)/shard_map/ppermute | solution.py:218
  57.0 2.5 %collective-permute-start.15 = (bf16[128,256]{1,0:T(8,128)(2,1)S(1)}, bf16[128,256]{1,0:T(8,128)(2,1)S(1)}, u32[]{:S(2)}, u32[]{:S(2)}) collective-permute-start(bf16[128,256]{1,0:T(8,128)(2,1)S(1)} %bitcast.32), channel_id=1, source_target_pairs={{16,0},{0,1},{1,2},{2,3},{3,4},{4,5},{5,6},{6,7},{7,8},{8,9},{9,10... | collective-permute-start | bytes 196616 | tf_op jit(solution)/shard_map/ppermute | solution.py:218
  59.6 2.7 %collective-permute-start.14 = (bf16[128,256]{1,0:T(8,128)(2,1)S(1)}, bf16[128,256]{1,0:T(8,128)(2,1)S(1)}, u32[]{:S(2)}, u32[]{:S(2)}) collective-permute-start(bf16[128,256]{1,0:T(8,128)(2,1)S(1)} %bitcast.31), channel_id=1, source_target_pairs={{16,0},{17,1},{0,2},{1,3},{2,4},{3,5},{4,6},{5,7},{6,8},{7,9},{8,1... | collective-permute-start | bytes 196616 | tf_op jit(solution)/shard_map/ppermute | solution.py:218
  62.3 0.0 copy-done.2
  62.3 0.7 %bitcast_and_fusion.3 = (pred[4]{0:T(512)(128)(4,1)S(1)}, pred[4]{0:T(512)(128)(4,1)S(1)}, pred[4]{0:T(512)(128)(4,1)S(1)}, pred[4]{0:T(512)(128)(4,1)S(1)}) fusion(s32[1,4]{1,0:T(1,128)S(1)} %copy-done.2, s32[]{:T(128)S(6)} %add.41, s32[]{:T(128)} %bitcast, s32[]{:T(128)S(6)} %add.44, s32[]{:T(128)S(6)} %add.46, s32[]{:T(128)S(6)} %add.45), kind=kLoop, calls=%fused_computation.15 | loop fusion | flops 36 | bytes 52 | tf_op jit(solution)/shard_map/and | solution.py:283
  63.0 0.0 collective-permute-done.17
  63.1 0.0 collective-permute-done.16
  63.1 0.0 collective-permute-done.15
  63.1 3.1 %collective-permute-done.14 = bf16[128,256]{1,0:T(8,128)(2,1)S(1)} collective-permute-done((bf16[128,256]{1,0:T(8,128)(2,1)S(1)}, bf16[128,256]{1,0:T(8,128)(2,1)S(1)}, u32[]{:S(2)}, u32[]{:S(2)}) %collective-permute-start.14) | collective-permute-done | bytes 65568 | tf_op jit(solution)/shard_map/ppermute | solution.py:218
  66.3 0.9 %select_select_fusion = f32[1,1,4,128,256]{4,3,2,1,0:T(8,128)} fusion(f32[128,256]{1,0:T(8,128)S(1)} %convert_element_type.19, f32[128,256]{1,0:T(8,128)S(1)} %convert_element_type.18, f32[128,256]{1,0:T(8,128)S(1)} %convert_element_type.17, f32[128,256]{1,0:T(8,128)S(1)} %convert_element_type.16, pred[4]{0:T(512)(128)(4,1)S(1)} %get-tuple-element.63, ...), kind=kLoop, calls=%fused_computation.1 | loop fusion | flops 524288 | bytes 1048592 | tf_op jit(solution)/shard_map/jit(_where)/select_n | solution.py:284
  (14 shorter events, 0.2 us)
Async XLA Ops:
  0.0 9.0 %collective-permute-start.4 = (bf16[8,16,8192]{2,1,0:T(8,128)(2,1)}, bf16[8,16,8192]{2,1,0:T(8,128)(2,1)}, u32[]{:S(2)}, u32[]{:S(2)}) collective-permute-start(bf16[8,16,8192]{2,1,0:T(8,128)(2,1)} %own.1), channel_id=1, source_target_pairs={{0,16},{16,0},{32,48},{48,32},{64,80},{80,64},{96,112},{112,96},{1... | collective-permute-start | bytes 6291464 | tf_op jit(solution)/shard_map/ppermute | solution.py:228
  0.0 1.6 %copy-start = (bf16[8,16,8192]{2,1,0:T(8,128)(2,1)S(1)}, bf16[8,16,8192]{2,1,0:T(8,128)(2,1)}, u32[]{:S(2)}) copy-start(bf16[8,16,8192]{2,1,0:T(8,128)(2,1)} %own.1) | copy-start | bytes 6291460
  1.6 7.4 %copy-start.1 = (bf16[8,16,8192]{2,1,0:T(8,128)(2,1)S(1)}, bf16[8,16,8192]{2,1,0:T(8,128)(2,1)}, u32[]{:S(2)}) copy-start(bf16[8,16,8192]{2,1,0:T(8,128)(2,1)} %own.1) | copy-start | bytes 6291460
  2.3 12.5 %collective-permute-start = (bf16[8,8192]{1,0:T(8,128)(2,1)S(1)}, bf16[8,8192]{1,0:T(8,128)(2,1)S(1)}, u32[]{:S(2)}, u32[]{:S(2)}) collective-permute-start(bf16[8,8192]{1,0:T(8,128)(2,1)S(1)} %whiten_source.1), channel_id=1, source_target_pairs={{0,1},{1,2},{2,3},{3,4},{4,5},{5,6},{6,7},{7,8},{8,9},{9,10},{10,1... | collective-permute-start | bytes 393224 | tf_op jit(solution)/shard_map/ppermute | solution.py:218
  3.8 11.0 %collective-permute-start.1 = (bf16[8,8192]{1,0:T(8,128)(2,1)S(1)}, bf16[8,8192]{1,0:T(8,128)(2,1)S(1)}, u32[]{:S(2)}, u32[]{:S(2)}) collective-permute-start(bf16[8,8192]{1,0:T(8,128)(2,1)S(1)} %whiten_source.1), channel_id=1, source_target_pairs={{0,2},{1,3},{2,4},{3,5},{4,6},{5,7},{6,8},{7,9},{8,10},{9,11},{10,... | collective-permute-start | bytes 393224 | tf_op jit(solution)/shard_map/ppermute | solution.py:218
  6.3 8.5 %collective-permute-start.2 = (bf16[8,8192]{1,0:T(8,128)(2,1)S(1)}, bf16[8,8192]{1,0:T(8,128)(2,1)S(1)}, u32[]{:S(2)}, u32[]{:S(2)}) collective-permute-start(bf16[8,8192]{1,0:T(8,128)(2,1)S(1)} %whiten_source.1), channel_id=1, source_target_pairs={{0,16},{1,0},{2,1},{3,2},{4,3},{5,4},{6,5},{7,6},{8,7},{9,8},{10,9... | collective-permute-start | bytes 393224 | tf_op jit(solution)/shard_map/ppermute | solution.py:218
  7.1 8.8 %collective-permute-start.3 = (bf16[8,8192]{1,0:T(8,128)(2,1)S(1)}, bf16[8,8192]{1,0:T(8,128)(2,1)S(1)}, u32[]{:S(2)}, u32[]{:S(2)}) collective-permute-start(bf16[8,8192]{1,0:T(8,128)(2,1)S(1)} %whiten_source.1), channel_id=1, source_target_pairs={{0,16},{1,17},{2,0},{3,1},{4,2},{5,3},{6,4},{7,5},{8,6},{9,7},{10,... | collective-permute-start | bytes 393224 | tf_op jit(solution)/shard_map/ppermute | solution.py:218
  15.9 10.3 %collective-permute-start.5 = (bf16[2,8,8192]{2,1,0:T(8,128)(2,1)S(1)}, bf16[2,8,8192]{2,1,0:T(8,128)(2,1)S(1)}, u32[]{:S(2)}, u32[]{:S(2)}) collective-permute-start(bf16[2,8,8192]{2,1,0:T(8,128)(2,1)S(1)} %pad_maximum_fusion.refs_2_), channel_id=1, source_target_pairs={{0,32},{16,48},{32,64},{48,80},{64,96},{80,112},{96,0},{112,16},{1... | collective-permute-start | bytes 786440 | tf_op jit(solution)/shard_map/ppermute | solution.py:223
  17.6 8.7 %collective-permute-start.6 = (bf16[2,8,8192]{2,1,0:T(8,128)(2,1)S(1)}, bf16[2,8,8192]{2,1,0:T(8,128)(2,1)S(1)}, u32[]{:S(2)}, u32[]{:S(2)}) collective-permute-start(bf16[2,8,8192]{2,1,0:T(8,128)(2,1)S(1)} %pad_maximum_fusion.refs_2_), channel_id=1, source_target_pairs={{0,96},{16,112},{32,0},{48,16},{64,32},{80,48},{96,64},{112,80},{1... | collective-permute-start | bytes 786440 | tf_op jit(solution)/shard_map/ppermute | solution.py:223
  22.9 8.5 %collective-permute-start.7 = (bf16[2,8,8192]{2,1,0:T(8,128)(2,1)S(1)}, bf16[2,8,8192]{2,1,0:T(8,128)(2,1)S(1)}, u32[]{:S(2)}, u32[]{:S(2)}) collective-permute-start(bf16[2,8,8192]{2,1,0:T(8,128)(2,1)S(1)} %pad_maximum_fusion.1.refs_2_), channel_id=1, source_target_pairs={{0,32},{16,48},{32,64},{48,80},{64,96},{80,112},{96,0},{112,16},{1... | collective-permute-start | bytes 786440 | tf_op jit(solution)/shard_map/ppermute | solution.py:223
  23.4 8.1 %collective-permute-start.8 = (bf16[2,8,8192]{2,1,0:T(8,128)(2,1)S(1)}, bf16[2,8,8192]{2,1,0:T(8,128)(2,1)S(1)}, u32[]{:S(2)}, u32[]{:S(2)}) collective-permute-start(bf16[2,8,8192]{2,1,0:T(8,128)(2,1)S(1)} %pad_maximum_fusion.1.refs_2_), channel_id=1, source_target_pairs={{0,96},{16,112},{32,0},{48,16},{64,32},{80,48},{96,64},{112,80},{1... | collective-permute-start | bytes 786440 | tf_op jit(solution)/shard_map/ppermute | solution.py:223
  31.4 8.1 %collective-permute-start.9 = (bf16[2,8,8192]{2,1,0:T(8,128)(2,1)S(1)}, bf16[2,8,8192]{2,1,0:T(8,128)(2,1)S(1)}, u32[]{:S(2)}, u32[]{:S(2)}) collective-permute-start(bf16[2,8,8192]{2,1,0:T(8,128)(2,1)S(1)} %collective-permute-done.6.refs_3_), channel_id=1, source_target_pairs={{0,96},{16,112},{32,0},{48,16},{64,32},{80,48},{96,64},{112,80},{1... | collective-permute-start | bytes 786440 | tf_op jit(solution)/shard_map/ppermute | solution.py:223
  34.4 7.6 %collective-permute-start.10 = (bf16[2,8,8192]{2,1,0:T(8,128)(2,1)S(1)}, bf16[2,8,8192]{2,1,0:T(8,128)(2,1)S(1)}, u32[]{:S(2)}, u32[]{:S(2)}) collective-permute-start(bf16[2,8,8192]{2,1,0:T(8,128)(2,1)S(1)} %collective-permute-done.7.refs_2_), channel_id=1, source_target_pairs={{0,32},{16,48},{32,64},{48,80},{64,96},{80,112},{96,0},{112,16},{1... | collective-permute-start | bytes 786440 | tf_op jit(solution)/shard_map/ppermute | solution.py:223
  47.2 5.9 %collective-permute-start.13 = (bf16[4,32,256]{2,1,0:T(8,128)(2,1)S(1)}, bf16[4,32,256]{2,1,0:T(8,128)(2,1)S(1)}, u32[]{:S(2)}, u32[]{:S(2)}) collective-permute-start(bf16[4,32,256]{2,1,0:T(8,128)(2,1)S(1)} %pad_maximum_fusion.4), channel_id=1, source_target_pairs={{0,96},{16,112},{32,0},{48,16},{64,32},{80,48},{96,64},{112,80},{1... | collective-permute-start | bytes 196616 | tf_op jit(solution)/shard_map/ppermute | solution.py:223
  48.1 5.8 %collective-permute-start.12 = (bf16[4,32,256]{2,1,0:T(8,128)(2,1)S(1)}, bf16[4,32,256]{2,1,0:T(8,128)(2,1)S(1)}, u32[]{:S(2)}, u32[]{:S(2)}) collective-permute-start(bf16[4,32,256]{2,1,0:T(8,128)(2,1)S(1)} %correlate_4.5), channel_id=1, source_target_pairs={{0,64},{16,80},{32,96},{48,112},{64,0},{80,16},{96,32},{112,48},{1... | collective-permute-start | bytes 196616 | tf_op jit(solution)/shard_map/ppermute | solution.py:223
  48.1 14.2 %copy-start.2 = (s32[1,4]{1,0:T(1,128)S(1)}, s32[1,4]{1,0:T(1,128)}, u32[]{:S(2)}) copy-start(s32[1,4]{1,0:T(1,128)} %param.5) | copy-start | bytes 52
  48.1 6.4 %collective-permute-start.11 = (bf16[4,32,256]{2,1,0:T(8,128)(2,1)S(1)}, bf16[4,32,256]{2,1,0:T(8,128)(2,1)S(1)}, u32[]{:S(2)}, u32[]{:S(2)}) collective-permute-start(bf16[4,32,256]{2,1,0:T(8,128)(2,1)S(1)} %pad_maximum_fusion.3), channel_id=1, source_target_pairs={{0,32},{16,48},{32,64},{48,80},{64,96},{80,112},{96,0},{112,16},{1... | collective-permute-start | bytes 196616 | tf_op jit(solution)/shard_map/ppermute | solution.py:223
  55.2 7.8 %collective-permute-start.17 = (bf16[128,256]{1,0:T(8,128)(2,1)S(1)}, bf16[128,256]{1,0:T(8,128)(2,1)S(1)}, u32[]{:S(2)}, u32[]{:S(2)}) collective-permute-start(bf16[128,256]{1,0:T(8,128)(2,1)S(1)} %bitcast.36), channel_id=1, source_target_pairs={{1,0},{2,1},{3,2},{4,3},{5,4},{6,5},{7,6},{8,7},{9,8},{10,9},{11,1... | collective-permute-start | bytes 196616 | tf_op jit(solution)/shard_map/ppermute | solution.py:218
  56.3 6.8 %collective-permute-start.16 = (bf16[128,256]{1,0:T(8,128)(2,1)S(1)}, bf16[128,256]{1,0:T(8,128)(2,1)S(1)}, u32[]{:S(2)}, u32[]{:S(2)}) collective-permute-start(bf16[128,256]{1,0:T(8,128)(2,1)S(1)} %bitcast.33), channel_id=1, source_target_pairs={{2,0},{3,1},{4,2},{5,3},{6,4},{7,5},{8,6},{9,7},{10,8},{11,9},{12,... | collective-permute-start | bytes 196616 | tf_op jit(solution)/shard_map/ppermute | solution.py:218
  57.0 6.1 %collective-permute-start.15 = (bf16[128,256]{1,0:T(8,128)(2,1)S(1)}, bf16[128,256]{1,0:T(8,128)(2,1)S(1)}, u32[]{:S(2)}, u32[]{:S(2)}) collective-permute-start(bf16[128,256]{1,0:T(8,128)(2,1)S(1)} %bitcast.32), channel_id=1, source_target_pairs={{16,0},{0,1},{1,2},{2,3},{3,4},{4,5},{5,6},{6,7},{7,8},{8,9},{9,10... | collective-permute-start | bytes 196616 | tf_op jit(solution)/shard_map/ppermute | solution.py:218
  59.6 6.7 %collective-permute-start.14 = (bf16[128,256]{1,0:T(8,128)(2,1)S(1)}, bf16[128,256]{1,0:T(8,128)(2,1)S(1)}, u32[]{:S(2)}, u32[]{:S(2)}) collective-permute-start(bf16[128,256]{1,0:T(8,128)(2,1)S(1)} %bitcast.31), channel_id=1, source_target_pairs={{16,0},{17,1},{0,2},{1,3},{2,4},{3,5},{4,6},{5,7},{6,8},{7,9},{8,1... | collective-permute-start | bytes 196616 | tf_op jit(solution)/shard_map/ppermute | solution.py:218
